TPU v7x, 256 devices: a whole 4x4x8 slice. The times are simulated.
256 devices in a mesh: row: 16 (over z_hi, y, core), col: 16 (over x, z_lo).
Axes of the slice: x: 4, y: 4, z: 8 (z_hi: 2, z_lo: 4; z = z_hi * 4 + z_lo), core: 2. Of those that a mesh axis runs over, the one named last changes fastest.
Arguments:
- x_blocks: bfloat16 [16, 16, 8, 128, 128], P('row', 'col'), may hold values from -1.5 to 1.5
- x_rows: int32 [16, 16, 8], replicated, may hold values from 0 to 31, as said below
- x_cols: int32 [16, 16, 8], replicated, may hold values from 0 to 31
- y_rows: int32 [16, 16, 16], replicated, may hold values from 0 to 31, as said below
- y_cols: int32 [16, 16, 16], replicated, may hold values from 0 to 31
- z_rows: int32 [16, 16, 24], replicated, may hold values from 0 to 31, as said below
- z_cols: int32 [16, 16, 24], replicated, may hold values from 0 to 31
Outputs:
- y_blocks: bfloat16 [16, 16, 16, 128, 128], P('row', 'col')
- next_blocks: bfloat16 [16, 16, 24, 128, 128], P('row', 'col')
Inputs may be any that keep to these rules, and one draw needn't show every extreme that they name: `x_rows`: together with x_cols: each tile lists exactly 8 distinct block positions, and a block row that appears in a tile appears there exactly 2 times. `y_rows`: together with y_cols: each tile lists exactly 16 distinct block positions. `z_rows`: together with z_cols: each tile lists exactly 24 distinct block positions.
All inputs are finite; a program needn't handle non-finite values.
Results may differ from a plain program's by a relative error of at most 0.0049.
Values may be sent and summed in bfloat16 or wider, within the bound.
No kernel may reach another device: no remote copies, remote signals or barrier semaphores. Data moves between devices by JAX's collectives and lax.ppermute only.
A program may use at most 64 MiB of HBM per device.

v0:
```python
import jax
import jax.numpy as jnp
from jax import lax
from jax.sharding import PartitionSpec as P

NBLOCKS = 512
ROW_MOST = 2


def left_plan(x_rows, x_cols, row_index, out_local, slab_cols, col_count):
    left_rows = x_rows[row_index]
    left_cols = x_cols[row_index]
    x_most = left_rows.shape[-1]
    hit = left_rows[None] == out_local[:, None, None]
    rank = jnp.cumsum(hit.astype(jnp.int32), axis=-1) - 1
    picks = hit[:, :, None, :] & (rank[:, :, None, :] == jnp.arange(ROW_MOST)[None, None, :, None])
    weights = picks.astype(jnp.int32)
    left_mask = jnp.any(picks, axis=-1)
    left_slot = jnp.sum(weights * jnp.arange(x_most), axis=-1)
    columns = jnp.sum(weights * left_cols[None, :, None, :], axis=-1)
    inner = jnp.arange(col_count)[None, :, None] * slab_cols + columns
    return (left_mask, left_slot, inner)


def right_plan(table_rows, table_cols, inner, left_mask, out_cols, col_index, slab_rows):
    owner = inner // slab_rows
    within = inner % slab_rows
    tile_rows = table_rows[owner, col_index]
    tile_cols = table_cols[owner, col_index]
    matched = (tile_rows == within[..., None]) & (tile_cols == out_cols[:, None, None, None])
    found = left_mask & jnp.any(matched, axis=-1)
    slot = jnp.sum(matched.astype(jnp.int32) * jnp.arange(tile_rows.shape[-1]), axis=-1)
    return (found, jnp.where(found, slot, 0))


def accumulate(
    left_fetch, right_fetch, left_mask, left_slot, right_mask, right_slot, col_count, block
):

    def step(section, total):
        left_tile = left_fetch(section)
        right_tile = right_fetch(section)
        left_pick = jnp.where(
            left_mask[:, section][:, :, None, None],
            left_tile[left_slot[:, section]],
            jnp.zeros((), left_tile.dtype),
        )
        right_pick = jnp.where(
            right_mask[:, section][:, :, None, None],
            right_tile[right_slot[:, section]],
            jnp.zeros((), right_tile.dtype),
        )
        return total + jnp.einsum(
            "neab,nebc->nac", left_pick, right_pick, preferred_element_type=jnp.float32
        )

    start = jnp.zeros((left_slot.shape[0], block, block), jnp.float32)
    return lax.fori_loop(0, col_count, step, start)


def shards(x_blocks, x_rows, x_cols, y_rows, y_cols, z_rows, z_cols):
    row_count = lax.axis_size("row")
    col_count = lax.axis_size("col")
    row_index = lax.axis_index("row")
    col_index = lax.axis_index("col")
    block = x_blocks.shape[-1]
    slab_rows = NBLOCKS // row_count
    slab_cols = NBLOCKS // col_count
    own_x = x_blocks[0, 0]
    whole_rows = lax.all_gather(x_blocks, "col", axis=1, tiled=True)[0]

    def left_first(section):
        return whole_rows[section]

    whole_cols = lax.all_gather(x_blocks, "row", axis=0, tiled=True)[:, 0]

    def right_first(section):
        return whole_cols[section * row_count // col_count]

    own_rows = y_rows[row_index, col_index]
    own_cols = y_cols[row_index, col_index]
    left_mask, left_slot, inner = left_plan(
        x_rows, x_cols, row_index, own_rows, slab_cols, col_count
    )
    right_mask, right_slot = right_plan(
        x_rows, x_cols, inner, left_mask, own_cols, col_index, slab_rows
    )
    product = accumulate(
        left_first, right_first, left_mask, left_slot, right_mask, right_slot, col_count, block
    )
    y_tile = product.astype(jnp.bfloat16)
    whole_product = lax.all_gather(y_tile[None, None], "row", axis=0, tiled=True)[:, 0]

    def right_second(section):
        return whole_product[section * row_count // col_count]

    own_rows_z = z_rows[row_index, col_index]
    own_cols_z = z_cols[row_index, col_index]
    left_mask_z, left_slot_z, inner_z = left_plan(
        x_rows, x_cols, row_index, own_rows_z, slab_cols, col_count
    )
    found, right_slot_z = right_plan(
        y_rows, y_cols, inner_z, left_mask_z, own_cols_z, col_index, slab_rows
    )
    z_total = accumulate(
        left_first, right_second, left_mask_z, left_slot_z, found, right_slot_z, col_count, block
    )
    here_rows = x_rows[row_index, col_index]
    here_cols = x_cols[row_index, col_index]
    here = (here_rows[None, :] == own_rows_z[:, None]) & (here_cols[None, :] == own_cols_z[:, None])
    present = jnp.any(here, axis=-1)
    own_slot = jnp.sum(here.astype(jnp.int32) * jnp.arange(here_rows.shape[0]), axis=-1)
    x_here = jnp.where(present[:, None, None], own_x[own_slot], jnp.zeros((), own_x.dtype)).astype(
        jnp.float32
    )
    update = (1.5 * x_here - 0.5 * z_total).astype(jnp.bfloat16)
    return (y_tile[None, None], update[None, None])


def solution(mesh):
    in_specs = (P("row", "col", None, None, None), P(), P(), P(), P(), P(), P())
    out_specs = (P("row", "col", None, None, None), P("row", "col", None, None, None))
    return jax.shard_map(shards, mesh=mesh, in_specs=in_specs, out_specs=out_specs, check_vma=False)
```

profile of v0, /device:TPU:1, one launch (start us, length us, event | category | flops | bytes accessed | tf_op | source)
XLA Modules:
  0.0 493.3 jit_solution(8097223732545904587)
XLA Ops:
  12.2 2.6 reduce_window_sum.22
  14.9 8.7 %select_reduce_fusion.2 = (s32[16,16,2]{2,1,0:T(8,128)S(1)}, s32[16,16,2]{2,1,0:T(8,128)S(1)}, pred[16,16,2,8]{3,2,1,0:T(4,128)(4,1)S(1)}) fusion(s32[16,8]{1,0:T(8,128)S(1)} %copy.77, s32[16,16,8]{2,1,0:T(8,128)S(1)} %broadcast_add_fusion, pred[16,16,8]{2,1,0:T(8,128)(4,1)S(1)} %get-tuple-element.537), kind=kLoop, calls=%fused_computation.57 | loop fusion | flops 23552 | bytes 18944 | tf_op jit(solution)/shard_map/reduce_sum | solution.py:20
  23.6 4.4 reduce_or.45
  28.7 3.7 gather_fusion.5
  32.4 3.8 gather_fusion.4
  36.4 4.9 select_reduce_fusion.1
  41.2 4.4 reduce_or.46
  46.1 69.3 %all-gather.5.cloned.1.call-done = bf16[1,16,8,128,128]{4,3,2,0,1:T(8,128)(2,1)} async-done(((bf16[1,1,8,128,128]{4,3,2,0,1:T(8,128)(2,1)}), bf16[1,16,8,128,128]{4,3,2,0,1:T(8,128)(2,1)}) %all-gather.5.cloned.1.call-update) | async-done | bytes 4194320 | tf_op jit(solution)/shard_map/all_gather | solution.py:70
  115.4 78.0 %all-gather.7.cloned.1.call-done = bf16[16,1,8,128,128]{4,3,2,1,0:T(8,128)(2,1)} async-done(((bf16[1,1,8,128,128]{4,3,2,1,0:T(8,128)(2,1)}), bf16[16,1,8,128,128]{4,3,2,1,0:T(8,128)(2,1)}) %all-gather.7.cloned.1.call-update) | async-done | bytes 4194320 | tf_op jit(solution)/shard_map/all_gather | solution.py:75
  193.4 64.3 %while.32 = (s32[]{:T(128)}, f32[16,128,128]{2,1,0:T(8,128)S(1)}, pred[16,16,2]{0,2,1:T(4,128)(4,1)S(1)}, bf16[16,8,128,128]{3,2,1,0:T(8,128)(2,1)}, s32[16,16,2...) while((s32[]{:T(128)}, f32[16,128,128]{2,1,0:T(8,128)S(1)}, ...), condition=%wide.region_7.8_spmd.clone, body=%wide.region_6.7_spmd.clone.sunk | while | flops 135792848 | bytes 9448107 | solution.py:58
  260.2 5.1 %gather_fusion.8 = s32[768,16]{1,0:T(8,128)S(1)} fusion(s32[16,16,16]{2,1,0:T(8,128)S(1)} %copy-done, s32[768]{0:T(1024)S(1)} %reshape.402), kind=kCustom, calls=%fused_computation.8 | custom fusion | bytes 104448 | tf_op jit(solution)/shard_map/gather | solution.py:29
  265.3 5.1 %gather_fusion.7 = s32[768,16]{1,0:T(8,128)S(1)} fusion(s32[16,16,16]{2,1,0:T(8,128)S(1)} %copy-done.1, s32[768]{0:T(1024)S(1)} %reshape.402), kind=kCustom, calls=%fused_computation.7 | custom fusion | bytes 104448 | tf_op jit(solution)/shard_map/gather | solution.py:28
  270.7 7.5 %select_reduce_fusion = (s32[24,16,2]{2,1,0:T(8,128)S(1)}, pred[24,16,2,16]{3,2,1,0:T(4,128)(4,1)S(1)}) fusion(s32[24,16,2,16]{3,2,1,0:T(2,128)S(1)} %bitcast.132, s32[24]{0:T(128)S(1)} %get-tuple-element.546, s32[24,16,2,16]{3,2,1,0:T(2,128)S(1)} %bitcast.133, s32[24,16,2]{2,1,0:T(8,128)S(1)} %copy.87), kind=kLoop, calls=%fused_computation.54 | loop fusion | flops 60672 | bytes 116832 | tf_op jit(solution)/shard_map/reduce_sum | solution.py:32
  278.4 6.6 %reduce_or.49 = pred[24,16,2]{2,1,0:T(8,128)(4,1)S(1)} reduce(pred[24,16,2,16]{3,2,1,0:T(4,128)(4,1)S(1)} %get-tuple-element.519, pred[]{:T(512)} %constant.251.clone.1), dimensions={3}, to_apply=%region_14.15 | reduce | flops 11520 | bytes 13057 | tf_op jit(solution)/shard_map/reduce_or | solution.py:31
  288.9 73.6 %all-gather.9.cloned.1.call-done = bf16[256,128,128]{2,1,0:T(8,128)(2,1)} async-done(((bf16[16,128,128]{2,1,0:T(8,128)(2,1)}), bf16[256,128,128]{2,1,0:T(8,128)(2,1)}) %all-gather.9.cloned.1.call-update) | async-done | bytes 8388624 | tf_op jit(solution)/shard_map/all_gather | solution.py:92
  362.6 121.3 %while.33 = (s32[]{:T(128)}, f32[24,128,128]{2,1,0:T(8,128)}, pred[24,16,2]{0,2,1:T(4,128)(4,1)S(1)}, bf16[16,8,128,128]{3,2,1,0:T(8,128)(2,1)}, s32[24,16,2]{0,...) while((s32[]{:T(128)}, f32[24,128,128]{2,1,0:T(8,128)}, ...), condition=%wide.region_17.18_spmd.clone, body=%wide.region_16.17_spmd.clone.sunk | while | flops 203688240 | bytes 14167883 | solution.py:58
  373.2 3.3 bitcast_add_fusion.4
  380.9 3.3 bitcast_add_fusion.4
  388.6 3.3 bitcast_add_fusion.4
  396.2 3.3 bitcast_add_fusion.4
  403.9 3.3 bitcast_add_fusion.4
  411.6 3.3 bitcast_add_fusion.4
  419.3 3.3 bitcast_add_fusion.4
  426.9 3.3 bitcast_add_fusion.4
  434.6 3.3 bitcast_add_fusion.4
  442.3 3.3 bitcast_add_fusion.4
  449.9 3.3 bitcast_add_fusion.4
  457.6 3.3 bitcast_add_fusion.4
  465.3 3.3 bitcast_add_fusion.4
  473.0 3.3 bitcast_add_fusion.4
  480.6 3.3 bitcast_add_fusion.4
  483.9 2.9 fusion.22
  (502 shorter events, 147.1 us)
Async XLA Ops:
  7.2 108.2 %all-gather.5.cloned.1.call-start = ((), (), s32[]{:S(2)}) async-start(), calls=%async_computation | async-start | bytes 4456448 | tf_op jit(solution)/shard_map/all_gather | solution.py:70
  7.9 185.5 %all-gather.7.cloned.1.call-start = ((), (), s32[]{:S(2)}) async-start(), calls=%async_computation.1 | async-start | bytes 4456448 | tf_op jit(solution)/shard_map/all_gather | solution.py:75
  8.6 353.9 %all-gather.9.cloned.1.call-start = ((), (), s32[]{:S(2)}) async-start(), calls=%async_computation.2 | async-start | bytes 8912896 | tf_op jit(solution)/shard_map/all_gather | solution.py:92
  257.7 2.5 copy-start
  260.1 5.1 %copy-start.1 = (s32[16,16,16]{2,1,0:T(8,128)S(1)}, s32[16,16,16]{2,1,0:T(8,128)}, u32[]{:S(2)}) copy-start(s32[16,16,16]{2,1,0:T(8,128)} %param.14) | copy-start | bytes 49156
  270.4 15.9 %copy-start.2 = (bf16[1,1,8,128,128]{4,3,2,1,0:T(8,128)(2,1)S(1)}, bf16[1,1,8,128,128]{4,3,2,1,0:T(8,128)(2,1)}, u32[]{:S(2)}) copy-start(bf16[1,1,8,128,128]{4,3,2,1,0:T(8,128)(2,1)} %param.11) | copy-start | bytes 786436
Sparse Core Ops, SparseCore 0:
  9.8 105.5 all-gather.4
  118.1 75.1 all-gather.6
  258.7 103.7 all-gather.8
where the time goes:
time: 496 us; the launch traced here: 493 us
  waiting for transfers between devices  222 us (45%)
  local copies, waits for them, and re-layouts  145 us (29%)
  matrix products  63.2 us (13%)
  other arithmetic  45.9 us (9%)
  between operations  14 us (3%)
    all_gather x1, waiting for transfers between devices, shards(): whole_cols = lax.all_gather(x_blocks, 'row', axis=0, tiled=True)[:, 0]  78 us
    all_gather x1, waiting for transfers between devices, shards(): lax.all_gather(y_tile[None, None], 'row', axis=0, tiled=True)[:, 0]  73.6 us
    all_gather x1, waiting for transfers between devices, shards(): whole_rows = lax.all_gather(x_blocks, 'col', axis=1, tiled=True)[0]  69.3 us
    dot_general x32, matrix products, step(): jnp.einsum('neab,nebc->nac', left_pick, right_pick, preferred_element_typ...  63.2 us
    gather x32, local copies, waits for them, and re-layouts, step(): left_tile[left_slot[:, section]]  25.6 us
    gather x32, local copies, waits for them, and re-layouts, step(): right_tile[right_slot[:, section]]  25.6 us
    squeeze x16, local copies, waits for them, and re-layouts, right_second(): return whole_product[section * row_count // col_count]  17.2 us
    squeeze x16, local copies, waits for them, and re-layouts, right_first(): return whole_cols[section * row_count // col_count]  17.1 us
  transfers between devices with their start and end apart: 3, of which 3 were waited for; matrix products, arithmetic and copies ran while one was open for 14% of the time, Pallas kernels for 0%

commit v1 on v0

v1 whole, which is shorter than its diff:
```python
import functools

import jax
import jax.numpy as jnp
from jax import lax
from jax.experimental import pallas as pl
from jax.experimental.pallas import tpu as pltpu
from jax.sharding import PartitionSpec as P

SLAB = 32
SIDE = 16
BLOCK = 128
TERMS = 32
COUNT = 32
OWN = 33
FLAG = 34
LEFT_FIRST = 10
LEFT_ALL = 17
RIGHT_FIRST = 10
MOST = 32

ROW = [(z, y, k) for z in range(2) for y in range(4) for k in range(2)]
COL = [(x, b) for x in range(4) for b in range(4)]


def row_at(z, y, k):
    return z * 8 + y % 4 * 2 + k


def col_at(x, b):
    return x % 4 * 4 + b


Z_SWAP = [(row_at(z, y, k), row_at(1 - z, y, k)) for z, y, k in ROW]
CORE_SWAP = [(row_at(z, y, k), row_at(z, y, 1 - k)) for z, y, k in ROW]
Y_RING = [[(row_at(z, y, k), row_at(z, y + d, k)) for z, y, k in ROW] for d in (1, 3, 2)]
X_RING = [[(col_at(x, b), col_at(x + d, b)) for x, b in COL] for d in (1, 3, 2)]
B_SWAP = [[(col_at(x, b), col_at(x, b ^ d)) for x, b in COL] for d in (1, 2, 3)]


def ring_piece(offset):
    return jnp.where(offset == 0, 0, jnp.where(offset == 1, 2, jnp.where(offset == 2, 3, 1)))


def iota(shape, dim):
    return lax.broadcasted_iota(jnp.int32, shape, dim)


def half(values):
    return values.astype(jnp.float32).astype(jnp.bfloat16)


def nn(a, b):
    return jnp.dot(half(a), half(b), preferred_element_type=jnp.float32)


def nt(a, b):
    return lax.dot_general(
        half(a), half(b), (((1,), (1,)), ((), ())), preferred_element_type=jnp.float32
    )


def eye(size):
    return iota((size, size), 0) == iota((size, size), 1)


def flat(table, by_col):
    most = table.shape[-1]
    size = SIDE * most
    values = table[...].reshape(SIDE * SIDE, most)
    wide = nn(values, (iota((most, size), 1) & (most - 1)) == iota((most, size), 0))
    tile = iota((SIDE * SIDE, size), 0)
    section = iota((SIDE * SIDE, size), 1) // most
    pick = iota((SIDE, SIDE * SIDE), 1)
    if by_col:
        wide = jnp.where(section == tile >> 4, wide, 0.0)
        pick = pick & 15
    else:
        wide = jnp.where(section == tile & 15, wide, 0.0)
        pick = pick >> 4
    return nn(pick == iota((SIDE, SIDE * SIDE), 0), wide)


def slab(table, row):
    most = table.shape[-1]
    size = SIDE * most
    wide = nn(table[row], (iota((most, size), 1) & (most - 1)) == iota((most, size), 0))
    wide = jnp.where(iota((SIDE, size), 1) // most == iota((SIDE, size), 0), wide, 0.0)
    return jnp.sum(wide, axis=0, keepdims=True)


def pick_row(values, index):
    return nn(iota((8, values.shape[0]), 1) == index, values)


def to_col(lanes):
    size = lanes.shape[1]
    return nt(eye(size), jnp.broadcast_to(lanes[:1], (8, size)))[:, :1]


def start_of(size, most, dim):
    shape = (1, size) if dim else (size, 1)
    return ((iota(shape, dim) // most) * SLAB).astype(jnp.float32)


def message(ranks, dest, mine, place):
    size, dests = ranks.shape
    rank = nn(ranks, iota((dests, 8), 0) == dest)[:, :1]
    lane = iota((size, 128), 1)
    slots = (rank == (lane + 1).astype(jnp.float32)) & mine
    return nn(jnp.broadcast_to(place, (8, size)), slots)[:1]


def table_of(rows, flag):
    sub, lane = iota((8, 128), 0), iota((8, 128), 1)
    table = jnp.where((sub == 3) & (lane == 0), flag, 0.0)
    for n, values in enumerate(rows):
        table = jnp.where(sub == n, values, table)
    return table.astype(jnp.int32)


def left_kernel(at, x_rows, x_cols, y_rows, y_cols, z_rows, z_cols, send, positions):
    row, col = at[0], at[1]
    x, b = col >> 2, col & 3
    n = SIDE * x_rows.shape[-1]
    left_i = to_col(slab(x_rows, row))
    left_k = to_col(slab(x_cols, row)) + start_of(n, x_rows.shape[-1], 0)

    def needed(rows, cols, out_rows, out_cols):
        most = rows.shape[-1]
        outs = out_rows.shape[-1]
        keys = flat(rows, True) + start_of(SIDE * most, most, 1)
        others = flat(cols, True)
        out_i = out_rows[row].astype(jnp.float32)
        out_j = nt(eye(outs), out_cols[row])
        result = jnp.zeros((n, SIDE), jnp.float32)
        for c in range(SIDE):
            same_k = left_k == keys[c : c + 1]
            same_j = out_j[:, c : c + 1] == others[c : c + 1]
            hit = (nt(same_k, same_j) > 0.5) & (left_i == out_i[c : c + 1])
            some = jnp.max(hit.astype(jnp.float32), axis=1, keepdims=True)
            result = jnp.where(iota((n, SIDE), 1) == c, some, result)
        return result

    for_y = needed(x_rows, x_cols, y_rows, y_cols)
    for_z = needed(y_rows, y_cols, z_rows, z_cols) * (1.0 - for_y)
    group = iota((n, n), 0) >> 3 & 3
    same = group == (iota((n, n), 1) >> 3 & 3)
    before = same & (iota((n, n), 1) <= iota((n, n), 0))
    total_y, total_z = nn(same, for_y), nn(same, for_z)
    ranks = jnp.where(
        for_y > 0.5, nn(before, for_y), jnp.where(for_z > 0.5, total_y + nn(before, for_z), 0.0)
    )
    crosses = (iota((n, SIDE), 0) >> 3 & 3) != (iota((n, SIDE), 1) & 3)
    over = crosses & ((total_y > LEFT_FIRST) | (total_y + total_z > LEFT_ALL))
    flag = jnp.max(over.astype(jnp.float32))

    lane = iota((1, n), 1)
    place = (ring_piece((lane >> 5) - x & 3) * 8 + (lane & 7)).astype(jnp.float32)
    mine = (iota((n, 1), 0) >> 3 & 3) == b
    rows = [message(ranks, (x << 2) + (b ^ d), mine, place) for d in (1, 2, 3)]
    send[...] = table_of(rows, flag)
    rank = nt(iota((8, SIDE), 1) == col, ranks)[:1]
    d = (lane >> 3 & 3) ^ b
    spot = jnp.where(d == 0, place, (d * MOST).astype(jnp.float32) + jnp.maximum(rank - 1.0, 0.0))
    positions[...] = jnp.broadcast_to(spot, (8, n)).astype(jnp.int32)


def terms_list(out_i, out_j, left_i, left_k, left_pos, right_k, right_j, right_pos):
    outs, size = out_i.shape[0], left_i.shape[1]
    found = nt(jnp.where(out_j == right_j, right_pos + 1.0, 0.0), left_k == right_k)
    hit = (out_i == left_i) & (found > 0.5)
    marks = hit.astype(jnp.float32)
    rank = nn(marks, iota((size, size), 0) <= iota((size, size), 1))
    code = left_pos * 256.0 + (found - 1.0)
    lane = iota((outs, 128), 1)
    table = jnp.where(lane == COUNT, jnp.sum(marks, axis=1, keepdims=True), 0.0)
    for q in range(TERMS):
        picked = jnp.where(hit & (rank == q + 1.0), code, 0.0)
        table = table + jnp.where(lane == q, jnp.sum(picked, axis=1, keepdims=True), 0.0)
    return table, lane


def right_kernel(
    at, left_send, positions, x_rows, x_cols, y_rows, y_cols, z_rows, z_cols, send, y_plan, z_plan
):
    row, col = at[0], at[1]
    z, y, k = row >> 3, row >> 1 & 3, row & 1
    most, y_most, z_most = x_rows.shape[-1], y_rows.shape[-1], z_rows.shape[-1]
    n, m = SIDE * most, SIDE * y_most
    rows_i = flat(x_rows, False)
    rows_k = flat(x_cols, False) + start_of(n, most, 1)
    y_i = pick_row(flat(y_rows, True), col)[:1]
    y_j = pick_row(flat(y_cols, True), col)[:1]
    key = to_col(y_i) + start_of(m, y_most, 0)
    other = to_col(y_j)
    tile = iota((SIDE, SIDE * SIDE), 1)
    ours = (tile >> 4 == iota((SIDE, SIDE * SIDE), 0)) & ((tile & 15) == col)
    z_i = nn(ours, z_rows[...].reshape(SIDE * SIDE, z_most))
    z_j = nn(ours, z_cols[...].reshape(SIDE * SIDE, z_most))
    z_t = nt(eye(z_most), z_i)
    need = jnp.zeros((m, SIDE), jnp.float32)
    for r in range(SIDE):
        same_k = key == rows_k[r : r + 1]
        same_i = z_t[:, r : r + 1] == rows_i[r : r + 1]
        hit = (nt(same_k, same_i) > 0.5) & (other == z_j[r : r + 1])
        some = jnp.max(hit.astype(jnp.float32), axis=1, keepdims=True)
        need = jnp.where(iota((m, SIDE), 1) == r, some, need)
    need = nn(need, iota((SIDE, 8), 0) >> 1 == iota((SIDE, 8), 1)) > 0.5
    same = iota((m, m), 0) >> 4 == iota((m, m), 1) >> 4
    before = same & (iota((m, m), 1) <= iota((m, m), 0))
    ranks = jnp.where(need, nn(before, need), 0.0)
    crosses = (iota((m, 8), 0) >> 5 & 3) != (iota((m, 8), 1) & 3)
    over = crosses & (nn(same, need) > RIGHT_FIRST)
    flag = jnp.max(over.astype(jnp.float32))

    lane = iota((1, m), 1)
    slot = (lane & 15).astype(jnp.float32)
    tile = iota((m, 1), 0) >> 4
    dests = [(z << 2) + (y + d & 3) for d in (1, 3, 2)]
    rows = [message(ranks, dest, tile == row, slot) for dest in dests]
    send[:8] = table_of(rows, flag)
    rows = [message(ranks, dest, tile == (row ^ 8), slot) for dest in dests]
    send[8:] = table_of(rows, flag)
    rank = nt(iota((8, 8), 1) == row >> 1, ranks)[:1]
    piece = ring_piece((lane >> 5 & 3) - y & 3)
    spot = jnp.where(piece == 0, slot, jnp.maximum(rank - 1.0, 0.0))
    base = (lane >> 4 & 1 ^ k) * 128 + piece * MOST + (lane >> 7 ^ z) * 16
    y_pos = base.astype(jnp.float32) + spot
    lane = iota((1, n), 1)
    piece = ring_piece((lane >> 4 & 3) - y & 3)
    x_pos = (lane >> 3 & 1 ^ k) * 64 + piece * 16 + (lane >> 6 ^ z) * 8 + (lane & 7)
    x_pos = x_pos.astype(jnp.float32)

    x_k = pick_row(flat(x_rows, True), col)[:1] + start_of(n, most, 1)
    x_j = pick_row(flat(x_cols, True), col)[:1]
    left_i = slab(x_rows, row)
    left_k = to_col(slab(x_cols, row)) + start_of(n, most, 0)
    left_pos = positions[:1].astype(jnp.float32)

    def own(table):
        return pick_row(table[row], col)[:1]

    left_flag = left_send[3, 0].astype(jnp.float32)
    table, lane = terms_list(
        to_col(own(y_rows)), to_col(own(y_cols)), left_i, left_k, left_pos, x_k, x_j, x_pos
    )
    y_plan[...] = jnp.where(lane == FLAG, left_flag, table).astype(jnp.int32)
    out_i, out_j = to_col(own(z_rows)), to_col(own(z_cols))
    table, lane = terms_list(
        out_i, out_j, left_i, left_k, left_pos,
        y_i + start_of(m, y_most, 1), y_j, y_pos,
    )
    here = (own(x_rows) == out_i) & (own(x_cols) == out_j)
    slot = (iota(here.shape, 1) + 1).astype(jnp.float32)
    slot = jnp.sum(jnp.where(here, slot, 0.0), axis=1, keepdims=True)
    table = table + jnp.where(lane == OWN, slot, 0.0)
    table = jnp.where(lane == FLAG, left_flag + 2.0 * flag, table)
    z_plan[...] = table.astype(jnp.int32)


def pack_kernel(unit, count, first_row, start, sizes, table, *refs):
    sources, outs = refs[:count], refs[count : count + 3 * len(sizes)]
    held, in_sems, out_sems = refs[count + 3 * len(sizes) :]
    loads = [
        pltpu.make_async_copy(source, held.at[pl.ds(n * unit, unit)], in_sems.at[n])
        for n, source in enumerate(sources)
    ]
    for load in loads:
        load.start()
    for load in loads:
        load.wait()
    copies = []
    at = start
    for group, size in enumerate(sizes):
        for n in range(size):
            for d in range(3):
                copies.append(
                    pltpu.make_async_copy(
                        held.at[table[first_row + d, at + n]],
                        outs[group * 3 + d].at[n],
                        out_sems.at[len(copies)],
                    )
                )
        at += size
    for copy in copies:
        copy.start()
    for copy in copies:
        copy.wait()


def pack(table, sources, first_row, start, *sizes):
    unit = sources[0].shape[0]
    return pl.pallas_call(
        functools.partial(pack_kernel, unit, len(sources), first_row, start, sizes),
        out_shape=[
            jax.ShapeDtypeStruct((size, BLOCK, BLOCK), jnp.bfloat16)
            for size in sizes
            for _ in range(3)
        ],
        in_specs=[pl.BlockSpec(memory_space=pltpu.SMEM)]
        + [pl.BlockSpec(memory_space=pl.ANY)] * len(sources),
        out_specs=[pl.BlockSpec(memory_space=pl.ANY)] * (3 * len(sizes)),
        scratch_shapes=[
            pltpu.VMEM((unit * len(sources), BLOCK, BLOCK), jnp.bfloat16),
            pltpu.SemaphoreType.DMA((len(sources),)),
            pltpu.SemaphoreType.DMA((3 * sum(sizes),)),
        ],
    )(table, *sources)


def nothing(count, size):
    return pl.pallas_call(
        lambda *refs: None,
        out_shape=[jax.ShapeDtypeStruct((size, BLOCK, BLOCK), jnp.bfloat16)] * count,
        out_specs=[pl.BlockSpec(memory_space=pl.ANY)] * count,
    )()


def products_kernel(layout, update, plan, *refs):
    pieces = refs[: len(layout)]
    out, left, right, total, sems = refs[len(layout) :]

    def copy(n):
        side, at, skip, size, _ = layout[n]
        buffer = (left, right)[side]
        source = pieces[n] if skip is None else pieces[n].at[pl.ds(skip, size)]
        return pltpu.make_async_copy(source, buffer.at[pl.ds(at, size)], sems.at[n])

    def each(act):
        for n, piece in enumerate(layout):
            if piece[4]:

                @pl.when(plan[0, FLAG] & piece[4] != 0)
                def _():
                    act(copy(n))

            else:
                act(copy(n))

    each(lambda c: c.start())
    each(lambda c: c.wait())

    def product(t, q):
        code = plan[t, q]
        return jnp.dot(
            left[code >> 8], right[code & 255], preferred_element_type=jnp.float32
        )

    outs = out.shape[0]
    for t in range(outs):
        total[t] = jnp.where(plan[t, COUNT] > 0, product(t, 0), 0.0)

    def more(t, carry):
        def term(q, inner):
            total[t] += product(t, q)
            return inner

        return lax.fori_loop(1, plan[t, COUNT], term, carry)

    lax.fori_loop(0, outs, more, 0)
    for t in range(outs):
        if update:
            slot = plan[t, OWN]
            x_here = left[jnp.maximum(slot - 1, 0)].astype(jnp.float32)
            x_here = jnp.where(slot > 0, x_here, 0.0)
            out[t] = (1.5 * x_here - 0.5 * total[t]).astype(jnp.bfloat16)
        else:
            out[t] = total[t].astype(jnp.bfloat16)


def products(plan, pieces, sizes, update):
    outs = plan.shape[0]
    layout = [
        (side, at, skip, p.shape[0] - (skip or 0), bit) for side, at, skip, bit, p in pieces
    ]
    return pl.pallas_call(
        functools.partial(products_kernel, layout, update),
        out_shape=jax.ShapeDtypeStruct((outs, BLOCK, BLOCK), jnp.bfloat16),
        in_specs=[pl.BlockSpec(memory_space=pltpu.SMEM)]
        + [pl.BlockSpec(memory_space=pl.ANY)] * len(pieces),
        out_specs=pl.BlockSpec(memory_space=pltpu.VMEM),
        scratch_shapes=[
            pltpu.VMEM((sizes[0], BLOCK, BLOCK), jnp.bfloat16),
            pltpu.VMEM((sizes[1], BLOCK, BLOCK), jnp.bfloat16),
            pltpu.VMEM((outs, BLOCK, BLOCK), jnp.float32),
            pltpu.SemaphoreType.DMA((len(pieces),)),
        ],
        compiler_params=pltpu.CompilerParams(vmem_limit_bytes=32 * 1024 * 1024),
    )(plan, *[p[-1] for p in pieces])


def row_send(blocks, perm):
    return lax.ppermute(blocks, "row", perm)


def col_send(blocks, perm):
    return lax.ppermute(blocks, "col", perm)


def after(value, *others):
    return lax.optimization_barrier((value, others))[0]


def shards(x_blocks, x_rows, x_cols, y_rows, y_cols, z_rows, z_cols):
    row = lax.axis_index("row")
    col = lax.axis_index("col")
    at = jnp.stack([row, col]).astype(jnp.int32)
    tables = (x_rows, x_cols, y_rows, y_cols, z_rows, z_cols)
    tile = x_blocks[0, 0]
    y_most, z_most = y_rows.shape[-1], z_rows.shape[-1]
    smem = pl.BlockSpec(memory_space=pltpu.SMEM)
    vmem = pl.BlockSpec(memory_space=pltpu.VMEM)

    far = row_send(tile, Z_SWAP)
    near = [col_send(tile, ring) for ring in X_RING]
    left_send, positions = pl.pallas_call(
        left_kernel,
        out_shape=(jax.ShapeDtypeStruct((8, 128), jnp.int32),) * 2,
        in_specs=[smem] + [vmem] * 6,
    )(at, *tables)
    near, left_send, positions = lax.optimization_barrier((near, left_send, positions))
    quad = [tile] + near
    first = pack(left_send, quad, 0, 0, LEFT_FIRST, LEFT_ALL - LEFT_FIRST)
    first, far = lax.optimization_barrier((first, far))
    first, second = first[:3], first[3:]
    first = [col_send(blocks, swap) for blocks, swap in zip(first, B_SWAP)]
    pair = jnp.concatenate([tile, far])
    across = row_send(pair, Y_RING[2])
    up = row_send(pair, Y_RING[0])
    down = row_send(after(pair, first[0]), Y_RING[1])
    pair_mate = row_send(after(pair, first[0]), CORE_SWAP)
    right_send, y_plan, z_plan = pl.pallas_call(
        right_kernel,
        out_shape=(
            jax.ShapeDtypeStruct((16, 128), jnp.int32),
            jax.ShapeDtypeStruct((y_most, 128), jnp.int32),
            jax.ShapeDtypeStruct((z_most, 128), jnp.int32),
        ),
        in_specs=[smem, smem] + [vmem] * 7,
    )(at, left_send, positions, *tables)
    first, up, down, across, pair_mate, right_send, y_plan, z_plan = lax.optimization_barrier(
        (first, up, down, across, pair_mate, right_send, y_plan, z_plan)
    )
    x_half = [pair, up, down, across]
    x_mate = [pair_mate] + [row_send(blocks, CORE_SWAP) for blocks in x_half[1:]]
    one = col_send(second[0], B_SWAP[0])

    def more_left():
        rest = pack(left_send, quad, 0, LEFT_FIRST, MOST - LEFT_FIRST)
        return tuple(col_send(blocks, swap) for blocks, swap in zip(rest, B_SWAP))

    rest = lax.cond(
        left_send[3, 0] > 0, more_left, lambda: tuple(nothing(3, MOST - LEFT_FIRST))
    )

    left = [(0, 8 * n, None, 0, p) for n, p in enumerate(quad)]
    left += [(0, MOST * (n + 1), None, 0, p) for n, p in enumerate(first)]
    right = [(1, 16 * n, None, 0, p) for n, p in enumerate(x_half + x_mate)]
    extra = [(0, MOST * (n + 1) + LEFT_FIRST, None, 1, p) for n, p in enumerate(rest)]
    y_tile = products(y_plan, left + right + extra, (4 * MOST, 128), False)

    y_far = row_send(y_tile, Z_SWAP)
    tile_mate = row_send(y_tile, CORE_SWAP)
    own_send = pack(right_send, [y_tile], 0, 0, RIGHT_FIRST)
    own_near = [row_send(blocks, ring) for blocks, ring in zip(own_send, Y_RING)]
    y_far, tile_mate, own_near, one = lax.optimization_barrier((y_far, tile_mate, own_near, one))
    far_send = pack(right_send, [y_far], 8, 0, RIGHT_FIRST)
    far_mate = row_send(y_far, CORE_SWAP)
    far_send, far_mate = lax.optimization_barrier((far_send, far_mate))
    far_near = [row_send(blocks, ring) for blocks, ring in zip(far_send, Y_RING)]
    second = [one] + [col_send(blocks, swap) for blocks, swap in zip(second[1:], B_SWAP[1:])]
    own_mate = [row_send(blocks, CORE_SWAP) for blocks in own_near]
    far_near, second, own_mate = lax.optimization_barrier((far_near, second, own_mate))
    far_near_mate = [row_send(blocks, CORE_SWAP) for blocks in far_near]

    def more_right():
        blocks = pack(right_send, [y_tile], 0, RIGHT_FIRST, y_most - RIGHT_FIRST)
        blocks += pack(right_send, [y_far], 8, RIGHT_FIRST, y_most - RIGHT_FIRST)
        blocks = [row_send(b, ring) for b, ring in zip(blocks, Y_RING + Y_RING)]
        return tuple(blocks + [row_send(b, CORE_SWAP) for b in blocks])

    more = lax.cond(
        right_send[3, 0] > 0, more_right, lambda: tuple(nothing(12, y_most - RIGHT_FIRST))
    )

    left += [(0, MOST * (n + 1) + LEFT_FIRST, None, 0, p) for n, p in enumerate(second)]
    extra = [
        (0, MOST * (n + 1) + LEFT_ALL, LEFT_ALL - LEFT_FIRST, 1, p) for n, p in enumerate(rest)
    ]
    right = []
    spots = [i * MOST + j * y_most for i in range(4) for j in range(2)]
    ours = [y_tile, y_far] + [p for both in zip(own_near, far_near) for p in both]
    theirs = [tile_mate, far_mate] + [p for both in zip(own_mate, far_near_mate) for p in both]
    for n, side in enumerate((ours, theirs)):
        right += [(1, n * 128 + spot, None, 0, p) for spot, p in zip(spots, side)]
        rest_spots = spots[2::2] + spots[3::2]
        extra += [
            (1, n * 128 + spot + RIGHT_FIRST, None, 2, p)
            for spot, p in zip(rest_spots, more[6 * n : 6 * n + 6])
        ]
    update = products(z_plan, left + right + extra, (4 * MOST, 8 * MOST), True)
    return (y_tile[None, None], update[None, None])


def solution(mesh):
    in_specs = (P("row", "col", None, None, None), P(), P(), P(), P(), P(), P())
    out_specs = (P("row", "col", None, None, None), P("row", "col", None, None, None))
    return jax.shard_map(shards, mesh=mesh, in_specs=in_specs, out_specs=out_specs, check_vma=False)
```

time: 496 us -> 142 us (0.29)
  waiting for transfers between devices: 222 us -> 51.2 us
  local copies, waits for them, and re-layouts: 145 us -> 4.33 us
  matrix products: 63.2 us -> 0 us
  starting transfers between devices: 0.11 us -> 52.4 us
  other arithmetic: 45.9 us -> 0.64 us
  Pallas kernels: 0 us -> 29.4 us
  between operations: 14 us -> 2.17 us
    all_gather x3 -> x0, waiting for transfers between devices: 221 us -> none  [the longest x1 78 us: shards(): whole_cols = lax.all_gather(x_blocks, 'row', axis=0, tiled=True)[:, 0]]
    gather x69 -> x0, local copies, waits for them, and re-layouts: 70.5 us -> none  [the longest x32 25.6 us: step(): left_tile[left_slot[:, section]]]
    dot_general x32 -> x0, matrix products: 63.2 us -> none  [step(): jnp.einsum('neab,nebc->nac', left_pick, right_pick, preferred_element_typ...]
    ppermute x0 -> x32, starting transfers between devices: none -> 52.4 us  [the longest x23 33.8 us: row_send(): return lax.ppermute(blocks, 'row', perm)]
    ppermute x0 -> x32, waiting for transfers between devices: none -> 51.2 us  [the longest x23 28.1 us: row_send(): return lax.ppermute(blocks, 'row', perm)]
    squeeze x48 -> x0, local copies, waits for them, and re-layouts: 49.8 us -> none  [the longest x16 17.2 us: right_second(): return whole_product[section * row_count // col_count]]
    pallas_call x0 -> x9, Pallas kernels: none -> 29.4 us  [the longest x3 9.15 us: pack(): pl.pallas_call(functools.partial(pack_kernel, unit, len(sources), first_r...]
    reduce_sum x5 -> x0, other arithmetic: 21.3 us -> none  [the longest x2 12.3 us: right_plan(): jnp.sum(matched.astype(jnp.int32) * jnp.arange(tile_rows.shape[-1]), axis...]
  transfers between devices with their start and end apart: 3 -> 32, of which waited for: 3 -> 10; matrix products, arithmetic and copies ran while one was open for 14% -> 3% of each run, Pallas kernels for 0% -> 17%
where the time goes in v1:
time: 142 us; the launch traced here: 140 us
  starting transfers between devices  52.4 us (37%)
  waiting for transfers between devices  51.2 us (36%)
  Pallas kernels  29.4 us (21%)
  local copies, waits for them, and re-layouts  4.33 us (3%)
  between operations  2.17 us (2%)
    ppermute x23, starting transfers between devices, row_send(): return lax.ppermute(blocks, 'row', perm)  33.8 us
    ppermute x23, waiting for transfers between devices, row_send(): return lax.ppermute(blocks, 'row', perm)  28.1 us
    ppermute x9, waiting for transfers between devices, col_send(): return lax.ppermute(blocks, 'col', perm)  23.1 us
    ppermute x9, starting transfers between devices, col_send(): return lax.ppermute(blocks, 'col', perm)  18.6 us
    pallas_call x3, Pallas kernels, pack(): pl.pallas_call(functools.partial(pack_kernel, unit, len(sources), first_r...  9.15 us
    pallas_call x2, Pallas kernels, products(): pl.pallas_call(functools.partial(products_kernel, layout, update), out_sh...  9.05 us
    pallas_call x1, Pallas kernels, shards(): pl.pallas_call(right_kernel, out_shape=(jax.ShapeDtypeStruct((16, 128), j...  6.59 us
    pallas_call x1, Pallas kernels, shards(): pl.pallas_call(left_kernel, out_shape=(jax.ShapeDtypeStruct((8, 128), jnp...  4.61 us
  transfers between devices with their start and end apart: 32, of which 10 were waited for; matrix products, arithmetic and copies ran while one was open for 3% of the time, Pallas kernels for 17%

profile of v1, /device:TPU:1, one launch (start us, length us, event | category | flops | bytes accessed | tf_op | source)
XLA Modules:
  0.0 140.4 jit_solution(16401616966692875915)
XLA Ops:
  0.6 2.1 %collective-permute-start.15 = (bf16[8,128,128]{2,1,0:T(8,128)(2,1)}, bf16[8,128,128]{2,1,0:T(8,128)(2,1)}, u32[]{:S(2)}, u32[]{:S(2)}) collective-permute-start(bf16[8,128,128]{2,1,0:T(8,128)(2,1)} %bitcast.7), channel_id=1, source_target_pairs={{0,4},{1,5},{2,6},{3,7},{4,8},{5,9},{6,10},{7,11},{8,12},{9,13},{1... | collective-permute-start | bytes 786440 | tf_op jit(solution)/shard_map/ppermute | solution.py:398
  2.7 1.4 collective-permute-start.16
  4.1 1.6 %collective-permute-start.17 = (bf16[8,128,128]{2,1,0:T(8,128)(2,1)}, bf16[8,128,128]{2,1,0:T(8,128)(2,1)}, u32[]{:S(2)}, u32[]{:S(2)}) collective-permute-start(bf16[8,128,128]{2,1,0:T(8,128)(2,1)} %bitcast.9), channel_id=1, source_target_pairs={{0,8},{1,9},{2,10},{3,11},{4,12},{5,13},{6,14},{7,15},{8,0},{9,1},... | collective-permute-start | bytes 786440 | tf_op jit(solution)/shard_map/ppermute | solution.py:398
  5.7 6.9 %collective-permute-start.18 = (bf16[8,128,128]{2,1,0:T(8,128)(2,1)}, bf16[8,128,128]{2,1,0:T(8,128)(2,1)S(1)}, u32[]{:S(2)}, u32[]{:S(2)}) collective-permute-start(bf16[8,128,128]{2,1,0:T(8,128)(2,1)} %bitcast.10), channel_id=1, source_target_pairs={{0,128},{16,144},{32,160},{48,176},{64,192},{80,208},{96,224},{112... | collective-permute-start | bytes 786440 | tf_op jit(solution)/shard_map/ppermute | solution.py:394
  12.7 1.6 %copy.10.x_cols = s32[16,16,8]{2,1,0:T(8,128)} copy(s32[16,16,8]{1,2,0:T(8,128)} %param.13) | data formatting | bytes 16384 | tf_op args[2]
  15.6 4.6 %shard_map.86 = (s32[8,128]{1,0:T(8,128)S(1)}, s32[8,128]{1,0:T(8,128)}) custom-call(s32[2]{0:T(128)} %pad_add_fusion.at, s32[16,16,8]{2,1,0:T(8,128)} %copy.9.x_rows, s32[16,16,8]{2,1,0:T(8,128)} %copy.10.x_cols, s32[16,16,16]{2,1,0:T(8,128)} %y_rows.3, s32[16,16,16]{2,1,0:T(8,128)} %y_cols.3, s32[16,16,24]{2,1,0:T(8,128)} %z_rows.3, s32[16,16,24]{2,1,0:T(8,128)} %z_cols.3), custom_call_target="tpu_custom_call" | custom-call | tf_op jit(solution)/shard_map/pallas_call | solution.py:417
  20.3 3.3 %shard_map.87 = (bf16[10,128,128]{2,1,0:T(8,128)(2,1)}, bf16[10,128,128]{2,1,0:T(8,128)(2,1)}, bf16[10,128,128]{2,1,0:T(8,128)(2,1)}, bf16[7,128,128]{2,1,0:T(8,...) custom-call(s32[8,128]{1,0:T(8,128)S(1)} %get-tuple-element.111.table.left_send, ...), custom_call_target="tpu_custom_call" | custom-call | tf_op jit(solution)/shard_map/pallas_call | solution.py:294
  24.5 1.5 %collective-permute-start.20 = (bf16[10,128,128]{2,1,0:T(8,128)(2,1)}, bf16[10,128,128]{2,1,0:T(8,128)(2,1)S(1)}, u32[]{:S(2)}, u32[]{:S(2)}) collective-permute-start(bf16[10,128,128]{2,1,0:T(8,128)(2,1)} %get-tuple-element.122), channel_id=1, source_target_pairs={{0,2},{1,3},{2,0},{3,1},{4,6},{5,7},{6,4},{7,5},{8,10},{9,11},{10,... | collective-permute-start | bytes 983048 | tf_op jit(solution)/shard_map/ppermute | solution.py:398
  27.2 1.4 collective-permute-start.22
  28.6 2.6 %collective-permute-start.24 = (bf16[16,128,128]{2,1,0:T(8,128)(2,1)S(1)}, bf16[16,128,128]{2,1,0:T(8,128)(2,1)S(1)}, u32[]{:S(2)}, u32[]{:S(2)}) collective-permute-start(bf16[16,128,128]{2,1,0:T(8,128)(2,1)S(1)} %pad_maximum_fusion.refs_7_), channel_id=1, source_target_pairs={{0,64},{16,80},{32,96},{48,112},{64,0},{80,16},{96,32},{112,48},{1... | collective-permute-start | bytes 1572872 | tf_op jit(solution)/shard_map/ppermute | solution.py:394
  31.2 7.7 %collective-permute-done.19.refs_4_ = bf16[10,128,128]{2,1,0:T(8,128)(2,1)S(1)} collective-permute-done((bf16[10,128,128]{2,1,0:T(8,128)(2,1)}, bf16[10,128,128]{2,1,0:T(8,128)(2,1)S(1)}, u32[]{:S(2)}, u32[]{:S(2)}) %collective-permute-start.19) | collective-permute-done | bytes 327712 | tf_op jit(solution)/shard_map/ppermute | solution.py:398
  38.9 2.7 %collective-permute-start.23 = (bf16[16,128,128]{2,1,0:T(8,128)(2,1)S(1)}, bf16[16,128,128]{2,1,0:T(8,128)(2,1)S(1)}, u32[]{:S(2)}, u32[]{:S(2)}) collective-permute-start(bf16[16,128,128]{2,1,0:T(8,128)(2,1)S(1)} %pad_maximum_fusion.refs_7_), channel_id=1, source_target_pairs={{0,96},{16,112},{32,0},{48,16},{64,32},{80,48},{96,64},{112,80},{1... | collective-permute-start | bytes 1572872 | tf_op jit(solution)/shard_map/ppermute | solution.py:394
  41.6 2.5 %collective-permute-start.25 = (bf16[16,128,128]{2,1,0:T(8,128)(2,1)S(1)}, bf16[16,128,128]{2,1,0:T(8,128)(2,1)}, u32[]{:S(2)}, u32[]{:S(2)}) collective-permute-start(bf16[16,128,128]{2,1,0:T(8,128)(2,1)S(1)} %pad_maximum_fusion.refs_7_), channel_id=1, source_target_pairs={{0,16},{16,0},{32,48},{48,32},{64,80},{80,64},{96,112},{112,96},{1... | collective-permute-start | bytes 1572872 | tf_op jit(solution)/shard_map/ppermute | solution.py:394
  44.3 6.6 %shard_map.88 = (s32[16,128]{1,0:T(8,128)S(1)}, s32[16,128]{1,0:T(8,128)}, s32[24,128]{1,0:T(8,128)}) custom-call(s32[2]{0:T(128)} %pad_add_fusion.at, s32[8,128]{1,0:T(8,128)S(1)} %get-tuple-element.111.table.left_send, s32[8,128]{1,0:T(8,128)} %get-tuple-element.126.positions, s32[16,16,8]{2,1,0:T(8,128)} %copy.9.x_rows, s32[16,16,8]{2,1,0:T(8,128)} %copy.10.x_cols, ...), custom_call_target="tpu_custom_call" | custom-call | tf_op jit(solution)/shard_map/pallas_call | solution.py:433
  50.9 4.6 %collective-permute-done.21.refs_6_ = bf16[10,128,128]{2,1,0:T(8,128)(2,1)S(1)} collective-permute-done((bf16[10,128,128]{2,1,0:T(8,128)(2,1)}, bf16[10,128,128]{2,1,0:T(8,128)(2,1)S(1)}, u32[]{:S(2)}, u32[]{:S(2)}) %collective-permute-start.21) | collective-permute-done | bytes 327712 | tf_op jit(solution)/shard_map/ppermute | solution.py:398
  57.0 4.5 %collective-permute-start.34 = (bf16[7,128,128]{2,1,0:T(8,128)(2,1)}, bf16[7,128,128]{2,1,0:T(8,128)(2,1)S(1)}, u32[]{:S(2)}, u32[]{:S(2)}) collective-permute-start(bf16[7,128,128]{2,1,0:T(8,128)(2,1)} %get-tuple-element.146), channel_id=1, source_target_pairs={{0,1},{1,0},{2,3},{3,2},{4,5},{5,4},{6,7},{7,6},{8,9},{9,8},{10,11... | collective-permute-start | bytes 688136 | tf_op jit(solution)/shard_map/ppermute | solution.py:398
  61.5 3.8 %shard_map.89.refs_0_.refs_10_ = bf16[16,128,128]{2,1,0:T(8,128)(2,1)} custom-call(s32[16,128]{1,0:T(8,128)S(1)} %copy-done.3, bf16[8,128,128]{2,1,0:T(8,128)(2,1)} %bitcast.11, bf16[8,128,128]{2,1,0:T(8,128)(2,1)} %collective-permute-done.15.refs_1_, bf16[8,128,128]{2,1,0:T(8,128)(2,1)} %collective-permute-done.16.refs_2_, ...), custom_call_target="tpu_custom_call" | custom-call | tf_op jit(solution)/shard_map/pallas_call | solution.py:377
  65.3 3.5 %collective-permute-start.29 = (bf16[16,128,128]{2,1,0:T(8,128)(2,1)}, bf16[16,128,128]{2,1,0:T(8,128)(2,1)}, u32[]{:S(2)}, u32[]{:S(2)}) collective-permute-start(bf16[16,128,128]{2,1,0:T(8,128)(2,1)} %shard_map.89.refs_0_.refs_10_), channel_id=1, source_target_pairs={{0,128},{16,144},{32,160},{48,176},{64,192},{80,208},{96,224},{112... | collective-permute-start | bytes 1572872 | tf_op jit(solution)/shard_map/ppermute | solution.py:394
  69.5 2.9 %shard_map.90 = (bf16[10,128,128]{2,1,0:T(8,128)(2,1)}, bf16[10,128,128]{2,1,0:T(8,128)(2,1)}, bf16[10,128,128]{2,1,0:T(8,128)(2,1)}) custom-call(s32[16,128]{1,0:T(8,128)S(1)} %get-tuple-element.142.table, bf16[16,128,128]{2,1,0:T(8,128)(2,1)} %shard_map.89.refs_0_.refs_10_), custom_call_target="tpu_custom_call" | custom-call | tf_op jit(solution)/shard_map/pallas_call | solution.py:294
  73.0 2.2 %collective-permute-start.32 = (bf16[10,128,128]{2,1,0:T(8,128)(2,1)}, bf16[10,128,128]{2,1,0:T(8,128)(2,1)S(1)}, u32[]{:S(2)}, u32[]{:S(2)}) collective-permute-start(bf16[10,128,128]{2,1,0:T(8,128)(2,1)} %get-tuple-element.144), channel_id=1, source_target_pairs={{0,96},{16,112},{32,0},{48,16},{64,32},{80,48},{96,64},{112,80},{1... | collective-permute-start | bytes 983048 | tf_op jit(solution)/shard_map/ppermute | solution.py:394
  77.1 6.2 %collective-permute-done.31.refs_12_ = bf16[10,128,128]{2,1,0:T(8,128)(2,1)S(1)} collective-permute-done((bf16[10,128,128]{2,1,0:T(8,128)(2,1)}, bf16[10,128,128]{2,1,0:T(8,128)(2,1)S(1)}, u32[]{:S(2)}, u32[]{:S(2)}) %collective-permute-start.31) | collective-permute-done | bytes 327712 | tf_op jit(solution)/shard_map/ppermute | solution.py:394
  83.4 7.4 %collective-permute-done.33.refs_16_ = bf16[10,128,128]{2,1,0:T(8,128)(2,1)S(1)} collective-permute-done((bf16[10,128,128]{2,1,0:T(8,128)(2,1)}, bf16[10,128,128]{2,1,0:T(8,128)(2,1)S(1)}, u32[]{:S(2)}, u32[]{:S(2)}) %collective-permute-start.33) | collective-permute-done | bytes 327712 | tf_op jit(solution)/shard_map/ppermute | solution.py:394
  92.0 5.5 %collective-permute-start.39 = (bf16[7,128,128]{2,1,0:T(8,128)(2,1)}, bf16[7,128,128]{2,1,0:T(8,128)(2,1)}, u32[]{:S(2)}, u32[]{:S(2)}) collective-permute-start(bf16[7,128,128]{2,1,0:T(8,128)(2,1)} %get-tuple-element.155), channel_id=1, source_target_pairs={{0,2},{1,3},{2,0},{3,1},{4,6},{5,7},{6,4},{7,5},{8,10},{9,11},{10,... | collective-permute-start | bytes 688136 | tf_op jit(solution)/shard_map/ppermute | solution.py:398
  98.4 2.9 %shard_map.91 = (bf16[10,128,128]{2,1,0:T(8,128)(2,1)}, bf16[10,128,128]{2,1,0:T(8,128)(2,1)}, bf16[10,128,128]{2,1,0:T(8,128)(2,1)}) custom-call(s32[16,128]{1,0:T(8,128)S(1)} %get-tuple-element.142.table, bf16[16,128,128]{2,1,0:T(8,128)(2,1)} %collective-permute-done.29.refs_0_.refs_11_), custom_call_target="tpu_custom_call" | custom-call | tf_op jit(solution)/shard_map/pallas_call | solution.py:294
  101.3 1.1 collective-permute-start.42
  102.5 10.8 %collective-permute-done.39.refs_8_ = bf16[7,128,128]{2,1,0:T(8,128)(2,1)} collective-permute-done((bf16[7,128,128]{2,1,0:T(8,128)(2,1)}, bf16[7,128,128]{2,1,0:T(8,128)(2,1)}, u32[]{:S(2)}, u32[]{:S(2)}) %collective-permute-start.39) | collective-permute-done | bytes 229408 | tf_op jit(solution)/shard_map/ppermute | solution.py:398
  113.3 2.7 %collective-permute-start.37 = (bf16[10,128,128]{2,1,0:T(8,128)(2,1)}, bf16[10,128,128]{2,1,0:T(8,128)(2,1)S(1)}, u32[]{:S(2)}, u32[]{:S(2)}) collective-permute-start(bf16[10,128,128]{2,1,0:T(8,128)(2,1)} %get-tuple-element.152), channel_id=1, source_target_pairs={{0,96},{16,112},{32,0},{48,16},{64,32},{80,48},{96,64},{112,80},{1... | collective-permute-start | bytes 983048 | tf_op jit(solution)/shard_map/ppermute | solution.py:394
  116.0 7.2 %collective-permute-done.36.refs_13_ = bf16[10,128,128]{2,1,0:T(8,128)(2,1)S(1)} collective-permute-done((bf16[10,128,128]{2,1,0:T(8,128)(2,1)}, bf16[10,128,128]{2,1,0:T(8,128)(2,1)S(1)}, u32[]{:S(2)}, u32[]{:S(2)}) %collective-permute-start.36) | collective-permute-done | bytes 327712 | tf_op jit(solution)/shard_map/ppermute | solution.py:394
  123.2 5.6 %collective-permute-done.38.refs_17_ = bf16[10,128,128]{2,1,0:T(8,128)(2,1)S(1)} collective-permute-done((bf16[10,128,128]{2,1,0:T(8,128)(2,1)}, bf16[10,128,128]{2,1,0:T(8,128)(2,1)S(1)}, u32[]{:S(2)}, u32[]{:S(2)}) %collective-permute-start.38) | collective-permute-done | bytes 327712 | tf_op jit(solution)/shard_map/ppermute | solution.py:394
  128.8 3.1 %collective-permute-start.44 = (bf16[10,128,128]{2,1,0:T(8,128)(2,1)S(1)}, bf16[10,128,128]{2,1,0:T(8,128)(2,1)S(1)}, u32[]{:S(2)}, u32[]{:S(2)}) collective-permute-start(bf16[10,128,128]{2,1,0:T(8,128)(2,1)S(1)} %collective-permute-done.36.refs_13_), channel_id=1, source_target_pairs={{0,16},{16,0},{32,48},{48,32},{64,80},{80,64},{96,112},{112,96},{1... | collective-permute-start | bytes 983048 | tf_op jit(solution)/shard_map/ppermute | solution.py:394
  134.0 0.9 copy-done.1
  135.0 5.2 %shard_map.92 = bf16[24,128,128]{2,1,0:T(8,128)(2,1)} custom-call(s32[24,128]{1,0:T(8,128)S(1)} %copy-done.2, bf16[8,128,128]{2,1,0:T(8,128)(2,1)} %bitcast.12, bf16[8,128,128]{2,1,0:T(8,128)(2,1)} %collective-permute-done.15.refs_1_, bf16[8,128,128]{2,1,0:T(8,128)(2,1)} %collective-permute-done.16.refs_2_, ...), custom_call_target="tpu_custom_call" | custom-call | tf_op jit(solution)/shard_map/pallas_call | solution.py:377
  (61 shorter events, 11.5 us)
Async XLA Ops:
  0.6 19.6 %collective-permute-start.15 = (bf16[8,128,128]{2,1,0:T(8,128)(2,1)}, bf16[8,128,128]{2,1,0:T(8,128)(2,1)}, u32[]{:S(2)}, u32[]{:S(2)}) collective-permute-start(bf16[8,128,128]{2,1,0:T(8,128)(2,1)} %bitcast.7), channel_id=1, source_target_pairs={{0,4},{1,5},{2,6},{3,7},{4,8},{5,9},{6,10},{7,11},{8,12},{9,13},{1... | collective-permute-start | bytes 786440 | tf_op jit(solution)/shard_map/ppermute | solution.py:398
  2.7 17.5 %collective-permute-start.16 = (bf16[8,128,128]{2,1,0:T(8,128)(2,1)}, bf16[8,128,128]{2,1,0:T(8,128)(2,1)}, u32[]{:S(2)}, u32[]{:S(2)}) collective-permute-start(bf16[8,128,128]{2,1,0:T(8,128)(2,1)} %bitcast.8), channel_id=1, source_target_pairs={{0,12},{1,13},{2,14},{3,15},{4,0},{5,1},{6,2},{7,3},{8,4},{9,5},{1... | collective-permute-start | bytes 786440 | tf_op jit(solution)/shard_map/ppermute | solution.py:398
  4.1 16.2 %collective-permute-start.17 = (bf16[8,128,128]{2,1,0:T(8,128)(2,1)}, bf16[8,128,128]{2,1,0:T(8,128)(2,1)}, u32[]{:S(2)}, u32[]{:S(2)}) collective-permute-start(bf16[8,128,128]{2,1,0:T(8,128)(2,1)} %bitcast.9), channel_id=1, source_target_pairs={{0,8},{1,9},{2,10},{3,11},{4,12},{5,13},{6,14},{7,15},{8,0},{9,1},... | collective-permute-start | bytes 786440 | tf_op jit(solution)/shard_map/ppermute | solution.py:398
  5.7 17.9 %collective-permute-start.18 = (bf16[8,128,128]{2,1,0:T(8,128)(2,1)}, bf16[8,128,128]{2,1,0:T(8,128)(2,1)S(1)}, u32[]{:S(2)}, u32[]{:S(2)}) collective-permute-start(bf16[8,128,128]{2,1,0:T(8,128)(2,1)} %bitcast.10), channel_id=1, source_target_pairs={{0,128},{16,144},{32,160},{48,176},{64,192},{80,208},{96,224},{112... | collective-permute-start | bytes 786440 | tf_op jit(solution)/shard_map/ppermute | solution.py:394
  23.6 15.2 %collective-permute-start.19 = (bf16[10,128,128]{2,1,0:T(8,128)(2,1)}, bf16[10,128,128]{2,1,0:T(8,128)(2,1)S(1)}, u32[]{:S(2)}, u32[]{:S(2)}) collective-permute-start(bf16[10,128,128]{2,1,0:T(8,128)(2,1)} %get-tuple-element.121), channel_id=1, source_target_pairs={{0,1},{1,0},{2,3},{3,2},{4,5},{5,4},{6,7},{7,6},{8,9},{9,8},{10,11... | collective-permute-start | bytes 983048 | tf_op jit(solution)/shard_map/ppermute | solution.py:398
  24.5 19.6 %collective-permute-start.20 = (bf16[10,128,128]{2,1,0:T(8,128)(2,1)}, bf16[10,128,128]{2,1,0:T(8,128)(2,1)S(1)}, u32[]{:S(2)}, u32[]{:S(2)}) collective-permute-start(bf16[10,128,128]{2,1,0:T(8,128)(2,1)} %get-tuple-element.122), channel_id=1, source_target_pairs={{0,2},{1,3},{2,0},{3,1},{4,6},{5,7},{6,4},{7,5},{8,10},{9,11},{10,... | collective-permute-start | bytes 983048 | tf_op jit(solution)/shard_map/ppermute | solution.py:398
  27.2 28.3 %collective-permute-start.22 = (bf16[16,128,128]{2,1,0:T(8,128)(2,1)S(1)}, bf16[16,128,128]{2,1,0:T(8,128)(2,1)S(1)}, u32[]{:S(2)}, u32[]{:S(2)}) collective-permute-start(bf16[16,128,128]{2,1,0:T(8,128)(2,1)S(1)} %pad_maximum_fusion.refs_7_), channel_id=1, source_target_pairs={{0,32},{16,48},{32,64},{48,80},{64,96},{80,112},{96,0},{112,16},{1... | collective-permute-start | bytes 1572872 | tf_op jit(solution)/shard_map/ppermute | solution.py:394
  28.6 26.9 %collective-permute-start.24 = (bf16[16,128,128]{2,1,0:T(8,128)(2,1)S(1)}, bf16[16,128,128]{2,1,0:T(8,128)(2,1)S(1)}, u32[]{:S(2)}, u32[]{:S(2)}) collective-permute-start(bf16[16,128,128]{2,1,0:T(8,128)(2,1)S(1)} %pad_maximum_fusion.refs_7_), channel_id=1, source_target_pairs={{0,64},{16,80},{32,96},{48,112},{64,0},{80,16},{96,32},{112,48},{1... | collective-permute-start | bytes 1572872 | tf_op jit(solution)/shard_map/ppermute | solution.py:394
  38.9 16.6 %collective-permute-start.23 = (bf16[16,128,128]{2,1,0:T(8,128)(2,1)S(1)}, bf16[16,128,128]{2,1,0:T(8,128)(2,1)S(1)}, u32[]{:S(2)}, u32[]{:S(2)}) collective-permute-start(bf16[16,128,128]{2,1,0:T(8,128)(2,1)S(1)} %pad_maximum_fusion.refs_7_), channel_id=1, source_target_pairs={{0,96},{16,112},{32,0},{48,16},{64,32},{80,48},{96,64},{112,80},{1... | collective-permute-start | bytes 1572872 | tf_op jit(solution)/shard_map/ppermute | solution.py:394
  41.6 13.9 %collective-permute-start.25 = (bf16[16,128,128]{2,1,0:T(8,128)(2,1)S(1)}, bf16[16,128,128]{2,1,0:T(8,128)(2,1)}, u32[]{:S(2)}, u32[]{:S(2)}) collective-permute-start(bf16[16,128,128]{2,1,0:T(8,128)(2,1)S(1)} %pad_maximum_fusion.refs_7_), channel_id=1, source_target_pairs={{0,16},{16,0},{32,48},{48,32},{64,80},{80,64},{96,112},{112,96},{1... | collective-permute-start | bytes 1572872 | tf_op jit(solution)/shard_map/ppermute | solution.py:394
  44.1 11.4 %collective-permute-start.21 = (bf16[10,128,128]{2,1,0:T(8,128)(2,1)}, bf16[10,128,128]{2,1,0:T(8,128)(2,1)S(1)}, u32[]{:S(2)}, u32[]{:S(2)}) collective-permute-start(bf16[10,128,128]{2,1,0:T(8,128)(2,1)} %get-tuple-element.123), channel_id=1, source_target_pairs={{0,3},{1,2},{2,1},{3,0},{4,7},{5,6},{6,5},{7,4},{8,11},{9,10},{10,... | collective-permute-start | bytes 983048 | tf_op jit(solution)/shard_map/ppermute | solution.py:398
  55.5 6.0 %collective-permute-start.26 = (bf16[16,128,128]{2,1,0:T(8,128)(2,1)S(1)}, bf16[16,128,128]{2,1,0:T(8,128)(2,1)S(1)}, u32[]{:S(2)}, u32[]{:S(2)}) collective-permute-start(bf16[16,128,128]{2,1,0:T(8,128)(2,1)S(1)} %collective-permute-done.22.refs_8_), channel_id=1, source_target_pairs={{0,16},{16,0},{32,48},{48,32},{64,80},{80,64},{96,112},{112,96},{1... | collective-permute-start | bytes 1572872 | tf_op jit(solution)/shard_map/ppermute | solution.py:394
  56.5 5.0 %collective-permute-start.27 = (bf16[16,128,128]{2,1,0:T(8,128)(2,1)S(1)}, bf16[16,128,128]{2,1,0:T(8,128)(2,1)S(1)}, u32[]{:S(2)}, u32[]{:S(2)}) collective-permute-start(bf16[16,128,128]{2,1,0:T(8,128)(2,1)S(1)} %collective-permute-done.23.refs_9_), channel_id=1, source_target_pairs={{0,16},{16,0},{32,48},{48,32},{64,80},{80,64},{96,112},{112,96},{1... | collective-permute-start | bytes 1572872 | tf_op jit(solution)/shard_map/ppermute | solution.py:394
  56.6 4.9 %collective-permute-start.28 = (bf16[16,128,128]{2,1,0:T(8,128)(2,1)S(1)}, bf16[16,128,128]{2,1,0:T(8,128)(2,1)S(1)}, u32[]{:S(2)}, u32[]{:S(2)}) collective-permute-start(bf16[16,128,128]{2,1,0:T(8,128)(2,1)S(1)} %collective-permute-done.24.refs_10_), channel_id=1, source_target_pairs={{0,16},{16,0},{32,48},{48,32},{64,80},{80,64},{96,112},{112,96},{1... | collective-permute-start | bytes 1572872 | tf_op jit(solution)/shard_map/ppermute | solution.py:394
  57.0 18.2 %collective-permute-start.34 = (bf16[7,128,128]{2,1,0:T(8,128)(2,1)}, bf16[7,128,128]{2,1,0:T(8,128)(2,1)S(1)}, u32[]{:S(2)}, u32[]{:S(2)}) collective-permute-start(bf16[7,128,128]{2,1,0:T(8,128)(2,1)} %get-tuple-element.146), channel_id=1, source_target_pairs={{0,1},{1,0},{2,3},{3,2},{4,5},{5,4},{6,7},{7,6},{8,9},{9,8},{10,11... | collective-permute-start | bytes 688136 | tf_op jit(solution)/shard_map/ppermute | solution.py:398
  65.3 25.4 %collective-permute-start.29 = (bf16[16,128,128]{2,1,0:T(8,128)(2,1)}, bf16[16,128,128]{2,1,0:T(8,128)(2,1)}, u32[]{:S(2)}, u32[]{:S(2)}) collective-permute-start(bf16[16,128,128]{2,1,0:T(8,128)(2,1)} %shard_map.89.refs_0_.refs_10_), channel_id=1, source_target_pairs={{0,128},{16,144},{32,160},{48,176},{64,192},{80,208},{96,224},{112... | collective-permute-start | bytes 1572872 | tf_op jit(solution)/shard_map/ppermute | solution.py:394
  68.9 21.9 %collective-permute-start.30 = (bf16[16,128,128]{2,1,0:T(8,128)(2,1)}, bf16[16,128,128]{2,1,0:T(8,128)(2,1)S(1)}, u32[]{:S(2)}, u32[]{:S(2)}) collective-permute-start(bf16[16,128,128]{2,1,0:T(8,128)(2,1)} %shard_map.89.refs_0_.refs_10_), channel_id=1, source_target_pairs={{0,16},{16,0},{32,48},{48,32},{64,80},{80,64},{96,112},{112,96},{1... | collective-permute-start | bytes 1572872 | tf_op jit(solution)/shard_map/ppermute | solution.py:394
  72.4 10.9 %collective-permute-start.31 = (bf16[10,128,128]{2,1,0:T(8,128)(2,1)}, bf16[10,128,128]{2,1,0:T(8,128)(2,1)S(1)}, u32[]{:S(2)}, u32[]{:S(2)}) collective-permute-start(bf16[10,128,128]{2,1,0:T(8,128)(2,1)} %get-tuple-element.143), channel_id=1, source_target_pairs={{0,32},{16,48},{32,64},{48,80},{64,96},{80,112},{96,0},{112,16},{1... | collective-permute-start | bytes 983048 | tf_op jit(solution)/shard_map/ppermute | solution.py:394
  73.0 10.4 %collective-permute-start.32 = (bf16[10,128,128]{2,1,0:T(8,128)(2,1)}, bf16[10,128,128]{2,1,0:T(8,128)(2,1)S(1)}, u32[]{:S(2)}, u32[]{:S(2)}) collective-permute-start(bf16[10,128,128]{2,1,0:T(8,128)(2,1)} %get-tuple-element.144), channel_id=1, source_target_pairs={{0,96},{16,112},{32,0},{48,16},{64,32},{80,48},{96,64},{112,80},{1... | collective-permute-start | bytes 983048 | tf_op jit(solution)/shard_map/ppermute | solution.py:394
  75.2 15.5 %collective-permute-start.33 = (bf16[10,128,128]{2,1,0:T(8,128)(2,1)}, bf16[10,128,128]{2,1,0:T(8,128)(2,1)S(1)}, u32[]{:S(2)}, u32[]{:S(2)}) collective-permute-start(bf16[10,128,128]{2,1,0:T(8,128)(2,1)} %get-tuple-element.145), channel_id=1, source_target_pairs={{0,64},{16,80},{32,96},{48,112},{64,0},{80,16},{96,32},{112,48},{1... | collective-permute-start | bytes 983048 | tf_op jit(solution)/shard_map/ppermute | solution.py:394
  91.0 11.4 %collective-permute-start.35 = (bf16[16,128,128]{2,1,0:T(8,128)(2,1)}, bf16[16,128,128]{2,1,0:T(8,128)(2,1)S(1)}, u32[]{:S(2)}, u32[]{:S(2)}) collective-permute-start(bf16[16,128,128]{2,1,0:T(8,128)(2,1)} %collective-permute-done.29.refs_0_.refs_11_), channel_id=1, source_target_pairs={{0,16},{16,0},{32,48},{48,32},{64,80},{80,64},{96,112},{112,96},{1... | collective-permute-start | bytes 1572872 | tf_op jit(solution)/shard_map/ppermute | solution.py:394
  91.9 24.1 %collective-permute-start.41 = (bf16[10,128,128]{2,1,0:T(8,128)(2,1)S(1)}, bf16[10,128,128]{2,1,0:T(8,128)(2,1)S(1)}, u32[]{:S(2)}, u32[]{:S(2)}) collective-permute-start(bf16[10,128,128]{2,1,0:T(8,128)(2,1)S(1)} %collective-permute-done.31.refs_12_), channel_id=1, source_target_pairs={{0,16},{16,0},{32,48},{48,32},{64,80},{80,64},{96,112},{112,96},{1... | collective-permute-start | bytes 983048 | tf_op jit(solution)/shard_map/ppermute | solution.py:394
  92.0 21.3 %collective-permute-start.39 = (bf16[7,128,128]{2,1,0:T(8,128)(2,1)}, bf16[7,128,128]{2,1,0:T(8,128)(2,1)}, u32[]{:S(2)}, u32[]{:S(2)}) collective-permute-start(bf16[7,128,128]{2,1,0:T(8,128)(2,1)} %get-tuple-element.155), channel_id=1, source_target_pairs={{0,2},{1,3},{2,0},{3,1},{4,6},{5,7},{6,4},{7,5},{8,10},{9,11},{10,... | collective-permute-start | bytes 688136 | tf_op jit(solution)/shard_map/ppermute | solution.py:398
  97.5 15.8 %collective-permute-start.40 = (bf16[7,128,128]{2,1,0:T(8,128)(2,1)}, bf16[7,128,128]{2,1,0:T(8,128)(2,1)}, u32[]{:S(2)}, u32[]{:S(2)}) collective-permute-start(bf16[7,128,128]{2,1,0:T(8,128)(2,1)} %get-tuple-element.156), channel_id=1, source_target_pairs={{0,3},{1,2},{2,1},{3,0},{4,7},{5,6},{6,5},{7,4},{8,11},{9,10},{10,... | collective-permute-start | bytes 688136 | tf_op jit(solution)/shard_map/ppermute | solution.py:398
  101.3 14.7 %collective-permute-start.42 = (bf16[10,128,128]{2,1,0:T(8,128)(2,1)S(1)}, bf16[10,128,128]{2,1,0:T(8,128)(2,1)S(1)}, u32[]{:S(2)}, u32[]{:S(2)}) collective-permute-start(bf16[10,128,128]{2,1,0:T(8,128)(2,1)S(1)} %collective-permute-done.32.refs_14_), channel_id=1, source_target_pairs={{0,16},{16,0},{32,48},{48,32},{64,80},{80,64},{96,112},{112,96},{1... | collective-permute-start | bytes 983048 | tf_op jit(solution)/shard_map/ppermute | solution.py:394
  102.3 13.6 %collective-permute-start.43 = (bf16[10,128,128]{2,1,0:T(8,128)(2,1)S(1)}, bf16[10,128,128]{2,1,0:T(8,128)(2,1)S(1)}, u32[]{:S(2)}, u32[]{:S(2)}) collective-permute-start(bf16[10,128,128]{2,1,0:T(8,128)(2,1)S(1)} %collective-permute-done.33.refs_16_), channel_id=1, source_target_pairs={{0,16},{16,0},{32,48},{48,32},{64,80},{80,64},{96,112},{112,96},{1... | collective-permute-start | bytes 983048 | tf_op jit(solution)/shard_map/ppermute | solution.py:394
  113.3 9.9 %collective-permute-start.36 = (bf16[10,128,128]{2,1,0:T(8,128)(2,1)}, bf16[10,128,128]{2,1,0:T(8,128)(2,1)S(1)}, u32[]{:S(2)}, u32[]{:S(2)}) collective-permute-start(bf16[10,128,128]{2,1,0:T(8,128)(2,1)} %get-tuple-element.151), channel_id=1, source_target_pairs={{0,32},{16,48},{32,64},{48,80},{64,96},{80,112},{96,0},{112,16},{1... | collective-permute-start | bytes 983048 | tf_op jit(solution)/shard_map/ppermute | solution.py:394
  113.3 9.9 %collective-permute-start.37 = (bf16[10,128,128]{2,1,0:T(8,128)(2,1)}, bf16[10,128,128]{2,1,0:T(8,128)(2,1)S(1)}, u32[]{:S(2)}, u32[]{:S(2)}) collective-permute-start(bf16[10,128,128]{2,1,0:T(8,128)(2,1)} %get-tuple-element.152), channel_id=1, source_target_pairs={{0,96},{16,112},{32,0},{48,16},{64,32},{80,48},{96,64},{112,80},{1... | collective-permute-start | bytes 983048 | tf_op jit(solution)/shard_map/ppermute | solution.py:394
  116.0 12.8 %collective-permute-start.38 = (bf16[10,128,128]{2,1,0:T(8,128)(2,1)}, bf16[10,128,128]{2,1,0:T(8,128)(2,1)S(1)}, u32[]{:S(2)}, u32[]{:S(2)}) collective-permute-start(bf16[10,128,128]{2,1,0:T(8,128)(2,1)} %get-tuple-element.153), channel_id=1, source_target_pairs={{0,64},{16,80},{32,96},{48,112},{64,0},{80,16},{96,32},{112,48},{1... | collective-permute-start | bytes 983048 | tf_op jit(solution)/shard_map/ppermute | solution.py:394
  128.8 4.3 %collective-permute-start.44 = (bf16[10,128,128]{2,1,0:T(8,128)(2,1)S(1)}, bf16[10,128,128]{2,1,0:T(8,128)(2,1)S(1)}, u32[]{:S(2)}, u32[]{:S(2)}) collective-permute-start(bf16[10,128,128]{2,1,0:T(8,128)(2,1)S(1)} %collective-permute-done.36.refs_13_), channel_id=1, source_target_pairs={{0,16},{16,0},{32,48},{48,32},{64,80},{80,64},{96,112},{112,96},{1... | collective-permute-start | bytes 983048 | tf_op jit(solution)/shard_map/ppermute | solution.py:394
  131.9 1.7 %collective-permute-start.45 = (bf16[10,128,128]{2,1,0:T(8,128)(2,1)S(1)}, bf16[10,128,128]{2,1,0:T(8,128)(2,1)S(1)}, u32[]{:S(2)}, u32[]{:S(2)}) collective-permute-start(bf16[10,128,128]{2,1,0:T(8,128)(2,1)S(1)} %collective-permute-done.37.refs_15_), channel_id=1, source_target_pairs={{0,16},{16,0},{32,48},{48,32},{64,80},{80,64},{96,112},{112,96},{1... | collective-permute-start | bytes 983048 | tf_op jit(solution)/shard_map/ppermute | solution.py:394
  131.9 2.1 %collective-permute-start.46 = (bf16[10,128,128]{2,1,0:T(8,128)(2,1)S(1)}, bf16[10,128,128]{2,1,0:T(8,128)(2,1)S(1)}, u32[]{:S(2)}, u32[]{:S(2)}) collective-permute-start(bf16[10,128,128]{2,1,0:T(8,128)(2,1)S(1)} %collective-permute-done.38.refs_17_), channel_id=1, source_target_pairs={{0,16},{16,0},{32,48},{48,32},{64,80},{80,64},{96,112},{112,96},{1... | collective-permute-start | bytes 983048 | tf_op jit(solution)/shard_map/ppermute | solution.py:394
  (6 other events, 64.9 us)

commit v2 on v1

--- a/solution.py
+++ b/solution.py
@@ -14,6 +14,8 @@
 COUNT = 32
 OWN = 33
 FLAG = 34
+MULTIS = 35
+MULTI = 40
 LEFT_FIRST = 10
 LEFT_ALL = 17
 RIGHT_FIRST = 10
@@ -178,6 +180,13 @@
     for q in range(TERMS):
         picked = jnp.where(hit & (rank == q + 1.0), code, 0.0)
         table = table + jnp.where(lane == q, jnp.sum(picked, axis=1, keepdims=True), 0.0)
+    multi = (jnp.sum(marks, axis=1, keepdims=True) > 1.5).astype(jnp.float32)
+    multi = jnp.broadcast_to(multi, (outs, 128))
+    order = nn(iota((outs, outs), 1) <= iota((outs, outs), 0), multi)
+    slots = (multi > 0.5) & (order == (lane - (MULTI - 1)).astype(jnp.float32))
+    entries = nn(iota((8, outs), 1), slots)[:1]
+    entries = entries + jnp.where(lane[:1] == MULTIS, jnp.sum(multi, axis=0, keepdims=True), 0.0)
+    table = table + jnp.where(iota((outs, 128), 0) == 0, entries, 0.0)
     return table, lane
 
 
@@ -259,10 +268,11 @@
     z_plan[...] = table.astype(jnp.int32)
 
 
-def pack_kernel(unit, count, first_row, start, sizes, table, *refs):
-    sources, outs = refs[:count], refs[count : count + 3 * len(sizes)]
-    held, in_sems, out_sems = refs[count + 3 * len(sizes) :]
-    loads = [
+def pack_kernel(unit, count, parts, given, *refs):
+    sources, outs = refs[:count], refs[count : count + len(parts)]
+    held, table, in_sems, out_sems = refs[count + len(parts) :]
+    loads = [pltpu.make_async_copy(given, table, in_sems.at[count])]
+    loads += [
         pltpu.make_async_copy(source, held.at[pl.ds(n * unit, unit)], in_sems.at[n])
         for n, source in enumerate(sources)
     ]
@@ -271,55 +281,49 @@
     for load in loads:
         load.wait()
     copies = []
-    at = start
-    for group, size in enumerate(sizes):
-        for n in range(size):
-            for d in range(3):
-                copies.append(
-                    pltpu.make_async_copy(
-                        held.at[table[first_row + d, at + n]],
-                        outs[group * 3 + d].at[n],
-                        out_sems.at[len(copies)],
-                    )
+    for (row, first, last), out in zip(parts, outs):
+        for n in range(last - first):
+            copies.append(
+                pltpu.make_async_copy(
+                    held.at[table[row, first + n]], out.at[n], out_sems.at[len(copies)]
                 )
-        at += size
+            )
     for copy in copies:
         copy.start()
     for copy in copies:
         copy.wait()
 
 
-def pack(table, sources, first_row, start, *sizes):
+def pack(table, sources, *parts):
     unit = sources[0].shape[0]
+    sizes = [last - first for _, first, last in parts]
     return pl.pallas_call(
-        functools.partial(pack_kernel, unit, len(sources), first_row, start, sizes),
-        out_shape=[
-            jax.ShapeDtypeStruct((size, BLOCK, BLOCK), jnp.bfloat16)
-            for size in sizes
-            for _ in range(3)
-        ],
-        in_specs=[pl.BlockSpec(memory_space=pltpu.SMEM)]
-        + [pl.BlockSpec(memory_space=pl.ANY)] * len(sources),
-        out_specs=[pl.BlockSpec(memory_space=pl.ANY)] * (3 * len(sizes)),
+        functools.partial(pack_kernel, unit, len(sources), parts),
+        out_shape=[jax.ShapeDtypeStruct((size, BLOCK, BLOCK), jnp.bfloat16) for size in sizes],
+        in_specs=[pl.BlockSpec(memory_space=pl.ANY)] * (1 + len(sources)),
+        out_specs=[pl.BlockSpec(memory_space=pl.ANY)] * len(sizes),
         scratch_shapes=[
             pltpu.VMEM((unit * len(sources), BLOCK, BLOCK), jnp.bfloat16),
-            pltpu.SemaphoreType.DMA((len(sources),)),
-            pltpu.SemaphoreType.DMA((3 * sum(sizes),)),
+            pltpu.SMEM(table.shape, jnp.int32),
+            pltpu.SemaphoreType.DMA((len(sources) + 1,)),
+            pltpu.SemaphoreType.DMA((sum(sizes),)),
         ],
     )(table, *sources)
 
 
-def nothing(count, size):
+def nothing(sizes):
     return pl.pallas_call(
         lambda *refs: None,
-        out_shape=[jax.ShapeDtypeStruct((size, BLOCK, BLOCK), jnp.bfloat16)] * count,
-        out_specs=[pl.BlockSpec(memory_space=pl.ANY)] * count,
+        out_shape=[jax.ShapeDtypeStruct((size, BLOCK, BLOCK), jnp.bfloat16) for size in sizes],
+        out_specs=[pl.BlockSpec(memory_space=pl.ANY)] * len(sizes),
     )()
 
 
-def products_kernel(layout, update, plan, *refs):
+def products_kernel(layout, update, given, *refs):
     pieces = refs[: len(layout)]
-    out, left, right, total, sems = refs[len(layout) :]
+    out, left, right, plan, sems = refs[len(layout) :]
+    fetch = pltpu.make_async_copy(given, plan, sems.at[len(layout)])
+    fetch.start()
 
     def copy(n):
         side, at, skip, size, _ = layout[n]
@@ -327,19 +331,29 @@
         source = pieces[n] if skip is None else pieces[n].at[pl.ds(skip, size)]
         return pltpu.make_async_copy(source, buffer.at[pl.ds(at, size)], sems.at[n])
 
-    def each(act):
+    def each(act, flagged):
         for n, piece in enumerate(layout):
-            if piece[4]:
-
-                @pl.when(plan[0, FLAG] & piece[4] != 0)
+            if (piece[4] > 0) != flagged:
+                continue
+            if flagged:
+
+                @pl.when(flag & piece[4] != 0)
                 def _():
                     act(copy(n))
 
             else:
                 act(copy(n))
 
-    each(lambda c: c.start())
-    each(lambda c: c.wait())
+    each(lambda c: c.start(), False)
+    fetch.wait()
+    flag = plan[0, FLAG]
+
+    @pl.when(flag > 0)
+    def _():
+        each(lambda c: c.start(), True)
+        each(lambda c: c.wait(), True)
+
+    each(lambda c: c.wait(), False)
 
     def product(t, q):
         code = plan[t, q]
@@ -347,26 +361,23 @@
             left[code >> 8], right[code & 255], preferred_element_type=jnp.float32
         )
 
-    outs = out.shape[0]
-    for t in range(outs):
-        total[t] = jnp.where(plan[t, COUNT] > 0, product(t, 0), 0.0)
-
-    def more(t, carry):
-        def term(q, inner):
-            total[t] += product(t, q)
-            return inner
-
-        return lax.fori_loop(1, plan[t, COUNT], term, carry)
-
-    lax.fori_loop(0, outs, more, 0)
-    for t in range(outs):
+    def write(t, value):
         if update:
             slot = plan[t, OWN]
             x_here = left[jnp.maximum(slot - 1, 0)].astype(jnp.float32)
-            x_here = jnp.where(slot > 0, x_here, 0.0)
-            out[t] = (1.5 * x_here - 0.5 * total[t]).astype(jnp.bfloat16)
-        else:
-            out[t] = total[t].astype(jnp.bfloat16)
+            value = 1.5 * jnp.where(slot > 0, x_here, 0.0) - 0.5 * value
+        out[t] = value.astype(jnp.bfloat16)
+
+    for t in range(out.shape[0]):
+        write(t, jnp.where(plan[t, COUNT] > 0, product(t, 0), 0.0))
+
+    def again(n, carry):
+        t = plan[0, MULTI + n]
+        terms = plan[t, COUNT]
+        write(t, lax.fori_loop(1, terms, lambda q, total: total + product(t, q), product(t, 0)))
+        return carry
+
+    lax.fori_loop(0, plan[0, MULTIS], again, 0)
 
 
 def products(plan, pieces, sizes, update):
@@ -377,14 +388,13 @@
     return pl.pallas_call(
         functools.partial(products_kernel, layout, update),
         out_shape=jax.ShapeDtypeStruct((outs, BLOCK, BLOCK), jnp.bfloat16),
-        in_specs=[pl.BlockSpec(memory_space=pltpu.SMEM)]
-        + [pl.BlockSpec(memory_space=pl.ANY)] * len(pieces),
+        in_specs=[pl.BlockSpec(memory_space=pl.ANY)] * (1 + len(pieces)),
         out_specs=pl.BlockSpec(memory_space=pltpu.VMEM),
         scratch_shapes=[
             pltpu.VMEM((sizes[0], BLOCK, BLOCK), jnp.bfloat16),
             pltpu.VMEM((sizes[1], BLOCK, BLOCK), jnp.bfloat16),
-            pltpu.VMEM((outs, BLOCK, BLOCK), jnp.float32),
-            pltpu.SemaphoreType.DMA((len(pieces),)),
+            pltpu.SMEM(plan.shape, jnp.int32),
+            pltpu.SemaphoreType.DMA((len(pieces) + 1,)),
         ],
         compiler_params=pltpu.CompilerParams(vmem_limit_bytes=32 * 1024 * 1024),
     )(plan, *[p[-1] for p in pieces])
@@ -421,15 +431,16 @@
     )(at, *tables)
     near, left_send, positions = lax.optimization_barrier((near, left_send, positions))
     quad = [tile] + near
-    first = pack(left_send, quad, 0, 0, LEFT_FIRST, LEFT_ALL - LEFT_FIRST)
+    ends = (LEFT_FIRST, LEFT_ALL, LEFT_FIRST)
+    parts = [(d, 0, end) for d, end in enumerate(ends)]
+    parts += [(d, LEFT_FIRST, LEFT_ALL) for d in (0, 2)]
+    first = pack(left_send, quad, *parts)
     first, far = lax.optimization_barrier((first, far))
     first, second = first[:3], first[3:]
-    first = [col_send(blocks, swap) for blocks, swap in zip(first, B_SWAP)]
+    one, two = [col_send(blocks, swap) for blocks, swap in zip(first[:2], B_SWAP[:2])]
+    first = [one, two, col_send(after(first[2], one), B_SWAP[2])]
     pair = jnp.concatenate([tile, far])
-    across = row_send(pair, Y_RING[2])
-    up = row_send(pair, Y_RING[0])
-    down = row_send(after(pair, first[0]), Y_RING[1])
-    pair_mate = row_send(after(pair, first[0]), CORE_SWAP)
+    across, up, down = [row_send(pair, Y_RING[n]) for n in (2, 0, 1)]
     right_send, y_plan, z_plan = pl.pallas_call(
         right_kernel,
         out_shape=(
@@ -439,54 +450,56 @@
         ),
         in_specs=[smem, smem] + [vmem] * 7,
     )(at, left_send, positions, *tables)
-    first, up, down, across, pair_mate, right_send, y_plan, z_plan = lax.optimization_barrier(
-        (first, up, down, across, pair_mate, right_send, y_plan, z_plan)
+    first, up, down, across, right_send, y_plan, z_plan = lax.optimization_barrier(
+        (first, up, down, across, right_send, y_plan, z_plan)
     )
     x_half = [pair, up, down, across]
-    x_mate = [pair_mate] + [row_send(blocks, CORE_SWAP) for blocks in x_half[1:]]
-    one = col_send(second[0], B_SWAP[0])
+    x_mate = [row_send(blocks, CORE_SWAP) for blocks in x_half]
 
     def more_left():
-        rest = pack(left_send, quad, 0, LEFT_FIRST, MOST - LEFT_FIRST)
+        rest = pack(left_send, quad, *[(d, end, MOST) for d, end in enumerate(ends)])
         return tuple(col_send(blocks, swap) for blocks, swap in zip(rest, B_SWAP))
 
     rest = lax.cond(
-        left_send[3, 0] > 0, more_left, lambda: tuple(nothing(3, MOST - LEFT_FIRST))
+        left_send[3, 0] > 0, more_left, lambda: tuple(nothing([MOST - end for end in ends]))
     )
 
     left = [(0, 8 * n, None, 0, p) for n, p in enumerate(quad)]
     left += [(0, MOST * (n + 1), None, 0, p) for n, p in enumerate(first)]
     right = [(1, 16 * n, None, 0, p) for n, p in enumerate(x_half + x_mate)]
-    extra = [(0, MOST * (n + 1) + LEFT_FIRST, None, 1, p) for n, p in enumerate(rest)]
+    extra = [(0, MOST * (n + 1) + end, None, 1, p) for n, (end, p) in enumerate(zip(ends, rest))]
     y_tile = products(y_plan, left + right + extra, (4 * MOST, 128), False)
 
     y_far = row_send(y_tile, Z_SWAP)
     tile_mate = row_send(y_tile, CORE_SWAP)
-    own_send = pack(right_send, [y_tile], 0, 0, RIGHT_FIRST)
+    own_send = pack(right_send, [y_tile], *[(d, 0, RIGHT_FIRST) for d in range(3)])
     own_near = [row_send(blocks, ring) for blocks, ring in zip(own_send, Y_RING)]
-    y_far, tile_mate, own_near, one = lax.optimization_barrier((y_far, tile_mate, own_near, one))
-    far_send = pack(right_send, [y_far], 8, 0, RIGHT_FIRST)
+    y_far, tile_mate, own_near = lax.optimization_barrier((y_far, tile_mate, own_near))
+    own_mate = [row_send(blocks, CORE_SWAP) for blocks in own_near]
+    far_send = pack(right_send, [y_far], *[(8 + d, 0, RIGHT_FIRST) for d in range(3)])
     far_mate = row_send(y_far, CORE_SWAP)
-    far_send, far_mate = lax.optimization_barrier((far_send, far_mate))
+    far_send, far_mate, own_mate, second = lax.optimization_barrier(
+        (far_send, far_mate, own_mate, second)
+    )
     far_near = [row_send(blocks, ring) for blocks, ring in zip(far_send, Y_RING)]
-    second = [one] + [col_send(blocks, swap) for blocks, swap in zip(second[1:], B_SWAP[1:])]
-    own_mate = [row_send(blocks, CORE_SWAP) for blocks in own_near]
-    far_near, second, own_mate = lax.optimization_barrier((far_near, second, own_mate))
+    second = [col_send(blocks, swap) for blocks, swap in zip(second, B_SWAP[::2])]
+    far_near, second = lax.optimization_barrier((far_near, second))
     far_near_mate = [row_send(blocks, CORE_SWAP) for blocks in far_near]
 
     def more_right():
-        blocks = pack(right_send, [y_tile], 0, RIGHT_FIRST, y_most - RIGHT_FIRST)
-        blocks += pack(right_send, [y_far], 8, RIGHT_FIRST, y_most - RIGHT_FIRST)
+        blocks = pack(right_send, [y_tile], *[(d, RIGHT_FIRST, y_most) for d in range(3)])
+        blocks += pack(right_send, [y_far], *[(8 + d, RIGHT_FIRST, y_most) for d in range(3)])
         blocks = [row_send(b, ring) for b, ring in zip(blocks, Y_RING + Y_RING)]
         return tuple(blocks + [row_send(b, CORE_SWAP) for b in blocks])
 
     more = lax.cond(
-        right_send[3, 0] > 0, more_right, lambda: tuple(nothing(12, y_most - RIGHT_FIRST))
-    )
-
-    left += [(0, MOST * (n + 1) + LEFT_FIRST, None, 0, p) for n, p in enumerate(second)]
+        right_send[3, 0] > 0, more_right, lambda: tuple(nothing([y_most - RIGHT_FIRST] * 12))
+    )
+
+    left += [(0, MOST * (2 * n + 1) + LEFT_FIRST, None, 0, p) for n, p in enumerate(second)]
     extra = [
-        (0, MOST * (n + 1) + LEFT_ALL, LEFT_ALL - LEFT_FIRST, 1, p) for n, p in enumerate(rest)
+        (0, MOST * (n + 1) + LEFT_ALL, LEFT_ALL - end, 1, p)
+        for n, (end, p) in enumerate(zip(ends, rest))
     ]
     right = []
     spots = [i * MOST + j * y_most for i in range(4) for j in range(2)]

time: 142 us -> 129 us (0.908)
  waiting for transfers between devices: 51.2 us -> 40.1 us
  Pallas kernels: 29.4 us -> 25.6 us
  starting transfers between devices: 52.4 us -> 56 us
    ppermute x23, starting transfers between devices: 33.8 us -> 40.2 us  [row_send(): return lax.ppermute(blocks, 'row', perm)]
    ppermute x23, waiting for transfers between devices: 28.1 us -> 22.1 us  [row_send(): return lax.ppermute(blocks, 'row', perm)]
    ppermute x9 -> x8, waiting for transfers between devices: 23.1 us -> 18 us  [col_send(): return lax.ppermute(blocks, 'col', perm)]
    ppermute x9 -> x8, starting transfers between devices: 18.6 us -> 15.8 us  [col_send(): return lax.ppermute(blocks, 'col', perm)]
    pallas_call x3, Pallas kernels: 9.15 us -> 6.78 us  [pack(): pl.pallas_call(functools.partial(pack_kernel, unit, len(sources), parts),...]
    pallas_call x2, Pallas kernels: 9.05 us -> 7.46 us  [products(): pl.pallas_call(functools.partial(products_kernel, layout, update), out_sh...]
    unnamed x14 -> x18, local copies, waits for them, and re-layouts: 3.34 us -> 2.4 us
  transfers between devices with their start and end apart: 32 -> 31, of which waited for: 10 -> 13; matrix products, arithmetic and copies ran while one was open for 3% -> 3% of each run, Pallas kernels for 17% -> 14%
where the time goes in v2:
time: 129 us; the launch traced here: 128 us
  starting transfers between devices  56 us (43%)
  waiting for transfers between devices  40.1 us (31%)
  Pallas kernels  25.6 us (20%)
  local copies, waits for them, and re-layouts  3.4 us (3%)
  between operations  2.2 us (2%)
    ppermute x23, starting transfers between devices, row_send(): return lax.ppermute(blocks, 'row', perm)  40.2 us
    ppermute x23, waiting for transfers between devices, row_send(): return lax.ppermute(blocks, 'row', perm)  22.1 us
    ppermute x8, waiting for transfers between devices, col_send(): return lax.ppermute(blocks, 'col', perm)  18 us
    ppermute x8, starting transfers between devices, col_send(): return lax.ppermute(blocks, 'col', perm)  15.8 us
    pallas_call x2, Pallas kernels, products(): pl.pallas_call(functools.partial(products_kernel, layout, update), out_sh...  7.46 us
    pallas_call x3, Pallas kernels, pack(): pl.pallas_call(functools.partial(pack_kernel, unit, len(sources), parts),...  6.78 us
    pallas_call x1, Pallas kernels, shards(): pl.pallas_call(right_kernel, out_shape=(jax.ShapeDtypeStruct((16, 128), j...  6.77 us
    pallas_call x1, Pallas kernels, shards(): pl.pallas_call(left_kernel, out_shape=(jax.ShapeDtypeStruct((8, 128), jnp...  4.62 us
  transfers between devices with their start and end apart: 31, of which 13 were waited for; matrix products, arithmetic and copies ran while one was open for 3% of the time, Pallas kernels for 14%

profile of v2, /device:TPU:1, one launch (start us, length us, event | category | flops | bytes accessed | tf_op | source)
XLA Modules:
  0.0 128.2 jit_solution(13090736742807412644)
XLA Ops:
  0.6 2.1 %collective-permute-start.15 = (bf16[8,128,128]{2,1,0:T(8,128)(2,1)}, bf16[8,128,128]{2,1,0:T(8,128)(2,1)S(1)}, u32[]{:S(2)}, u32[]{:S(2)}) collective-permute-start(bf16[8,128,128]{2,1,0:T(8,128)(2,1)} %bitcast.7), channel_id=1, source_target_pairs={{0,4},{1,5},{2,6},{3,7},{4,8},{5,9},{6,10},{7,11},{8,12},{9,13},{1... | collective-permute-start | bytes 786440 | tf_op jit(solution)/shard_map/ppermute | solution.py:408
  2.7 1.4 %collective-permute-start.16 = (bf16[8,128,128]{2,1,0:T(8,128)(2,1)}, bf16[8,128,128]{2,1,0:T(8,128)(2,1)S(1)}, u32[]{:S(2)}, u32[]{:S(2)}) collective-permute-start(bf16[8,128,128]{2,1,0:T(8,128)(2,1)} %bitcast.8), channel_id=1, source_target_pairs={{0,12},{1,13},{2,14},{3,15},{4,0},{5,1},{6,2},{7,3},{8,4},{9,5},{1... | collective-permute-start | bytes 786440 | tf_op jit(solution)/shard_map/ppermute | solution.py:408
  4.1 1.6 %collective-permute-start.17 = (bf16[8,128,128]{2,1,0:T(8,128)(2,1)}, bf16[8,128,128]{2,1,0:T(8,128)(2,1)S(1)}, u32[]{:S(2)}, u32[]{:S(2)}) collective-permute-start(bf16[8,128,128]{2,1,0:T(8,128)(2,1)} %bitcast.9), channel_id=1, source_target_pairs={{0,8},{1,9},{2,10},{3,11},{4,12},{5,13},{6,14},{7,15},{8,0},{9,1},... | collective-permute-start | bytes 786440 | tf_op jit(solution)/shard_map/ppermute | solution.py:408
  5.7 6.9 %collective-permute-start.18 = (bf16[8,128,128]{2,1,0:T(8,128)(2,1)}, bf16[8,128,128]{2,1,0:T(8,128)(2,1)S(1)}, u32[]{:S(2)}, u32[]{:S(2)}) collective-permute-start(bf16[8,128,128]{2,1,0:T(8,128)(2,1)} %bitcast.10), channel_id=1, source_target_pairs={{0,128},{16,144},{32,160},{48,176},{64,192},{80,208},{96,224},{112... | collective-permute-start | bytes 786440 | tf_op jit(solution)/shard_map/ppermute | solution.py:404
  12.7 1.6 %copy.10.x_cols = s32[16,16,8]{2,1,0:T(8,128)} copy(s32[16,16,8]{1,2,0:T(8,128)} %param.13) | data formatting | bytes 16384 | tf_op args[2]
  15.6 4.6 %shard_map.86 = (s32[8,128]{1,0:T(8,128)S(1)}, s32[8,128]{1,0:T(8,128)}) custom-call(s32[2]{0:T(128)} %pad_add_fusion.at, s32[16,16,8]{2,1,0:T(8,128)} %copy.9.x_rows, s32[16,16,8]{2,1,0:T(8,128)} %copy.10.x_cols, s32[16,16,16]{2,1,0:T(8,128)} %y_rows.3, s32[16,16,16]{2,1,0:T(8,128)} %y_cols.3, s32[16,16,24]{2,1,0:T(8,128)} %z_rows.3, s32[16,16,24]{2,1,0:T(8,128)} %z_cols.3), custom_call_target="tpu_custom_call" | custom-call | tf_op jit(solution)/shard_map/pallas_call | solution.py:427
  20.3 2.3 %shard_map.87 = (bf16[10,128,128]{2,1,0:T(8,128)(2,1)}, bf16[17,128,128]{2,1,0:T(8,128)(2,1)}, bf16[10,128,128]{2,1,0:T(8,128)(2,1)}, bf16[7,128,128]{2,1,0:T(8,128)(2,1)}, bf16[7,128,128]{2,1,0:T(8,128)(2,1)}) custom-call(s32[8,128]{1,0:T(8,128)S(1)} %get-tuple-element.108.given.left_send, bf16[8,128,128]{2,1,0:T(8,128)(2,1)S(1)} %bitcast.12, ...), custom_call_target="tpu_custom_call" | custom-call | tf_op jit(solution)/shard_map/pallas_call | solution.py:300
  23.4 2.5 %collective-permute-start.20 = (bf16[17,128,128]{2,1,0:T(8,128)(2,1)}, bf16[17,128,128]{2,1,0:T(8,128)(2,1)S(1)}, u32[]{:S(2)}, u32[]{:S(2)}) collective-permute-start(bf16[17,128,128]{2,1,0:T(8,128)(2,1)} %get-tuple-element.118), channel_id=1, source_target_pairs={{0,2},{1,3},{2,0},{3,1},{4,6},{5,7},{6,4},{7,5},{8,10},{9,11},{10,... | collective-permute-start | bytes 1671176 | tf_op jit(solution)/shard_map/ppermute | solution.py:408
  27.3 1.4 %collective-permute-start.22 = (bf16[16,128,128]{2,1,0:T(8,128)(2,1)S(1)}, bf16[16,128,128]{2,1,0:T(8,128)(2,1)S(1)}, u32[]{:S(2)}, u32[]{:S(2)}) collective-permute-start(bf16[16,128,128]{2,1,0:T(8,128)(2,1)S(1)} %pad_maximum_fusion.refs_7_), channel_id=1, source_target_pairs={{0,32},{16,48},{32,64},{48,80},{64,96},{80,112},{96,0},{112,16},{1... | collective-permute-start | bytes 1572872 | tf_op jit(solution)/shard_map/ppermute | solution.py:404
  28.6 1.5 %collective-permute-start.23 = (bf16[16,128,128]{2,1,0:T(8,128)(2,1)S(1)}, bf16[16,128,128]{2,1,0:T(8,128)(2,1)S(1)}, u32[]{:S(2)}, u32[]{:S(2)}) collective-permute-start(bf16[16,128,128]{2,1,0:T(8,128)(2,1)S(1)} %pad_maximum_fusion.refs_7_), channel_id=1, source_target_pairs={{0,96},{16,112},{32,0},{48,16},{64,32},{80,48},{96,64},{112,80},{1... | collective-permute-start | bytes 1572872 | tf_op jit(solution)/shard_map/ppermute | solution.py:404
  30.2 1.6 %collective-permute-start.24 = (bf16[16,128,128]{2,1,0:T(8,128)(2,1)S(1)}, bf16[16,128,128]{2,1,0:T(8,128)(2,1)S(1)}, u32[]{:S(2)}, u32[]{:S(2)}) collective-permute-start(bf16[16,128,128]{2,1,0:T(8,128)(2,1)S(1)} %pad_maximum_fusion.refs_7_), channel_id=1, source_target_pairs={{0,64},{16,80},{32,96},{48,112},{64,0},{80,16},{96,32},{112,48},{1... | collective-permute-start | bytes 1572872 | tf_op jit(solution)/shard_map/ppermute | solution.py:404
  31.7 8.1 %collective-permute-done.19.refs_4_ = bf16[10,128,128]{2,1,0:T(8,128)(2,1)S(1)} collective-permute-done((bf16[10,128,128]{2,1,0:T(8,128)(2,1)}, bf16[10,128,128]{2,1,0:T(8,128)(2,1)S(1)}, u32[]{:S(2)}, u32[]{:S(2)}) %collective-permute-start.19) | collective-permute-done | bytes 327712 | tf_op jit(solution)/shard_map/ppermute | solution.py:408
  39.9 6.8 %shard_map.88 = (s32[16,128]{1,0:T(8,128)S(1)}, s32[16,128]{1,0:T(8,128)}, s32[24,128]{1,0:T(8,128)}) custom-call(s32[2]{0:T(128)} %pad_add_fusion.at, s32[8,128]{1,0:T(8,128)S(1)} %get-tuple-element.108.given.left_send, s32[8,128]{1,0:T(8,128)} %get-tuple-element.122.positions, s32[16,16,8]{2,1,0:T(8,128)} %copy.9.x_rows, s32[16,16,8]{2,1,0:T(8,128)} %copy.10.x_cols, ...), custom_call_target="tpu_custom_call" | custom-call | tf_op jit(solution)/shard_map/pallas_call | solution.py:444
  46.6 2.0 %collective-permute-start.25 = (bf16[16,128,128]{2,1,0:T(8,128)(2,1)S(1)}, bf16[16,128,128]{2,1,0:T(8,128)(2,1)S(1)}, u32[]{:S(2)}, u32[]{:S(2)}) collective-permute-start(bf16[16,128,128]{2,1,0:T(8,128)(2,1)S(1)} %pad_maximum_fusion.refs_7_), channel_id=1, source_target_pairs={{0,16},{16,0},{32,48},{48,32},{64,80},{80,64},{96,112},{112,96},{1... | collective-permute-start | bytes 1572872 | tf_op jit(solution)/shard_map/ppermute | solution.py:404
  48.6 4.1 %collective-permute-done.24.refs_10_ = bf16[16,128,128]{2,1,0:T(8,128)(2,1)S(1)} collective-permute-done((bf16[16,128,128]{2,1,0:T(8,128)(2,1)S(1)}, bf16[16,128,128]{2,1,0:T(8,128)(2,1)S(1)}, u32[]{:S(2)}, u32[]{:S(2)}) %collective-permute-start.24) | collective-permute-done | bytes 524320 | tf_op jit(solution)/shard_map/ppermute | solution.py:404
  52.7 9.5 %collective-permute-start.26 = (bf16[16,128,128]{2,1,0:T(8,128)(2,1)S(1)}, bf16[16,128,128]{2,1,0:T(8,128)(2,1)S(1)}, u32[]{:S(2)}, u32[]{:S(2)}) collective-permute-start(bf16[16,128,128]{2,1,0:T(8,128)(2,1)S(1)} %collective-permute-done.22.refs_8_), channel_id=1, source_target_pairs={{0,16},{16,0},{32,48},{48,32},{64,80},{80,64},{96,112},{112,96},{1... | collective-permute-start | bytes 1572872 | tf_op jit(solution)/shard_map/ppermute | solution.py:404
  65.3 2.5 %shard_map.89.refs_0_.refs_9_ = bf16[16,128,128]{2,1,0:T(8,128)(2,1)} custom-call(s32[16,128]{1,0:T(8,128)S(1)} %copy-done.1, bf16[8,128,128]{2,1,0:T(8,128)(2,1)} %bitcast.11, bf16[8,128,128]{2,1,0:T(8,128)(2,1)} %copy-done.4, bf16[8,128,128]{2,1,0:T(8,128)(2,1)} %copy-done.5, bf16[8,128,128]{2,1,0:T(8,128)(2,1)} %copy-done.6, ...), custom_call_target="tpu_custom_call" | custom-call | tf_op jit(solution)/shard_map/pallas_call | solution.py:388
  67.8 4.9 %collective-permute-start.29 = (bf16[16,128,128]{2,1,0:T(8,128)(2,1)}, bf16[16,128,128]{2,1,0:T(8,128)(2,1)}, u32[]{:S(2)}, u32[]{:S(2)}) collective-permute-start(bf16[16,128,128]{2,1,0:T(8,128)(2,1)} %shard_map.89.refs_0_.refs_9_), channel_id=1, source_target_pairs={{0,128},{16,144},{32,160},{48,176},{64,192},{80,208},{96,224},{112... | collective-permute-start | bytes 1572872 | tf_op jit(solution)/shard_map/ppermute | solution.py:404
  73.4 2.2 %shard_map.90 = (bf16[10,128,128]{2,1,0:T(8,128)(2,1)}, bf16[10,128,128]{2,1,0:T(8,128)(2,1)}, bf16[10,128,128]{2,1,0:T(8,128)(2,1)}) custom-call(s32[16,128]{1,0:T(8,128)S(1)} %get-tuple-element.137.given, bf16[16,128,128]{2,1,0:T(8,128)(2,1)} %shard_map.89.refs_0_.refs_9_), custom_call_target="tpu_custom_call" | custom-call | tf_op jit(solution)/shard_map/pallas_call | solution.py:300
  75.6 1.4 %collective-permute-start.31 = (bf16[10,128,128]{2,1,0:T(8,128)(2,1)}, bf16[10,128,128]{2,1,0:T(8,128)(2,1)S(1)}, u32[]{:S(2)}, u32[]{:S(2)}) collective-permute-start(bf16[10,128,128]{2,1,0:T(8,128)(2,1)} %get-tuple-element.138), channel_id=1, source_target_pairs={{0,32},{16,48},{32,64},{48,80},{64,96},{80,112},{96,0},{112,16},{1... | collective-permute-start | bytes 983048 | tf_op jit(solution)/shard_map/ppermute | solution.py:404
  77.0 1.5 %collective-permute-start.32 = (bf16[10,128,128]{2,1,0:T(8,128)(2,1)}, bf16[10,128,128]{2,1,0:T(8,128)(2,1)S(1)}, u32[]{:S(2)}, u32[]{:S(2)}) collective-permute-start(bf16[10,128,128]{2,1,0:T(8,128)(2,1)} %get-tuple-element.139), channel_id=1, source_target_pairs={{0,96},{16,112},{32,0},{48,16},{64,32},{80,48},{96,64},{112,80},{1... | collective-permute-start | bytes 983048 | tf_op jit(solution)/shard_map/ppermute | solution.py:404
  78.5 1.6 %collective-permute-start.33 = (bf16[10,128,128]{2,1,0:T(8,128)(2,1)}, bf16[10,128,128]{2,1,0:T(8,128)(2,1)S(1)}, u32[]{:S(2)}, u32[]{:S(2)}) collective-permute-start(bf16[10,128,128]{2,1,0:T(8,128)(2,1)} %get-tuple-element.140), channel_id=1, source_target_pairs={{0,64},{16,80},{32,96},{48,112},{64,0},{80,16},{96,32},{112,48},{1... | collective-permute-start | bytes 983048 | tf_op jit(solution)/shard_map/ppermute | solution.py:404
  81.1 5.5 %collective-permute-done.31.refs_11_ = bf16[10,128,128]{2,1,0:T(8,128)(2,1)S(1)} collective-permute-done((bf16[10,128,128]{2,1,0:T(8,128)(2,1)}, bf16[10,128,128]{2,1,0:T(8,128)(2,1)S(1)}, u32[]{:S(2)}, u32[]{:S(2)}) %collective-permute-start.31) | collective-permute-done | bytes 327712 | tf_op jit(solution)/shard_map/ppermute | solution.py:404
  86.6 8.1 %collective-permute-done.33.refs_15_ = bf16[10,128,128]{2,1,0:T(8,128)(2,1)S(1)} collective-permute-done((bf16[10,128,128]{2,1,0:T(8,128)(2,1)}, bf16[10,128,128]{2,1,0:T(8,128)(2,1)S(1)}, u32[]{:S(2)}, u32[]{:S(2)}) %collective-permute-start.33) | collective-permute-done | bytes 327712 | tf_op jit(solution)/shard_map/ppermute | solution.py:404
  96.5 2.2 %shard_map.91 = (bf16[10,128,128]{2,1,0:T(8,128)(2,1)}, bf16[10,128,128]{2,1,0:T(8,128)(2,1)}, bf16[10,128,128]{2,1,0:T(8,128)(2,1)}) custom-call(s32[16,128]{1,0:T(8,128)S(1)} %get-tuple-element.137.given, bf16[16,128,128]{2,1,0:T(8,128)(2,1)} %collective-permute-done.29.refs_0_.refs_10_), custom_call_target="tpu_custom_call" | custom-call | tf_op jit(solution)/shard_map/pallas_call | solution.py:300
  99.8 1.8 %collective-permute-start.39 = (bf16[10,128,128]{2,1,0:T(8,128)(2,1)}, bf16[10,128,128]{2,1,0:T(8,128)(2,1)S(1)}, u32[]{:S(2)}, u32[]{:S(2)}) collective-permute-start(bf16[10,128,128]{2,1,0:T(8,128)(2,1)} %get-tuple-element.151), channel_id=1, source_target_pairs={{0,96},{16,112},{32,0},{48,16},{64,32},{80,48},{96,64},{112,80},{1... | collective-permute-start | bytes 983048 | tf_op jit(solution)/shard_map/ppermute | solution.py:404
  101.7 4.9 %collective-permute-start.41 = (bf16[7,128,128]{2,1,0:T(8,128)(2,1)}, bf16[7,128,128]{2,1,0:T(8,128)(2,1)S(1)}, u32[]{:S(2)}, u32[]{:S(2)}) collective-permute-start(bf16[7,128,128]{2,1,0:T(8,128)(2,1)} %get-tuple-element.153), channel_id=1, source_target_pairs={{0,1},{1,0},{2,3},{3,2},{4,5},{5,4},{6,7},{7,6},{8,9},{9,8},{10,11... | collective-permute-start | bytes 688136 | tf_op jit(solution)/shard_map/ppermute | solution.py:408
  106.6 2.4 %collective-permute-start.42 = (bf16[7,128,128]{2,1,0:T(8,128)(2,1)}, bf16[7,128,128]{2,1,0:T(8,128)(2,1)S(1)}, u32[]{:S(2)}, u32[]{:S(2)}) collective-permute-start(bf16[7,128,128]{2,1,0:T(8,128)(2,1)} %get-tuple-element.154), channel_id=1, source_target_pairs={{0,3},{1,2},{2,1},{3,0},{4,7},{5,6},{6,5},{7,4},{8,11},{9,10},{10,... | collective-permute-start | bytes 688136 | tf_op jit(solution)/shard_map/ppermute | solution.py:408
  109.0 2.5 %collective-permute-done.41.refs_7_ = bf16[7,128,128]{2,1,0:T(8,128)(2,1)S(1)} collective-permute-done((bf16[7,128,128]{2,1,0:T(8,128)(2,1)}, bf16[7,128,128]{2,1,0:T(8,128)(2,1)S(1)}, u32[]{:S(2)}, u32[]{:S(2)}) %collective-permute-start.41) | collective-permute-done | bytes 229408 | tf_op jit(solution)/shard_map/ppermute | solution.py:408
  111.5 7.3 %collective-permute-done.42.refs_8_ = bf16[7,128,128]{2,1,0:T(8,128)(2,1)S(1)} collective-permute-done((bf16[7,128,128]{2,1,0:T(8,128)(2,1)}, bf16[7,128,128]{2,1,0:T(8,128)(2,1)S(1)}, u32[]{:S(2)}, u32[]{:S(2)}) %collective-permute-start.42) | collective-permute-done | bytes 229408 | tf_op jit(solution)/shard_map/ppermute | solution.py:408
  118.8 1.9 %collective-permute-start.43 = (bf16[10,128,128]{2,1,0:T(8,128)(2,1)S(1)}, bf16[10,128,128]{2,1,0:T(8,128)(2,1)S(1)}, u32[]{:S(2)}, u32[]{:S(2)}) collective-permute-start(bf16[10,128,128]{2,1,0:T(8,128)(2,1)S(1)} %collective-permute-done.38.refs_12_), channel_id=1, source_target_pairs={{0,16},{16,0},{32,48},{48,32},{64,80},{80,64},{96,112},{112,96},{1... | collective-permute-start | bytes 983048 | tf_op jit(solution)/shard_map/ppermute | solution.py:404
  123.0 5.0 %shard_map.92 = bf16[24,128,128]{2,1,0:T(8,128)(2,1)} custom-call(s32[24,128]{1,0:T(8,128)S(1)} %copy-done, bf16[8,128,128]{2,1,0:T(8,128)(2,1)S(1)} %bitcast.15, bf16[8,128,128]{2,1,0:T(8,128)(2,1)} %copy-done.4, bf16[8,128,128]{2,1,0:T(8,128)(2,1)} %copy-done.5, bf16[8,128,128]{2,1,0:T(8,128)(2,1)} %copy-done.6, ...), custom_call_target="tpu_custom_call" | custom-call | tf_op jit(solution)/shard_map/pallas_call | solution.py:388
  (63 shorter events, 12.1 us)
Async XLA Ops:
  0.6 19.6 %collective-permute-start.15 = (bf16[8,128,128]{2,1,0:T(8,128)(2,1)}, bf16[8,128,128]{2,1,0:T(8,128)(2,1)S(1)}, u32[]{:S(2)}, u32[]{:S(2)}) collective-permute-start(bf16[8,128,128]{2,1,0:T(8,128)(2,1)} %bitcast.7), channel_id=1, source_target_pairs={{0,4},{1,5},{2,6},{3,7},{4,8},{5,9},{6,10},{7,11},{8,12},{9,13},{1... | collective-permute-start | bytes 786440 | tf_op jit(solution)/shard_map/ppermute | solution.py:408
  2.7 17.5 %collective-permute-start.16 = (bf16[8,128,128]{2,1,0:T(8,128)(2,1)}, bf16[8,128,128]{2,1,0:T(8,128)(2,1)S(1)}, u32[]{:S(2)}, u32[]{:S(2)}) collective-permute-start(bf16[8,128,128]{2,1,0:T(8,128)(2,1)} %bitcast.8), channel_id=1, source_target_pairs={{0,12},{1,13},{2,14},{3,15},{4,0},{5,1},{6,2},{7,3},{8,4},{9,5},{1... | collective-permute-start | bytes 786440 | tf_op jit(solution)/shard_map/ppermute | solution.py:408
  4.1 16.1 %collective-permute-start.17 = (bf16[8,128,128]{2,1,0:T(8,128)(2,1)}, bf16[8,128,128]{2,1,0:T(8,128)(2,1)S(1)}, u32[]{:S(2)}, u32[]{:S(2)}) collective-permute-start(bf16[8,128,128]{2,1,0:T(8,128)(2,1)} %bitcast.9), channel_id=1, source_target_pairs={{0,8},{1,9},{2,10},{3,11},{4,12},{5,13},{6,14},{7,15},{8,0},{9,1},... | collective-permute-start | bytes 786440 | tf_op jit(solution)/shard_map/ppermute | solution.py:408
  5.7 16.9 %collective-permute-start.18 = (bf16[8,128,128]{2,1,0:T(8,128)(2,1)}, bf16[8,128,128]{2,1,0:T(8,128)(2,1)S(1)}, u32[]{:S(2)}, u32[]{:S(2)}) collective-permute-start(bf16[8,128,128]{2,1,0:T(8,128)(2,1)} %bitcast.10), channel_id=1, source_target_pairs={{0,128},{16,144},{32,160},{48,176},{64,192},{80,208},{96,224},{112... | collective-permute-start | bytes 786440 | tf_op jit(solution)/shard_map/ppermute | solution.py:404
  22.6 17.2 %collective-permute-start.19 = (bf16[10,128,128]{2,1,0:T(8,128)(2,1)}, bf16[10,128,128]{2,1,0:T(8,128)(2,1)S(1)}, u32[]{:S(2)}, u32[]{:S(2)}) collective-permute-start(bf16[10,128,128]{2,1,0:T(8,128)(2,1)} %get-tuple-element.117), channel_id=1, source_target_pairs={{0,1},{1,0},{2,3},{3,2},{4,5},{5,4},{6,7},{7,6},{8,9},{9,8},{10,11... | collective-permute-start | bytes 983048 | tf_op jit(solution)/shard_map/ppermute | solution.py:408
  23.4 29.3 %collective-permute-start.20 = (bf16[17,128,128]{2,1,0:T(8,128)(2,1)}, bf16[17,128,128]{2,1,0:T(8,128)(2,1)S(1)}, u32[]{:S(2)}, u32[]{:S(2)}) collective-permute-start(bf16[17,128,128]{2,1,0:T(8,128)(2,1)} %get-tuple-element.118), channel_id=1, source_target_pairs={{0,2},{1,3},{2,0},{3,1},{4,6},{5,7},{6,4},{7,5},{8,10},{9,11},{10,... | collective-permute-start | bytes 1671176 | tf_op jit(solution)/shard_map/ppermute | solution.py:408
  27.3 19.4 %collective-permute-start.22 = (bf16[16,128,128]{2,1,0:T(8,128)(2,1)S(1)}, bf16[16,128,128]{2,1,0:T(8,128)(2,1)S(1)}, u32[]{:S(2)}, u32[]{:S(2)}) collective-permute-start(bf16[16,128,128]{2,1,0:T(8,128)(2,1)S(1)} %pad_maximum_fusion.refs_7_), channel_id=1, source_target_pairs={{0,32},{16,48},{32,64},{48,80},{64,96},{80,112},{96,0},{112,16},{1... | collective-permute-start | bytes 1572872 | tf_op jit(solution)/shard_map/ppermute | solution.py:404
  28.6 20.0 %collective-permute-start.23 = (bf16[16,128,128]{2,1,0:T(8,128)(2,1)S(1)}, bf16[16,128,128]{2,1,0:T(8,128)(2,1)S(1)}, u32[]{:S(2)}, u32[]{:S(2)}) collective-permute-start(bf16[16,128,128]{2,1,0:T(8,128)(2,1)S(1)} %pad_maximum_fusion.refs_7_), channel_id=1, source_target_pairs={{0,96},{16,112},{32,0},{48,16},{64,32},{80,48},{96,64},{112,80},{1... | collective-permute-start | bytes 1572872 | tf_op jit(solution)/shard_map/ppermute | solution.py:404
  30.2 22.6 %collective-permute-start.24 = (bf16[16,128,128]{2,1,0:T(8,128)(2,1)S(1)}, bf16[16,128,128]{2,1,0:T(8,128)(2,1)S(1)}, u32[]{:S(2)}, u32[]{:S(2)}) collective-permute-start(bf16[16,128,128]{2,1,0:T(8,128)(2,1)S(1)} %pad_maximum_fusion.refs_7_), channel_id=1, source_target_pairs={{0,64},{16,80},{32,96},{48,112},{64,0},{80,16},{96,32},{112,48},{1... | collective-permute-start | bytes 1572872 | tf_op jit(solution)/shard_map/ppermute | solution.py:404
  39.8 12.9 %collective-permute-start.21 = (bf16[10,128,128]{2,1,0:T(8,128)(2,1)}, bf16[10,128,128]{2,1,0:T(8,128)(2,1)S(1)}, u32[]{:S(2)}, u32[]{:S(2)}) collective-permute-start(bf16[10,128,128]{2,1,0:T(8,128)(2,1)} %get-tuple-element.120), channel_id=1, source_target_pairs={{0,3},{1,2},{2,1},{3,0},{4,7},{5,6},{6,5},{7,4},{8,11},{9,10},{10,... | collective-permute-start | bytes 983048 | tf_op jit(solution)/shard_map/ppermute | solution.py:408
  46.6 16.2 %collective-permute-start.25 = (bf16[16,128,128]{2,1,0:T(8,128)(2,1)S(1)}, bf16[16,128,128]{2,1,0:T(8,128)(2,1)S(1)}, u32[]{:S(2)}, u32[]{:S(2)}) collective-permute-start(bf16[16,128,128]{2,1,0:T(8,128)(2,1)S(1)} %pad_maximum_fusion.refs_7_), channel_id=1, source_target_pairs={{0,16},{16,0},{32,48},{48,32},{64,80},{80,64},{96,112},{112,96},{1... | collective-permute-start | bytes 1572872 | tf_op jit(solution)/shard_map/ppermute | solution.py:404
  52.7 11.1 %collective-permute-start.26 = (bf16[16,128,128]{2,1,0:T(8,128)(2,1)S(1)}, bf16[16,128,128]{2,1,0:T(8,128)(2,1)S(1)}, u32[]{:S(2)}, u32[]{:S(2)}) collective-permute-start(bf16[16,128,128]{2,1,0:T(8,128)(2,1)S(1)} %collective-permute-done.22.refs_8_), channel_id=1, source_target_pairs={{0,16},{16,0},{32,48},{48,32},{64,80},{80,64},{96,112},{112,96},{1... | collective-permute-start | bytes 1572872 | tf_op jit(solution)/shard_map/ppermute | solution.py:404
  62.3 2.3 %collective-permute-start.27 = (bf16[16,128,128]{2,1,0:T(8,128)(2,1)S(1)}, bf16[16,128,128]{2,1,0:T(8,128)(2,1)S(1)}, u32[]{:S(2)}, u32[]{:S(2)}) collective-permute-start(bf16[16,128,128]{2,1,0:T(8,128)(2,1)S(1)} %collective-permute-done.23.refs_9_), channel_id=1, source_target_pairs={{0,16},{16,0},{32,48},{48,32},{64,80},{80,64},{96,112},{112,96},{1... | collective-permute-start | bytes 1572872 | tf_op jit(solution)/shard_map/ppermute | solution.py:404
  62.3 3.0 %collective-permute-start.28 = (bf16[16,128,128]{2,1,0:T(8,128)(2,1)S(1)}, bf16[16,128,128]{2,1,0:T(8,128)(2,1)S(1)}, u32[]{:S(2)}, u32[]{:S(2)}) collective-permute-start(bf16[16,128,128]{2,1,0:T(8,128)(2,1)S(1)} %collective-permute-done.24.refs_10_), channel_id=1, source_target_pairs={{0,16},{16,0},{32,48},{48,32},{64,80},{80,64},{96,112},{112,96},{1... | collective-permute-start | bytes 1572872 | tf_op jit(solution)/shard_map/ppermute | solution.py:404
  67.8 26.9 %collective-permute-start.29 = (bf16[16,128,128]{2,1,0:T(8,128)(2,1)}, bf16[16,128,128]{2,1,0:T(8,128)(2,1)}, u32[]{:S(2)}, u32[]{:S(2)}) collective-permute-start(bf16[16,128,128]{2,1,0:T(8,128)(2,1)} %shard_map.89.refs_0_.refs_9_), channel_id=1, source_target_pairs={{0,128},{16,144},{32,160},{48,176},{64,192},{80,208},{96,224},{112... | collective-permute-start | bytes 1572872 | tf_op jit(solution)/shard_map/ppermute | solution.py:404
  72.7 22.0 %collective-permute-start.30 = (bf16[16,128,128]{2,1,0:T(8,128)(2,1)}, bf16[16,128,128]{2,1,0:T(8,128)(2,1)S(1)}, u32[]{:S(2)}, u32[]{:S(2)}) collective-permute-start(bf16[16,128,128]{2,1,0:T(8,128)(2,1)} %shard_map.89.refs_0_.refs_9_), channel_id=1, source_target_pairs={{0,16},{16,0},{32,48},{48,32},{64,80},{80,64},{96,112},{112,96},{1... | collective-permute-start | bytes 1572872 | tf_op jit(solution)/shard_map/ppermute | solution.py:404
  75.6 10.9 %collective-permute-start.31 = (bf16[10,128,128]{2,1,0:T(8,128)(2,1)}, bf16[10,128,128]{2,1,0:T(8,128)(2,1)S(1)}, u32[]{:S(2)}, u32[]{:S(2)}) collective-permute-start(bf16[10,128,128]{2,1,0:T(8,128)(2,1)} %get-tuple-element.138), channel_id=1, source_target_pairs={{0,32},{16,48},{32,64},{48,80},{64,96},{80,112},{96,0},{112,16},{1... | collective-permute-start | bytes 983048 | tf_op jit(solution)/shard_map/ppermute | solution.py:404
  77.0 9.6 %collective-permute-start.32 = (bf16[10,128,128]{2,1,0:T(8,128)(2,1)}, bf16[10,128,128]{2,1,0:T(8,128)(2,1)S(1)}, u32[]{:S(2)}, u32[]{:S(2)}) collective-permute-start(bf16[10,128,128]{2,1,0:T(8,128)(2,1)} %get-tuple-element.139), channel_id=1, source_target_pairs={{0,96},{16,112},{32,0},{48,16},{64,32},{80,48},{96,64},{112,80},{1... | collective-permute-start | bytes 983048 | tf_op jit(solution)/shard_map/ppermute | solution.py:404
  78.5 16.2 %collective-permute-start.33 = (bf16[10,128,128]{2,1,0:T(8,128)(2,1)}, bf16[10,128,128]{2,1,0:T(8,128)(2,1)S(1)}, u32[]{:S(2)}, u32[]{:S(2)}) collective-permute-start(bf16[10,128,128]{2,1,0:T(8,128)(2,1)} %get-tuple-element.140), channel_id=1, source_target_pairs={{0,64},{16,80},{32,96},{48,112},{64,0},{80,16},{96,32},{112,48},{1... | collective-permute-start | bytes 983048 | tf_op jit(solution)/shard_map/ppermute | solution.py:404
  94.9 28.1 %copy-start.3 = (bf16[1,1,8,128,128]{4,3,2,1,0:T(8,128)(2,1)S(1)}, bf16[1,1,8,128,128]{4,3,2,1,0:T(8,128)(2,1)}, u32[]{:S(2)}) copy-start(bf16[1,1,8,128,128]{4,3,2,1,0:T(8,128)(2,1)} %param.11) | copy-start | bytes 786436
  94.9 4.0 %collective-permute-start.34 = (bf16[16,128,128]{2,1,0:T(8,128)(2,1)}, bf16[16,128,128]{2,1,0:T(8,128)(2,1)S(1)}, u32[]{:S(2)}, u32[]{:S(2)}) collective-permute-start(bf16[16,128,128]{2,1,0:T(8,128)(2,1)} %collective-permute-done.29.refs_0_.refs_10_), channel_id=1, source_target_pairs={{0,16},{16,0},{32,48},{48,32},{64,80},{80,64},{96,112},{112,96},{1... | collective-permute-start | bytes 1572872 | tf_op jit(solution)/shard_map/ppermute | solution.py:404
  95.8 2.9 %collective-permute-start.35 = (bf16[10,128,128]{2,1,0:T(8,128)(2,1)S(1)}, bf16[10,128,128]{2,1,0:T(8,128)(2,1)}, u32[]{:S(2)}, u32[]{:S(2)}) collective-permute-start(bf16[10,128,128]{2,1,0:T(8,128)(2,1)S(1)} %collective-permute-done.31.refs_11_), channel_id=1, source_target_pairs={{0,16},{16,0},{32,48},{48,32},{64,80},{80,64},{96,112},{112,96},{1... | collective-permute-start | bytes 983048 | tf_op jit(solution)/shard_map/ppermute | solution.py:404
  95.9 2.8 %collective-permute-start.36 = (bf16[10,128,128]{2,1,0:T(8,128)(2,1)S(1)}, bf16[10,128,128]{2,1,0:T(8,128)(2,1)}, u32[]{:S(2)}, u32[]{:S(2)}) collective-permute-start(bf16[10,128,128]{2,1,0:T(8,128)(2,1)S(1)} %collective-permute-done.32.refs_13_), channel_id=1, source_target_pairs={{0,16},{16,0},{32,48},{48,32},{64,80},{80,64},{96,112},{112,96},{1... | collective-permute-start | bytes 983048 | tf_op jit(solution)/shard_map/ppermute | solution.py:404
  96.4 2.6 %collective-permute-start.37 = (bf16[10,128,128]{2,1,0:T(8,128)(2,1)S(1)}, bf16[10,128,128]{2,1,0:T(8,128)(2,1)}, u32[]{:S(2)}, u32[]{:S(2)}) collective-permute-start(bf16[10,128,128]{2,1,0:T(8,128)(2,1)S(1)} %collective-permute-done.33.refs_15_), channel_id=1, source_target_pairs={{0,16},{16,0},{32,48},{48,32},{64,80},{80,64},{96,112},{112,96},{1... | collective-permute-start | bytes 983048 | tf_op jit(solution)/shard_map/ppermute | solution.py:404
  98.9 19.9 %collective-permute-start.38 = (bf16[10,128,128]{2,1,0:T(8,128)(2,1)}, bf16[10,128,128]{2,1,0:T(8,128)(2,1)S(1)}, u32[]{:S(2)}, u32[]{:S(2)}) collective-permute-start(bf16[10,128,128]{2,1,0:T(8,128)(2,1)} %get-tuple-element.150), channel_id=1, source_target_pairs={{0,32},{16,48},{32,64},{48,80},{64,96},{80,112},{96,0},{112,16},{1... | collective-permute-start | bytes 983048 | tf_op jit(solution)/shard_map/ppermute | solution.py:404
  99.8 19.1 %collective-permute-start.39 = (bf16[10,128,128]{2,1,0:T(8,128)(2,1)}, bf16[10,128,128]{2,1,0:T(8,128)(2,1)S(1)}, u32[]{:S(2)}, u32[]{:S(2)}) collective-permute-start(bf16[10,128,128]{2,1,0:T(8,128)(2,1)} %get-tuple-element.151), channel_id=1, source_target_pairs={{0,96},{16,112},{32,0},{48,16},{64,32},{80,48},{96,64},{112,80},{1... | collective-permute-start | bytes 983048 | tf_op jit(solution)/shard_map/ppermute | solution.py:404
  101.6 17.2 %collective-permute-start.40 = (bf16[10,128,128]{2,1,0:T(8,128)(2,1)}, bf16[10,128,128]{2,1,0:T(8,128)(2,1)S(1)}, u32[]{:S(2)}, u32[]{:S(2)}) collective-permute-start(bf16[10,128,128]{2,1,0:T(8,128)(2,1)} %get-tuple-element.152), channel_id=1, source_target_pairs={{0,64},{16,80},{32,96},{48,112},{64,0},{80,16},{96,32},{112,48},{1... | collective-permute-start | bytes 983048 | tf_op jit(solution)/shard_map/ppermute | solution.py:404
  101.7 9.8 %collective-permute-start.41 = (bf16[7,128,128]{2,1,0:T(8,128)(2,1)}, bf16[7,128,128]{2,1,0:T(8,128)(2,1)S(1)}, u32[]{:S(2)}, u32[]{:S(2)}) collective-permute-start(bf16[7,128,128]{2,1,0:T(8,128)(2,1)} %get-tuple-element.153), channel_id=1, source_target_pairs={{0,1},{1,0},{2,3},{3,2},{4,5},{5,4},{6,7},{7,6},{8,9},{9,8},{10,11... | collective-permute-start | bytes 688136 | tf_op jit(solution)/shard_map/ppermute | solution.py:408
  106.6 12.2 %collective-permute-start.42 = (bf16[7,128,128]{2,1,0:T(8,128)(2,1)}, bf16[7,128,128]{2,1,0:T(8,128)(2,1)S(1)}, u32[]{:S(2)}, u32[]{:S(2)}) collective-permute-start(bf16[7,128,128]{2,1,0:T(8,128)(2,1)} %get-tuple-element.154), channel_id=1, source_target_pairs={{0,3},{1,2},{2,1},{3,0},{4,7},{5,6},{6,5},{7,4},{8,11},{9,10},{10,... | collective-permute-start | bytes 688136 | tf_op jit(solution)/shard_map/ppermute | solution.py:408
  118.8 3.2 %collective-permute-start.43 = (bf16[10,128,128]{2,1,0:T(8,128)(2,1)S(1)}, bf16[10,128,128]{2,1,0:T(8,128)(2,1)S(1)}, u32[]{:S(2)}, u32[]{:S(2)}) collective-permute-start(bf16[10,128,128]{2,1,0:T(8,128)(2,1)S(1)} %collective-permute-done.38.refs_12_), channel_id=1, source_target_pairs={{0,16},{16,0},{32,48},{48,32},{64,80},{80,64},{96,112},{112,96},{1... | collective-permute-start | bytes 983048 | tf_op jit(solution)/shard_map/ppermute | solution.py:404
  120.8 1.7 %collective-permute-start.44 = (bf16[10,128,128]{2,1,0:T(8,128)(2,1)S(1)}, bf16[10,128,128]{2,1,0:T(8,128)(2,1)S(1)}, u32[]{:S(2)}, u32[]{:S(2)}) collective-permute-start(bf16[10,128,128]{2,1,0:T(8,128)(2,1)S(1)} %collective-permute-done.39.refs_14_), channel_id=1, source_target_pairs={{0,16},{16,0},{32,48},{48,32},{64,80},{80,64},{96,112},{112,96},{1... | collective-permute-start | bytes 983048 | tf_op jit(solution)/shard_map/ppermute | solution.py:404
  120.9 2.1 %collective-permute-start.45 = (bf16[10,128,128]{2,1,0:T(8,128)(2,1)S(1)}, bf16[10,128,128]{2,1,0:T(8,128)(2,1)S(1)}, u32[]{:S(2)}, u32[]{:S(2)}) collective-permute-start(bf16[10,128,128]{2,1,0:T(8,128)(2,1)S(1)} %collective-permute-done.40.refs_16_), channel_id=1, source_target_pairs={{0,16},{16,0},{32,48},{48,32},{64,80},{80,64},{96,112},{112,96},{1... | collective-permute-start | bytes 983048 | tf_op jit(solution)/shard_map/ppermute | solution.py:404
  (7 other events, 69.9 us)

commit v3 on v2

--- a/solution.py
+++ b/solution.py
@@ -435,7 +435,6 @@
     parts = [(d, 0, end) for d, end in enumerate(ends)]
     parts += [(d, LEFT_FIRST, LEFT_ALL) for d in (0, 2)]
     first = pack(left_send, quad, *parts)
-    first, far = lax.optimization_barrier((first, far))
     first, second = first[:3], first[3:]
     one, two = [col_send(blocks, swap) for blocks, swap in zip(first[:2], B_SWAP[:2])]
     first = [one, two, col_send(after(first[2], one), B_SWAP[2])]

time: 129 us -> 127 us (0.984)
  starting transfers between devices: 56 us -> 52.7 us
  waiting for transfers between devices: 40.1 us -> 42.3 us
    ppermute x23, starting transfers between devices: 40.2 us -> 34.8 us  [row_send(): return lax.ppermute(blocks, 'row', perm)]
    ppermute x8, waiting for transfers between devices: 18 us -> 22.2 us  [col_send(): return lax.ppermute(blocks, 'col', perm)]
    ppermute x8, starting transfers between devices: 15.8 us -> 17.9 us  [col_send(): return lax.ppermute(blocks, 'col', perm)]
    ppermute x23, waiting for transfers between devices: 22.1 us -> 20.1 us  [row_send(): return lax.ppermute(blocks, 'row', perm)]
  transfers between devices with their start and end apart: 31 -> 31, of which waited for: 13 -> 14; matrix products, arithmetic and copies ran while one was open for 3% -> 3% of each run, Pallas kernels for 14% -> 14%
where the time goes in v3:
time: 127 us
  starting transfers between devices  52.7 us (41%)
  waiting for transfers between devices  42.3 us (33%)
  Pallas kernels  25.3 us (20%)
  local copies, waits for them, and re-layouts  3.4 us (3%)
  between operations  2.19 us (2%)
    ppermute x23, starting transfers between devices, row_send(): return lax.ppermute(blocks, 'row', perm)  34.8 us
    ppermute x8, waiting for transfers between devices, col_send(): return lax.ppermute(blocks, 'col', perm)  22.2 us
    ppermute x23, waiting for transfers between devices, row_send(): return lax.ppermute(blocks, 'row', perm)  20.1 us
    ppermute x8, starting transfers between devices, col_send(): return lax.ppermute(blocks, 'col', perm)  17.9 us
    pallas_call x2, Pallas kernels, products(): pl.pallas_call(functools.partial(products_kernel, layout, update), out_sh...  7.16 us
    pallas_call x3, Pallas kernels, pack(): pl.pallas_call(functools.partial(pack_kernel, unit, len(sources), parts),...  6.78 us
    pallas_call x1, Pallas kernels, shards(): pl.pallas_call(right_kernel, out_shape=(jax.ShapeDtypeStruct((16, 128), j...  6.77 us
    pallas_call x1, Pallas kernels, shards(): pl.pallas_call(left_kernel, out_shape=(jax.ShapeDtypeStruct((8, 128), jnp...  4.62 us
  transfers between devices with their start and end apart: 31, of which 14 were waited for; matrix products, arithmetic and copies ran while one was open for 3% of the time, Pallas kernels for 14%

profile of v3, /device:TPU:1, one launch (start us, length us, event | category | flops | bytes accessed | tf_op | source)
XLA Modules:
  0.0 126.8 jit_solution(1846309152285613666)
XLA Ops:
  0.6 2.1 %collective-permute-start.15 = (bf16[8,128,128]{2,1,0:T(8,128)(2,1)}, bf16[8,128,128]{2,1,0:T(8,128)(2,1)S(1)}, u32[]{:S(2)}, u32[]{:S(2)}) collective-permute-start(bf16[8,128,128]{2,1,0:T(8,128)(2,1)} %bitcast.7), channel_id=1, source_target_pairs={{0,4},{1,5},{2,6},{3,7},{4,8},{5,9},{6,10},{7,11},{8,12},{9,13},{1... | collective-permute-start | bytes 786440 | tf_op jit(solution)/shard_map/ppermute | solution.py:408
  2.7 1.4 %collective-permute-start.16 = (bf16[8,128,128]{2,1,0:T(8,128)(2,1)}, bf16[8,128,128]{2,1,0:T(8,128)(2,1)S(1)}, u32[]{:S(2)}, u32[]{:S(2)}) collective-permute-start(bf16[8,128,128]{2,1,0:T(8,128)(2,1)} %bitcast.8), channel_id=1, source_target_pairs={{0,12},{1,13},{2,14},{3,15},{4,0},{5,1},{6,2},{7,3},{8,4},{9,5},{1... | collective-permute-start | bytes 786440 | tf_op jit(solution)/shard_map/ppermute | solution.py:408
  4.1 1.6 %collective-permute-start.17 = (bf16[8,128,128]{2,1,0:T(8,128)(2,1)}, bf16[8,128,128]{2,1,0:T(8,128)(2,1)S(1)}, u32[]{:S(2)}, u32[]{:S(2)}) collective-permute-start(bf16[8,128,128]{2,1,0:T(8,128)(2,1)} %bitcast.9), channel_id=1, source_target_pairs={{0,8},{1,9},{2,10},{3,11},{4,12},{5,13},{6,14},{7,15},{8,0},{9,1},... | collective-permute-start | bytes 786440 | tf_op jit(solution)/shard_map/ppermute | solution.py:408
  5.7 6.9 %collective-permute-start.21 = (bf16[8,128,128]{2,1,0:T(8,128)(2,1)}, bf16[8,128,128]{2,1,0:T(8,128)(2,1)S(1)}, u32[]{:S(2)}, u32[]{:S(2)}) collective-permute-start(bf16[8,128,128]{2,1,0:T(8,128)(2,1)} %bitcast.10), channel_id=1, source_target_pairs={{0,128},{16,144},{32,160},{48,176},{64,192},{80,208},{96,224},{112... | collective-permute-start | bytes 786440 | tf_op jit(solution)/shard_map/ppermute | solution.py:404
  12.7 1.6 %copy.10.x_cols = s32[16,16,8]{2,1,0:T(8,128)} copy(s32[16,16,8]{1,2,0:T(8,128)} %param.13) | data formatting | bytes 16384 | tf_op args[2]
  15.6 4.6 %shard_map.86 = (s32[8,128]{1,0:T(8,128)S(1)}, s32[8,128]{1,0:T(8,128)}) custom-call(s32[2]{0:T(128)} %pad_add_fusion.at, s32[16,16,8]{2,1,0:T(8,128)} %copy.9.x_rows, s32[16,16,8]{2,1,0:T(8,128)} %copy.10.x_cols, s32[16,16,16]{2,1,0:T(8,128)} %y_rows.3, s32[16,16,16]{2,1,0:T(8,128)} %y_cols.3, s32[16,16,24]{2,1,0:T(8,128)} %z_rows.3, s32[16,16,24]{2,1,0:T(8,128)} %z_cols.3), custom_call_target="tpu_custom_call" | custom-call | tf_op jit(solution)/shard_map/pallas_call | solution.py:427
  20.3 2.3 %shard_map.87 = (bf16[10,128,128]{2,1,0:T(8,128)(2,1)}, bf16[17,128,128]{2,1,0:T(8,128)(2,1)}, bf16[10,128,128]{2,1,0:T(8,128)(2,1)}, bf16[7,128,128]{2,1,0:T(8,128)(2,1)}, bf16[7,128,128]{2,1,0:T(8,128)(2,1)}) custom-call(s32[8,128]{1,0:T(8,128)S(1)} %get-tuple-element.102.given.left_send, bf16[8,128,128]{2,1,0:T(8,128)(2,1)S(1)} %bitcast.12, ...), custom_call_target="tpu_custom_call" | custom-call | tf_op jit(solution)/shard_map/pallas_call | solution.py:300
  25.9 1.4 %collective-permute-start.22 = (bf16[16,128,128]{2,1,0:T(8,128)(2,1)S(1)}, bf16[16,128,128]{2,1,0:T(8,128)(2,1)S(1)}, u32[]{:S(2)}, u32[]{:S(2)}) collective-permute-start(bf16[16,128,128]{2,1,0:T(8,128)(2,1)S(1)} %pad_maximum_fusion.refs_7_), channel_id=1, source_target_pairs={{0,32},{16,48},{32,64},{48,80},{64,96},{80,112},{96,0},{112,16},{1... | collective-permute-start | bytes 1572872 | tf_op jit(solution)/shard_map/ppermute | solution.py:404
  27.3 1.5 %collective-permute-start.23 = (bf16[16,128,128]{2,1,0:T(8,128)(2,1)S(1)}, bf16[16,128,128]{2,1,0:T(8,128)(2,1)S(1)}, u32[]{:S(2)}, u32[]{:S(2)}) collective-permute-start(bf16[16,128,128]{2,1,0:T(8,128)(2,1)S(1)} %pad_maximum_fusion.refs_7_), channel_id=1, source_target_pairs={{0,96},{16,112},{32,0},{48,16},{64,32},{80,48},{96,64},{112,80},{1... | collective-permute-start | bytes 1572872 | tf_op jit(solution)/shard_map/ppermute | solution.py:404
  28.8 1.6 %collective-permute-start.24 = (bf16[16,128,128]{2,1,0:T(8,128)(2,1)S(1)}, bf16[16,128,128]{2,1,0:T(8,128)(2,1)S(1)}, u32[]{:S(2)}, u32[]{:S(2)}) collective-permute-start(bf16[16,128,128]{2,1,0:T(8,128)(2,1)S(1)} %pad_maximum_fusion.refs_7_), channel_id=1, source_target_pairs={{0,64},{16,80},{32,96},{48,112},{64,0},{80,16},{96,32},{112,48},{1... | collective-permute-start | bytes 1572872 | tf_op jit(solution)/shard_map/ppermute | solution.py:404
  30.4 7.8 %collective-permute-done.18.refs_4_ = bf16[10,128,128]{2,1,0:T(8,128)(2,1)S(1)} collective-permute-done((bf16[10,128,128]{2,1,0:T(8,128)(2,1)}, bf16[10,128,128]{2,1,0:T(8,128)(2,1)S(1)}, u32[]{:S(2)}, u32[]{:S(2)}) %collective-permute-start.18) | collective-permute-done | bytes 327712 | tf_op jit(solution)/shard_map/ppermute | solution.py:408
  38.1 1.6 %collective-permute-start.20 = (bf16[10,128,128]{2,1,0:T(8,128)(2,1)}, bf16[10,128,128]{2,1,0:T(8,128)(2,1)S(1)}, u32[]{:S(2)}, u32[]{:S(2)}) collective-permute-start(bf16[10,128,128]{2,1,0:T(8,128)(2,1)} %get-tuple-element.109), channel_id=1, source_target_pairs={{0,3},{1,2},{2,1},{3,0},{4,7},{5,6},{6,5},{7,4},{8,11},{9,10},{10,... | collective-permute-start | bytes 983048 | tf_op jit(solution)/shard_map/ppermute | solution.py:408
  39.8 6.8 %shard_map.88 = (s32[16,128]{1,0:T(8,128)S(1)}, s32[16,128]{1,0:T(8,128)}, s32[24,128]{1,0:T(8,128)}) custom-call(s32[2]{0:T(128)} %pad_add_fusion.at, s32[8,128]{1,0:T(8,128)S(1)} %get-tuple-element.102.given.left_send, s32[8,128]{1,0:T(8,128)} %get-tuple-element.110.positions, s32[16,16,8]{2,1,0:T(8,128)} %copy.9.x_rows, s32[16,16,8]{2,1,0:T(8,128)} %copy.10.x_cols, ...), custom_call_target="tpu_custom_call" | custom-call | tf_op jit(solution)/shard_map/pallas_call | solution.py:443
  46.5 2.1 %collective-permute-start.25 = (bf16[16,128,128]{2,1,0:T(8,128)(2,1)S(1)}, bf16[16,128,128]{2,1,0:T(8,128)(2,1)S(1)}, u32[]{:S(2)}, u32[]{:S(2)}) collective-permute-start(bf16[16,128,128]{2,1,0:T(8,128)(2,1)S(1)} %pad_maximum_fusion.refs_7_), channel_id=1, source_target_pairs={{0,16},{16,0},{32,48},{48,32},{64,80},{80,64},{96,112},{112,96},{1... | collective-permute-start | bytes 1572872 | tf_op jit(solution)/shard_map/ppermute | solution.py:404
  48.6 2.1 %collective-permute-done.24.refs_10_ = bf16[16,128,128]{2,1,0:T(8,128)(2,1)S(1)} collective-permute-done((bf16[16,128,128]{2,1,0:T(8,128)(2,1)S(1)}, bf16[16,128,128]{2,1,0:T(8,128)(2,1)S(1)}, u32[]{:S(2)}, u32[]{:S(2)}) %collective-permute-start.24) | collective-permute-done | bytes 524320 | tf_op jit(solution)/shard_map/ppermute | solution.py:404
  50.7 4.9 %collective-permute-done.19.refs_5_ = bf16[17,128,128]{2,1,0:T(8,128)(2,1)S(1)} collective-permute-done((bf16[17,128,128]{2,1,0:T(8,128)(2,1)}, bf16[17,128,128]{2,1,0:T(8,128)(2,1)S(1)}, u32[]{:S(2)}, u32[]{:S(2)}) %collective-permute-start.19) | collective-permute-done | bytes 557088 | tf_op jit(solution)/shard_map/ppermute | solution.py:408
  55.6 5.5 %collective-permute-start.26 = (bf16[16,128,128]{2,1,0:T(8,128)(2,1)S(1)}, bf16[16,128,128]{2,1,0:T(8,128)(2,1)S(1)}, u32[]{:S(2)}, u32[]{:S(2)}) collective-permute-start(bf16[16,128,128]{2,1,0:T(8,128)(2,1)S(1)} %collective-permute-done.22.refs_8_), channel_id=1, source_target_pairs={{0,16},{16,0},{32,48},{48,32},{64,80},{80,64},{96,112},{112,96},{1... | collective-permute-start | bytes 1572872 | tf_op jit(solution)/shard_map/ppermute | solution.py:404
  64.2 2.5 %shard_map.89.refs_0_.refs_9_ = bf16[16,128,128]{2,1,0:T(8,128)(2,1)} custom-call(s32[16,128]{1,0:T(8,128)S(1)} %copy-done.1, bf16[8,128,128]{2,1,0:T(8,128)(2,1)} %bitcast.11, bf16[8,128,128]{2,1,0:T(8,128)(2,1)} %copy-done.4, bf16[8,128,128]{2,1,0:T(8,128)(2,1)} %copy-done.5, bf16[8,128,128]{2,1,0:T(8,128)(2,1)} %copy-done.6, ...), custom_call_target="tpu_custom_call" | custom-call | tf_op jit(solution)/shard_map/pallas_call | solution.py:388
  66.7 3.2 %collective-permute-start.29 = (bf16[16,128,128]{2,1,0:T(8,128)(2,1)}, bf16[16,128,128]{2,1,0:T(8,128)(2,1)}, u32[]{:S(2)}, u32[]{:S(2)}) collective-permute-start(bf16[16,128,128]{2,1,0:T(8,128)(2,1)} %shard_map.89.refs_0_.refs_9_), channel_id=1, source_target_pairs={{0,128},{16,144},{32,160},{48,176},{64,192},{80,208},{96,224},{112... | collective-permute-start | bytes 1572872 | tf_op jit(solution)/shard_map/ppermute | solution.py:404
  70.5 2.2 %shard_map.90 = (bf16[10,128,128]{2,1,0:T(8,128)(2,1)}, bf16[10,128,128]{2,1,0:T(8,128)(2,1)}, bf16[10,128,128]{2,1,0:T(8,128)(2,1)}) custom-call(s32[16,128]{1,0:T(8,128)S(1)} %get-tuple-element.125.given, bf16[16,128,128]{2,1,0:T(8,128)(2,1)} %shard_map.89.refs_0_.refs_9_), custom_call_target="tpu_custom_call" | custom-call | tf_op jit(solution)/shard_map/pallas_call | solution.py:300
  72.7 1.7 %collective-permute-start.31 = (bf16[10,128,128]{2,1,0:T(8,128)(2,1)}, bf16[10,128,128]{2,1,0:T(8,128)(2,1)S(1)}, u32[]{:S(2)}, u32[]{:S(2)}) collective-permute-start(bf16[10,128,128]{2,1,0:T(8,128)(2,1)} %get-tuple-element.126), channel_id=1, source_target_pairs={{0,32},{16,48},{32,64},{48,80},{64,96},{80,112},{96,0},{112,16},{1... | collective-permute-start | bytes 983048 | tf_op jit(solution)/shard_map/ppermute | solution.py:404
  75.6 1.6 %collective-permute-start.33 = (bf16[10,128,128]{2,1,0:T(8,128)(2,1)}, bf16[10,128,128]{2,1,0:T(8,128)(2,1)S(1)}, u32[]{:S(2)}, u32[]{:S(2)}) collective-permute-start(bf16[10,128,128]{2,1,0:T(8,128)(2,1)} %get-tuple-element.128), channel_id=1, source_target_pairs={{0,64},{16,80},{32,96},{48,112},{64,0},{80,16},{96,32},{112,48},{1... | collective-permute-start | bytes 983048 | tf_op jit(solution)/shard_map/ppermute | solution.py:404
  78.2 5.6 %collective-permute-done.31.refs_11_ = bf16[10,128,128]{2,1,0:T(8,128)(2,1)S(1)} collective-permute-done((bf16[10,128,128]{2,1,0:T(8,128)(2,1)}, bf16[10,128,128]{2,1,0:T(8,128)(2,1)S(1)}, u32[]{:S(2)}, u32[]{:S(2)}) %collective-permute-start.31) | collective-permute-done | bytes 327712 | tf_op jit(solution)/shard_map/ppermute | solution.py:404
  83.8 8.0 %collective-permute-done.33.refs_15_ = bf16[10,128,128]{2,1,0:T(8,128)(2,1)S(1)} collective-permute-done((bf16[10,128,128]{2,1,0:T(8,128)(2,1)}, bf16[10,128,128]{2,1,0:T(8,128)(2,1)S(1)}, u32[]{:S(2)}, u32[]{:S(2)}) %collective-permute-start.33) | collective-permute-done | bytes 327712 | tf_op jit(solution)/shard_map/ppermute | solution.py:404
  93.6 2.2 %shard_map.91 = (bf16[10,128,128]{2,1,0:T(8,128)(2,1)}, bf16[10,128,128]{2,1,0:T(8,128)(2,1)}, bf16[10,128,128]{2,1,0:T(8,128)(2,1)}) custom-call(s32[16,128]{1,0:T(8,128)S(1)} %get-tuple-element.125.given, bf16[16,128,128]{2,1,0:T(8,128)(2,1)} %collective-permute-done.29.refs_0_.refs_10_), custom_call_target="tpu_custom_call" | custom-call | tf_op jit(solution)/shard_map/pallas_call | solution.py:300
  96.9 1.8 %collective-permute-start.39 = (bf16[10,128,128]{2,1,0:T(8,128)(2,1)}, bf16[10,128,128]{2,1,0:T(8,128)(2,1)S(1)}, u32[]{:S(2)}, u32[]{:S(2)}) collective-permute-start(bf16[10,128,128]{2,1,0:T(8,128)(2,1)} %get-tuple-element.139), channel_id=1, source_target_pairs={{0,96},{16,112},{32,0},{48,16},{64,32},{80,48},{96,64},{112,80},{1... | collective-permute-start | bytes 983048 | tf_op jit(solution)/shard_map/ppermute | solution.py:404
  98.8 6.9 %collective-permute-start.41 = (bf16[7,128,128]{2,1,0:T(8,128)(2,1)}, bf16[7,128,128]{2,1,0:T(8,128)(2,1)S(1)}, u32[]{:S(2)}, u32[]{:S(2)}) collective-permute-start(bf16[7,128,128]{2,1,0:T(8,128)(2,1)} %get-tuple-element.141), channel_id=1, source_target_pairs={{0,1},{1,0},{2,3},{3,2},{4,5},{5,4},{6,7},{7,6},{8,9},{9,8},{10,11... | collective-permute-start | bytes 688136 | tf_op jit(solution)/shard_map/ppermute | solution.py:408
  105.7 2.2 %collective-permute-start.42 = (bf16[7,128,128]{2,1,0:T(8,128)(2,1)}, bf16[7,128,128]{2,1,0:T(8,128)(2,1)S(1)}, u32[]{:S(2)}, u32[]{:S(2)}) collective-permute-start(bf16[7,128,128]{2,1,0:T(8,128)(2,1)} %get-tuple-element.142), channel_id=1, source_target_pairs={{0,3},{1,2},{2,1},{3,0},{4,7},{5,6},{6,5},{7,4},{8,11},{9,10},{10,... | collective-permute-start | bytes 688136 | tf_op jit(solution)/shard_map/ppermute | solution.py:408
  107.9 2.7 %collective-permute-done.41.refs_7_ = bf16[7,128,128]{2,1,0:T(8,128)(2,1)S(1)} collective-permute-done((bf16[7,128,128]{2,1,0:T(8,128)(2,1)}, bf16[7,128,128]{2,1,0:T(8,128)(2,1)S(1)}, u32[]{:S(2)}, u32[]{:S(2)}) %collective-permute-start.41) | collective-permute-done | bytes 229408 | tf_op jit(solution)/shard_map/ppermute | solution.py:408
  110.6 6.8 %collective-permute-done.42.refs_8_ = bf16[7,128,128]{2,1,0:T(8,128)(2,1)S(1)} collective-permute-done((bf16[7,128,128]{2,1,0:T(8,128)(2,1)}, bf16[7,128,128]{2,1,0:T(8,128)(2,1)S(1)}, u32[]{:S(2)}, u32[]{:S(2)}) %collective-permute-start.42) | collective-permute-done | bytes 229408 | tf_op jit(solution)/shard_map/ppermute | solution.py:408
  117.5 2.2 %collective-permute-start.43 = (bf16[10,128,128]{2,1,0:T(8,128)(2,1)S(1)}, bf16[10,128,128]{2,1,0:T(8,128)(2,1)S(1)}, u32[]{:S(2)}, u32[]{:S(2)}) collective-permute-start(bf16[10,128,128]{2,1,0:T(8,128)(2,1)S(1)} %collective-permute-done.38.refs_12_), channel_id=1, source_target_pairs={{0,16},{16,0},{32,48},{48,32},{64,80},{80,64},{96,112},{112,96},{1... | collective-permute-start | bytes 983048 | tf_op jit(solution)/shard_map/ppermute | solution.py:404
  121.9 4.7 %shard_map.92 = bf16[24,128,128]{2,1,0:T(8,128)(2,1)} custom-call(s32[24,128]{1,0:T(8,128)S(1)} %copy-done, bf16[8,128,128]{2,1,0:T(8,128)(2,1)S(1)} %bitcast.15, bf16[8,128,128]{2,1,0:T(8,128)(2,1)} %copy-done.4, bf16[8,128,128]{2,1,0:T(8,128)(2,1)} %copy-done.5, bf16[8,128,128]{2,1,0:T(8,128)(2,1)} %copy-done.6, ...), custom_call_target="tpu_custom_call" | custom-call | tf_op jit(solution)/shard_map/pallas_call | solution.py:388
  (63 shorter events, 14.5 us)
Async XLA Ops:
  0.6 19.6 %collective-permute-start.15 = (bf16[8,128,128]{2,1,0:T(8,128)(2,1)}, bf16[8,128,128]{2,1,0:T(8,128)(2,1)S(1)}, u32[]{:S(2)}, u32[]{:S(2)}) collective-permute-start(bf16[8,128,128]{2,1,0:T(8,128)(2,1)} %bitcast.7), channel_id=1, source_target_pairs={{0,4},{1,5},{2,6},{3,7},{4,8},{5,9},{6,10},{7,11},{8,12},{9,13},{1... | collective-permute-start | bytes 786440 | tf_op jit(solution)/shard_map/ppermute | solution.py:408
  2.7 17.5 %collective-permute-start.16 = (bf16[8,128,128]{2,1,0:T(8,128)(2,1)}, bf16[8,128,128]{2,1,0:T(8,128)(2,1)S(1)}, u32[]{:S(2)}, u32[]{:S(2)}) collective-permute-start(bf16[8,128,128]{2,1,0:T(8,128)(2,1)} %bitcast.8), channel_id=1, source_target_pairs={{0,12},{1,13},{2,14},{3,15},{4,0},{5,1},{6,2},{7,3},{8,4},{9,5},{1... | collective-permute-start | bytes 786440 | tf_op jit(solution)/shard_map/ppermute | solution.py:408
  4.1 16.1 %collective-permute-start.17 = (bf16[8,128,128]{2,1,0:T(8,128)(2,1)}, bf16[8,128,128]{2,1,0:T(8,128)(2,1)S(1)}, u32[]{:S(2)}, u32[]{:S(2)}) collective-permute-start(bf16[8,128,128]{2,1,0:T(8,128)(2,1)} %bitcast.9), channel_id=1, source_target_pairs={{0,8},{1,9},{2,10},{3,11},{4,12},{5,13},{6,14},{7,15},{8,0},{9,1},... | collective-permute-start | bytes 786440 | tf_op jit(solution)/shard_map/ppermute | solution.py:408
  5.7 18.9 %collective-permute-start.21 = (bf16[8,128,128]{2,1,0:T(8,128)(2,1)}, bf16[8,128,128]{2,1,0:T(8,128)(2,1)S(1)}, u32[]{:S(2)}, u32[]{:S(2)}) collective-permute-start(bf16[8,128,128]{2,1,0:T(8,128)(2,1)} %bitcast.10), channel_id=1, source_target_pairs={{0,128},{16,144},{32,160},{48,176},{64,192},{80,208},{96,224},{112... | collective-permute-start | bytes 786440 | tf_op jit(solution)/shard_map/ppermute | solution.py:404
  22.6 15.5 %collective-permute-start.18 = (bf16[10,128,128]{2,1,0:T(8,128)(2,1)}, bf16[10,128,128]{2,1,0:T(8,128)(2,1)S(1)}, u32[]{:S(2)}, u32[]{:S(2)}) collective-permute-start(bf16[10,128,128]{2,1,0:T(8,128)(2,1)} %get-tuple-element.106), channel_id=1, source_target_pairs={{0,1},{1,0},{2,3},{3,2},{4,5},{5,4},{6,7},{7,6},{8,9},{9,8},{10,11... | collective-permute-start | bytes 983048 | tf_op jit(solution)/shard_map/ppermute | solution.py:408
  23.4 32.2 %collective-permute-start.19 = (bf16[17,128,128]{2,1,0:T(8,128)(2,1)}, bf16[17,128,128]{2,1,0:T(8,128)(2,1)S(1)}, u32[]{:S(2)}, u32[]{:S(2)}) collective-permute-start(bf16[17,128,128]{2,1,0:T(8,128)(2,1)} %get-tuple-element.107), channel_id=1, source_target_pairs={{0,2},{1,3},{2,0},{3,1},{4,6},{5,7},{6,4},{7,5},{8,10},{9,11},{10,... | collective-permute-start | bytes 1671176 | tf_op jit(solution)/shard_map/ppermute | solution.py:408
  25.9 20.6 %collective-permute-start.22 = (bf16[16,128,128]{2,1,0:T(8,128)(2,1)S(1)}, bf16[16,128,128]{2,1,0:T(8,128)(2,1)S(1)}, u32[]{:S(2)}, u32[]{:S(2)}) collective-permute-start(bf16[16,128,128]{2,1,0:T(8,128)(2,1)S(1)} %pad_maximum_fusion.refs_7_), channel_id=1, source_target_pairs={{0,32},{16,48},{32,64},{48,80},{64,96},{80,112},{96,0},{112,16},{1... | collective-permute-start | bytes 1572872 | tf_op jit(solution)/shard_map/ppermute | solution.py:404
  27.3 21.3 %collective-permute-start.23 = (bf16[16,128,128]{2,1,0:T(8,128)(2,1)S(1)}, bf16[16,128,128]{2,1,0:T(8,128)(2,1)S(1)}, u32[]{:S(2)}, u32[]{:S(2)}) collective-permute-start(bf16[16,128,128]{2,1,0:T(8,128)(2,1)S(1)} %pad_maximum_fusion.refs_7_), channel_id=1, source_target_pairs={{0,96},{16,112},{32,0},{48,16},{64,32},{80,48},{96,64},{112,80},{1... | collective-permute-start | bytes 1572872 | tf_op jit(solution)/shard_map/ppermute | solution.py:404
  28.8 21.9 %collective-permute-start.24 = (bf16[16,128,128]{2,1,0:T(8,128)(2,1)S(1)}, bf16[16,128,128]{2,1,0:T(8,128)(2,1)S(1)}, u32[]{:S(2)}, u32[]{:S(2)}) collective-permute-start(bf16[16,128,128]{2,1,0:T(8,128)(2,1)S(1)} %pad_maximum_fusion.refs_7_), channel_id=1, source_target_pairs={{0,64},{16,80},{32,96},{48,112},{64,0},{80,16},{96,32},{112,48},{1... | collective-permute-start | bytes 1572872 | tf_op jit(solution)/shard_map/ppermute | solution.py:404
  38.1 17.5 %collective-permute-start.20 = (bf16[10,128,128]{2,1,0:T(8,128)(2,1)}, bf16[10,128,128]{2,1,0:T(8,128)(2,1)S(1)}, u32[]{:S(2)}, u32[]{:S(2)}) collective-permute-start(bf16[10,128,128]{2,1,0:T(8,128)(2,1)} %get-tuple-element.109), channel_id=1, source_target_pairs={{0,3},{1,2},{2,1},{3,0},{4,7},{5,6},{6,5},{7,4},{8,11},{9,10},{10,... | collective-permute-start | bytes 983048 | tf_op jit(solution)/shard_map/ppermute | solution.py:408
  46.5 15.1 %collective-permute-start.25 = (bf16[16,128,128]{2,1,0:T(8,128)(2,1)S(1)}, bf16[16,128,128]{2,1,0:T(8,128)(2,1)S(1)}, u32[]{:S(2)}, u32[]{:S(2)}) collective-permute-start(bf16[16,128,128]{2,1,0:T(8,128)(2,1)S(1)} %pad_maximum_fusion.refs_7_), channel_id=1, source_target_pairs={{0,16},{16,0},{32,48},{48,32},{64,80},{80,64},{96,112},{112,96},{1... | collective-permute-start | bytes 1572872 | tf_op jit(solution)/shard_map/ppermute | solution.py:404
  55.6 7.0 %collective-permute-start.26 = (bf16[16,128,128]{2,1,0:T(8,128)(2,1)S(1)}, bf16[16,128,128]{2,1,0:T(8,128)(2,1)S(1)}, u32[]{:S(2)}, u32[]{:S(2)}) collective-permute-start(bf16[16,128,128]{2,1,0:T(8,128)(2,1)S(1)} %collective-permute-done.22.refs_8_), channel_id=1, source_target_pairs={{0,16},{16,0},{32,48},{48,32},{64,80},{80,64},{96,112},{112,96},{1... | collective-permute-start | bytes 1572872 | tf_op jit(solution)/shard_map/ppermute | solution.py:404
  61.1 2.3 %collective-permute-start.27 = (bf16[16,128,128]{2,1,0:T(8,128)(2,1)S(1)}, bf16[16,128,128]{2,1,0:T(8,128)(2,1)S(1)}, u32[]{:S(2)}, u32[]{:S(2)}) collective-permute-start(bf16[16,128,128]{2,1,0:T(8,128)(2,1)S(1)} %collective-permute-done.23.refs_9_), channel_id=1, source_target_pairs={{0,16},{16,0},{32,48},{48,32},{64,80},{80,64},{96,112},{112,96},{1... | collective-permute-start | bytes 1572872 | tf_op jit(solution)/shard_map/ppermute | solution.py:404
  61.1 3.0 %collective-permute-start.28 = (bf16[16,128,128]{2,1,0:T(8,128)(2,1)S(1)}, bf16[16,128,128]{2,1,0:T(8,128)(2,1)S(1)}, u32[]{:S(2)}, u32[]{:S(2)}) collective-permute-start(bf16[16,128,128]{2,1,0:T(8,128)(2,1)S(1)} %collective-permute-done.24.refs_10_), channel_id=1, source_target_pairs={{0,16},{16,0},{32,48},{48,32},{64,80},{80,64},{96,112},{112,96},{1... | collective-permute-start | bytes 1572872 | tf_op jit(solution)/shard_map/ppermute | solution.py:404
  66.7 25.2 %collective-permute-start.29 = (bf16[16,128,128]{2,1,0:T(8,128)(2,1)}, bf16[16,128,128]{2,1,0:T(8,128)(2,1)}, u32[]{:S(2)}, u32[]{:S(2)}) collective-permute-start(bf16[16,128,128]{2,1,0:T(8,128)(2,1)} %shard_map.89.refs_0_.refs_9_), channel_id=1, source_target_pairs={{0,128},{16,144},{32,160},{48,176},{64,192},{80,208},{96,224},{112... | collective-permute-start | bytes 1572872 | tf_op jit(solution)/shard_map/ppermute | solution.py:404
  69.9 22.0 %collective-permute-start.30 = (bf16[16,128,128]{2,1,0:T(8,128)(2,1)}, bf16[16,128,128]{2,1,0:T(8,128)(2,1)S(1)}, u32[]{:S(2)}, u32[]{:S(2)}) collective-permute-start(bf16[16,128,128]{2,1,0:T(8,128)(2,1)} %shard_map.89.refs_0_.refs_9_), channel_id=1, source_target_pairs={{0,16},{16,0},{32,48},{48,32},{64,80},{80,64},{96,112},{112,96},{1... | collective-permute-start | bytes 1572872 | tf_op jit(solution)/shard_map/ppermute | solution.py:404
  72.7 11.0 %collective-permute-start.31 = (bf16[10,128,128]{2,1,0:T(8,128)(2,1)}, bf16[10,128,128]{2,1,0:T(8,128)(2,1)S(1)}, u32[]{:S(2)}, u32[]{:S(2)}) collective-permute-start(bf16[10,128,128]{2,1,0:T(8,128)(2,1)} %get-tuple-element.126), channel_id=1, source_target_pairs={{0,32},{16,48},{32,64},{48,80},{64,96},{80,112},{96,0},{112,16},{1... | collective-permute-start | bytes 983048 | tf_op jit(solution)/shard_map/ppermute | solution.py:404
  74.4 9.4 %collective-permute-start.32 = (bf16[10,128,128]{2,1,0:T(8,128)(2,1)}, bf16[10,128,128]{2,1,0:T(8,128)(2,1)S(1)}, u32[]{:S(2)}, u32[]{:S(2)}) collective-permute-start(bf16[10,128,128]{2,1,0:T(8,128)(2,1)} %get-tuple-element.127), channel_id=1, source_target_pairs={{0,96},{16,112},{32,0},{48,16},{64,32},{80,48},{96,64},{112,80},{1... | collective-permute-start | bytes 983048 | tf_op jit(solution)/shard_map/ppermute | solution.py:404
  75.6 16.2 %collective-permute-start.33 = (bf16[10,128,128]{2,1,0:T(8,128)(2,1)}, bf16[10,128,128]{2,1,0:T(8,128)(2,1)S(1)}, u32[]{:S(2)}, u32[]{:S(2)}) collective-permute-start(bf16[10,128,128]{2,1,0:T(8,128)(2,1)} %get-tuple-element.128), channel_id=1, source_target_pairs={{0,64},{16,80},{32,96},{48,112},{64,0},{80,16},{96,32},{112,48},{1... | collective-permute-start | bytes 983048 | tf_op jit(solution)/shard_map/ppermute | solution.py:404
  92.1 29.8 %copy-start.3 = (bf16[1,1,8,128,128]{4,3,2,1,0:T(8,128)(2,1)S(1)}, bf16[1,1,8,128,128]{4,3,2,1,0:T(8,128)(2,1)}, u32[]{:S(2)}) copy-start(bf16[1,1,8,128,128]{4,3,2,1,0:T(8,128)(2,1)} %param.11) | copy-start | bytes 786436
  92.1 4.0 %collective-permute-start.34 = (bf16[16,128,128]{2,1,0:T(8,128)(2,1)}, bf16[16,128,128]{2,1,0:T(8,128)(2,1)S(1)}, u32[]{:S(2)}, u32[]{:S(2)}) collective-permute-start(bf16[16,128,128]{2,1,0:T(8,128)(2,1)} %collective-permute-done.29.refs_0_.refs_10_), channel_id=1, source_target_pairs={{0,16},{16,0},{32,48},{48,32},{64,80},{80,64},{96,112},{112,96},{1... | collective-permute-start | bytes 1572872 | tf_op jit(solution)/shard_map/ppermute | solution.py:404
  93.0 2.9 %collective-permute-start.35 = (bf16[10,128,128]{2,1,0:T(8,128)(2,1)S(1)}, bf16[10,128,128]{2,1,0:T(8,128)(2,1)}, u32[]{:S(2)}, u32[]{:S(2)}) collective-permute-start(bf16[10,128,128]{2,1,0:T(8,128)(2,1)S(1)} %collective-permute-done.31.refs_11_), channel_id=1, source_target_pairs={{0,16},{16,0},{32,48},{48,32},{64,80},{80,64},{96,112},{112,96},{1... | collective-permute-start | bytes 983048 | tf_op jit(solution)/shard_map/ppermute | solution.py:404
  93.1 2.8 %collective-permute-start.36 = (bf16[10,128,128]{2,1,0:T(8,128)(2,1)S(1)}, bf16[10,128,128]{2,1,0:T(8,128)(2,1)}, u32[]{:S(2)}, u32[]{:S(2)}) collective-permute-start(bf16[10,128,128]{2,1,0:T(8,128)(2,1)S(1)} %collective-permute-done.32.refs_13_), channel_id=1, source_target_pairs={{0,16},{16,0},{32,48},{48,32},{64,80},{80,64},{96,112},{112,96},{1... | collective-permute-start | bytes 983048 | tf_op jit(solution)/shard_map/ppermute | solution.py:404
  93.5 2.6 %collective-permute-start.37 = (bf16[10,128,128]{2,1,0:T(8,128)(2,1)S(1)}, bf16[10,128,128]{2,1,0:T(8,128)(2,1)}, u32[]{:S(2)}, u32[]{:S(2)}) collective-permute-start(bf16[10,128,128]{2,1,0:T(8,128)(2,1)S(1)} %collective-permute-done.33.refs_15_), channel_id=1, source_target_pairs={{0,16},{16,0},{32,48},{48,32},{64,80},{80,64},{96,112},{112,96},{1... | collective-permute-start | bytes 983048 | tf_op jit(solution)/shard_map/ppermute | solution.py:404
  96.1 21.4 %collective-permute-start.38 = (bf16[10,128,128]{2,1,0:T(8,128)(2,1)}, bf16[10,128,128]{2,1,0:T(8,128)(2,1)S(1)}, u32[]{:S(2)}, u32[]{:S(2)}) collective-permute-start(bf16[10,128,128]{2,1,0:T(8,128)(2,1)} %get-tuple-element.138), channel_id=1, source_target_pairs={{0,32},{16,48},{32,64},{48,80},{64,96},{80,112},{96,0},{112,16},{1... | collective-permute-start | bytes 983048 | tf_op jit(solution)/shard_map/ppermute | solution.py:404
  96.9 20.6 %collective-permute-start.39 = (bf16[10,128,128]{2,1,0:T(8,128)(2,1)}, bf16[10,128,128]{2,1,0:T(8,128)(2,1)S(1)}, u32[]{:S(2)}, u32[]{:S(2)}) collective-permute-start(bf16[10,128,128]{2,1,0:T(8,128)(2,1)} %get-tuple-element.139), channel_id=1, source_target_pairs={{0,96},{16,112},{32,0},{48,16},{64,32},{80,48},{96,64},{112,80},{1... | collective-permute-start | bytes 983048 | tf_op jit(solution)/shard_map/ppermute | solution.py:404
  98.7 18.7 %collective-permute-start.40 = (bf16[10,128,128]{2,1,0:T(8,128)(2,1)}, bf16[10,128,128]{2,1,0:T(8,128)(2,1)S(1)}, u32[]{:S(2)}, u32[]{:S(2)}) collective-permute-start(bf16[10,128,128]{2,1,0:T(8,128)(2,1)} %get-tuple-element.140), channel_id=1, source_target_pairs={{0,64},{16,80},{32,96},{48,112},{64,0},{80,16},{96,32},{112,48},{1... | collective-permute-start | bytes 983048 | tf_op jit(solution)/shard_map/ppermute | solution.py:404
  98.8 11.8 %collective-permute-start.41 = (bf16[7,128,128]{2,1,0:T(8,128)(2,1)}, bf16[7,128,128]{2,1,0:T(8,128)(2,1)S(1)}, u32[]{:S(2)}, u32[]{:S(2)}) collective-permute-start(bf16[7,128,128]{2,1,0:T(8,128)(2,1)} %get-tuple-element.141), channel_id=1, source_target_pairs={{0,1},{1,0},{2,3},{3,2},{4,5},{5,4},{6,7},{7,6},{8,9},{9,8},{10,11... | collective-permute-start | bytes 688136 | tf_op jit(solution)/shard_map/ppermute | solution.py:408
  105.7 11.7 %collective-permute-start.42 = (bf16[7,128,128]{2,1,0:T(8,128)(2,1)}, bf16[7,128,128]{2,1,0:T(8,128)(2,1)S(1)}, u32[]{:S(2)}, u32[]{:S(2)}) collective-permute-start(bf16[7,128,128]{2,1,0:T(8,128)(2,1)} %get-tuple-element.142), channel_id=1, source_target_pairs={{0,3},{1,2},{2,1},{3,0},{4,7},{5,6},{6,5},{7,4},{8,11},{9,10},{10,... | collective-permute-start | bytes 688136 | tf_op jit(solution)/shard_map/ppermute | solution.py:408
  117.5 3.5 %collective-permute-start.43 = (bf16[10,128,128]{2,1,0:T(8,128)(2,1)S(1)}, bf16[10,128,128]{2,1,0:T(8,128)(2,1)S(1)}, u32[]{:S(2)}, u32[]{:S(2)}) collective-permute-start(bf16[10,128,128]{2,1,0:T(8,128)(2,1)S(1)} %collective-permute-done.38.refs_12_), channel_id=1, source_target_pairs={{0,16},{16,0},{32,48},{48,32},{64,80},{80,64},{96,112},{112,96},{1... | collective-permute-start | bytes 983048 | tf_op jit(solution)/shard_map/ppermute | solution.py:404
  119.7 1.7 %collective-permute-start.44 = (bf16[10,128,128]{2,1,0:T(8,128)(2,1)S(1)}, bf16[10,128,128]{2,1,0:T(8,128)(2,1)S(1)}, u32[]{:S(2)}, u32[]{:S(2)}) collective-permute-start(bf16[10,128,128]{2,1,0:T(8,128)(2,1)S(1)} %collective-permute-done.39.refs_14_), channel_id=1, source_target_pairs={{0,16},{16,0},{32,48},{48,32},{64,80},{80,64},{96,112},{112,96},{1... | collective-permute-start | bytes 983048 | tf_op jit(solution)/shard_map/ppermute | solution.py:404
  119.8 2.1 %collective-permute-start.45 = (bf16[10,128,128]{2,1,0:T(8,128)(2,1)S(1)}, bf16[10,128,128]{2,1,0:T(8,128)(2,1)S(1)}, u32[]{:S(2)}, u32[]{:S(2)}) collective-permute-start(bf16[10,128,128]{2,1,0:T(8,128)(2,1)S(1)} %collective-permute-done.40.refs_16_), channel_id=1, source_target_pairs={{0,16},{16,0},{32,48},{48,32},{64,80},{80,64},{96,112},{112,96},{1... | collective-permute-start | bytes 983048 | tf_op jit(solution)/shard_map/ppermute | solution.py:404
  (7 other events, 66.6 us)

commit v4 on v3

--- a/solution.py
+++ b/solution.py
@@ -329,7 +329,8 @@
         side, at, skip, size, _ = layout[n]
         buffer = (left, right)[side]
         source = pieces[n] if skip is None else pieces[n].at[pl.ds(skip, size)]
-        return pltpu.make_async_copy(source, buffer.at[pl.ds(at, size)], sems.at[n])
+        sem = sems.at[n if layout[n][4] else len(layout) + 1 + side]
+        return pltpu.make_async_copy(source, buffer.at[pl.ds(at, size)], sem)
 
     def each(act, flagged):
         for n, piece in enumerate(layout):
@@ -353,7 +354,10 @@
         each(lambda c: c.start(), True)
         each(lambda c: c.wait(), True)
 
-    each(lambda c: c.wait(), False)
+    for side, buffer in enumerate((left, right)):
+        total = sum(piece[3] for piece in layout if piece[0] == side and not piece[4])
+        span = buffer.at[pl.ds(0, total)]
+        pltpu.make_async_copy(span, span, sems.at[len(layout) + 1 + side]).wait()
 
     def product(t, q):
         code = plan[t, q]
@@ -394,7 +398,7 @@
             pltpu.VMEM((sizes[0], BLOCK, BLOCK), jnp.bfloat16),
             pltpu.VMEM((sizes[1], BLOCK, BLOCK), jnp.bfloat16),
             pltpu.SMEM(plan.shape, jnp.int32),
-            pltpu.SemaphoreType.DMA((len(pieces) + 1,)),
+            pltpu.SemaphoreType.DMA((len(pieces) + 3,)),
         ],
         compiler_params=pltpu.CompilerParams(vmem_limit_bytes=32 * 1024 * 1024),
     )(plan, *[p[-1] for p in pieces])

time: 127 us -> 127 us (level)
  no operation moved by 1% of the time
where the time goes in v4:
time: 127 us
  starting transfers between devices  52.4 us (41%)
  waiting for transfers between devices  42 us (33%)
  Pallas kernels  25.9 us (20%)
  local copies, waits for them, and re-layouts  3.4 us (3%)
  between operations  2.19 us (2%)
    ppermute x23, starting transfers between devices, row_send(): return lax.ppermute(blocks, 'row', perm)  35.1 us
    ppermute x8, waiting for transfers between devices, col_send(): return lax.ppermute(blocks, 'col', perm)  22.2 us
    ppermute x23, waiting for transfers between devices, row_send(): return lax.ppermute(blocks, 'row', perm)  19.8 us
    ppermute x8, starting transfers between devices, col_send(): return lax.ppermute(blocks, 'col', perm)  17.3 us
    pallas_call x2, Pallas kernels, products(): pl.pallas_call(functools.partial(products_kernel, layout, update), out_sh...  7.77 us
    pallas_call x3, Pallas kernels, pack(): pl.pallas_call(functools.partial(pack_kernel, unit, len(sources), parts),...  6.78 us
    pallas_call x1, Pallas kernels, shards(): pl.pallas_call(right_kernel, out_shape=(jax.ShapeDtypeStruct((16, 128), j...  6.77 us
    pallas_call x1, Pallas kernels, shards(): pl.pallas_call(left_kernel, out_shape=(jax.ShapeDtypeStruct((8, 128), jnp...  4.62 us
  transfers between devices with their start and end apart: 31, of which 14 were waited for; matrix products, arithmetic and copies ran while one was open for 3% of the time, Pallas kernels for 14%

profile of v4, /device:TPU:1, one launch (start us, length us, event | category | flops | bytes accessed | tf_op | source)
XLA Modules:
  0.0 126.8 jit_solution(10573627233551018185)
XLA Ops:
  0.6 2.1 %collective-permute-start.15 = (bf16[8,128,128]{2,1,0:T(8,128)(2,1)}, bf16[8,128,128]{2,1,0:T(8,128)(2,1)S(1)}, u32[]{:S(2)}, u32[]{:S(2)}) collective-permute-start(bf16[8,128,128]{2,1,0:T(8,128)(2,1)} %bitcast.7), channel_id=1, source_target_pairs={{0,4},{1,5},{2,6},{3,7},{4,8},{5,9},{6,10},{7,11},{8,12},{9,13},{1... | collective-permute-start | bytes 786440 | tf_op jit(solution)/shard_map/ppermute | solution.py:412
  4.1 1.6 %collective-permute-start.17 = (bf16[8,128,128]{2,1,0:T(8,128)(2,1)}, bf16[8,128,128]{2,1,0:T(8,128)(2,1)S(1)}, u32[]{:S(2)}, u32[]{:S(2)}) collective-permute-start(bf16[8,128,128]{2,1,0:T(8,128)(2,1)} %bitcast.9), channel_id=1, source_target_pairs={{0,8},{1,9},{2,10},{3,11},{4,12},{5,13},{6,14},{7,15},{8,0},{9,1},... | collective-permute-start | bytes 786440 | tf_op jit(solution)/shard_map/ppermute | solution.py:412
  5.7 6.9 %collective-permute-start.21 = (bf16[8,128,128]{2,1,0:T(8,128)(2,1)}, bf16[8,128,128]{2,1,0:T(8,128)(2,1)S(1)}, u32[]{:S(2)}, u32[]{:S(2)}) collective-permute-start(bf16[8,128,128]{2,1,0:T(8,128)(2,1)} %bitcast.10), channel_id=1, source_target_pairs={{0,128},{16,144},{32,160},{48,176},{64,192},{80,208},{96,224},{112... | collective-permute-start | bytes 786440 | tf_op jit(solution)/shard_map/ppermute | solution.py:408
  12.7 1.6 %copy.10.x_cols = s32[16,16,8]{2,1,0:T(8,128)} copy(s32[16,16,8]{1,2,0:T(8,128)} %param.13) | data formatting | bytes 16384 | tf_op args[2]
  15.6 4.6 %shard_map.86 = (s32[8,128]{1,0:T(8,128)S(1)}, s32[8,128]{1,0:T(8,128)}) custom-call(s32[2]{0:T(128)} %pad_add_fusion.at, s32[16,16,8]{2,1,0:T(8,128)} %copy.9.x_rows, s32[16,16,8]{2,1,0:T(8,128)} %copy.10.x_cols, s32[16,16,16]{2,1,0:T(8,128)} %y_rows.3, s32[16,16,16]{2,1,0:T(8,128)} %y_cols.3, s32[16,16,24]{2,1,0:T(8,128)} %z_rows.3, s32[16,16,24]{2,1,0:T(8,128)} %z_cols.3), custom_call_target="tpu_custom_call" | custom-call | tf_op jit(solution)/shard_map/pallas_call | solution.py:431
  20.3 2.3 %shard_map.87 = (bf16[10,128,128]{2,1,0:T(8,128)(2,1)}, bf16[17,128,128]{2,1,0:T(8,128)(2,1)}, bf16[10,128,128]{2,1,0:T(8,128)(2,1)}, bf16[7,128,128]{2,1,0:T(8,128)(2,1)}, bf16[7,128,128]{2,1,0:T(8,128)(2,1)}) custom-call(s32[8,128]{1,0:T(8,128)S(1)} %get-tuple-element.102.given.left_send, bf16[8,128,128]{2,1,0:T(8,128)(2,1)S(1)} %bitcast.12, ...), custom_call_target="tpu_custom_call" | custom-call | tf_op jit(solution)/shard_map/pallas_call | solution.py:300
  25.9 1.4 %collective-permute-start.22 = (bf16[16,128,128]{2,1,0:T(8,128)(2,1)S(1)}, bf16[16,128,128]{2,1,0:T(8,128)(2,1)S(1)}, u32[]{:S(2)}, u32[]{:S(2)}) collective-permute-start(bf16[16,128,128]{2,1,0:T(8,128)(2,1)S(1)} %pad_maximum_fusion.refs_7_), channel_id=1, source_target_pairs={{0,32},{16,48},{32,64},{48,80},{64,96},{80,112},{96,0},{112,16},{1... | collective-permute-start | bytes 1572872 | tf_op jit(solution)/shard_map/ppermute | solution.py:408
  27.3 1.5 %collective-permute-start.23 = (bf16[16,128,128]{2,1,0:T(8,128)(2,1)S(1)}, bf16[16,128,128]{2,1,0:T(8,128)(2,1)S(1)}, u32[]{:S(2)}, u32[]{:S(2)}) collective-permute-start(bf16[16,128,128]{2,1,0:T(8,128)(2,1)S(1)} %pad_maximum_fusion.refs_7_), channel_id=1, source_target_pairs={{0,96},{16,112},{32,0},{48,16},{64,32},{80,48},{96,64},{112,80},{1... | collective-permute-start | bytes 1572872 | tf_op jit(solution)/shard_map/ppermute | solution.py:408
  28.8 1.6 %collective-permute-start.24 = (bf16[16,128,128]{2,1,0:T(8,128)(2,1)S(1)}, bf16[16,128,128]{2,1,0:T(8,128)(2,1)S(1)}, u32[]{:S(2)}, u32[]{:S(2)}) collective-permute-start(bf16[16,128,128]{2,1,0:T(8,128)(2,1)S(1)} %pad_maximum_fusion.refs_7_), channel_id=1, source_target_pairs={{0,64},{16,80},{32,96},{48,112},{64,0},{80,16},{96,32},{112,48},{1... | collective-permute-start | bytes 1572872 | tf_op jit(solution)/shard_map/ppermute | solution.py:408
  30.4 7.8 %collective-permute-done.18.refs_4_ = bf16[10,128,128]{2,1,0:T(8,128)(2,1)S(1)} collective-permute-done((bf16[10,128,128]{2,1,0:T(8,128)(2,1)}, bf16[10,128,128]{2,1,0:T(8,128)(2,1)S(1)}, u32[]{:S(2)}, u32[]{:S(2)}) %collective-permute-start.18) | collective-permute-done | bytes 327712 | tf_op jit(solution)/shard_map/ppermute | solution.py:412
  38.1 1.6 %collective-permute-start.20 = (bf16[10,128,128]{2,1,0:T(8,128)(2,1)}, bf16[10,128,128]{2,1,0:T(8,128)(2,1)S(1)}, u32[]{:S(2)}, u32[]{:S(2)}) collective-permute-start(bf16[10,128,128]{2,1,0:T(8,128)(2,1)} %get-tuple-element.109), channel_id=1, source_target_pairs={{0,3},{1,2},{2,1},{3,0},{4,7},{5,6},{6,5},{7,4},{8,11},{9,10},{10,... | collective-permute-start | bytes 983048 | tf_op jit(solution)/shard_map/ppermute | solution.py:412
  39.8 6.8 %shard_map.88 = (s32[16,128]{1,0:T(8,128)S(1)}, s32[16,128]{1,0:T(8,128)}, s32[24,128]{1,0:T(8,128)}) custom-call(s32[2]{0:T(128)} %pad_add_fusion.at, s32[8,128]{1,0:T(8,128)S(1)} %get-tuple-element.102.given.left_send, s32[8,128]{1,0:T(8,128)} %get-tuple-element.110.positions, s32[16,16,8]{2,1,0:T(8,128)} %copy.9.x_rows, s32[16,16,8]{2,1,0:T(8,128)} %copy.10.x_cols, ...), custom_call_target="tpu_custom_call" | custom-call | tf_op jit(solution)/shard_map/pallas_call | solution.py:447
  46.5 2.1 %collective-permute-start.25 = (bf16[16,128,128]{2,1,0:T(8,128)(2,1)S(1)}, bf16[16,128,128]{2,1,0:T(8,128)(2,1)S(1)}, u32[]{:S(2)}, u32[]{:S(2)}) collective-permute-start(bf16[16,128,128]{2,1,0:T(8,128)(2,1)S(1)} %pad_maximum_fusion.refs_7_), channel_id=1, source_target_pairs={{0,16},{16,0},{32,48},{48,32},{64,80},{80,64},{96,112},{112,96},{1... | collective-permute-start | bytes 1572872 | tf_op jit(solution)/shard_map/ppermute | solution.py:408
  48.6 2.1 %collective-permute-done.24.refs_10_ = bf16[16,128,128]{2,1,0:T(8,128)(2,1)S(1)} collective-permute-done((bf16[16,128,128]{2,1,0:T(8,128)(2,1)S(1)}, bf16[16,128,128]{2,1,0:T(8,128)(2,1)S(1)}, u32[]{:S(2)}, u32[]{:S(2)}) %collective-permute-start.24) | collective-permute-done | bytes 524320 | tf_op jit(solution)/shard_map/ppermute | solution.py:408
  50.7 4.9 %collective-permute-done.19.refs_5_ = bf16[17,128,128]{2,1,0:T(8,128)(2,1)S(1)} collective-permute-done((bf16[17,128,128]{2,1,0:T(8,128)(2,1)}, bf16[17,128,128]{2,1,0:T(8,128)(2,1)S(1)}, u32[]{:S(2)}, u32[]{:S(2)}) %collective-permute-start.19) | collective-permute-done | bytes 557088 | tf_op jit(solution)/shard_map/ppermute | solution.py:412
  55.6 5.5 %collective-permute-start.26 = (bf16[16,128,128]{2,1,0:T(8,128)(2,1)S(1)}, bf16[16,128,128]{2,1,0:T(8,128)(2,1)S(1)}, u32[]{:S(2)}, u32[]{:S(2)}) collective-permute-start(bf16[16,128,128]{2,1,0:T(8,128)(2,1)S(1)} %collective-permute-done.22.refs_8_), channel_id=1, source_target_pairs={{0,16},{16,0},{32,48},{48,32},{64,80},{80,64},{96,112},{112,96},{1... | collective-permute-start | bytes 1572872 | tf_op jit(solution)/shard_map/ppermute | solution.py:408
  64.2 2.5 %shard_map.89.refs_0_.refs_9_ = bf16[16,128,128]{2,1,0:T(8,128)(2,1)} custom-call(s32[16,128]{1,0:T(8,128)S(1)} %copy-done.1, bf16[8,128,128]{2,1,0:T(8,128)(2,1)} %bitcast.11, bf16[8,128,128]{2,1,0:T(8,128)(2,1)} %copy-done.4, bf16[8,128,128]{2,1,0:T(8,128)(2,1)} %copy-done.5, bf16[8,128,128]{2,1,0:T(8,128)(2,1)} %copy-done.6, ...), custom_call_target="tpu_custom_call" | custom-call | tf_op jit(solution)/shard_map/pallas_call | solution.py:392
  66.7 3.2 %collective-permute-start.29 = (bf16[16,128,128]{2,1,0:T(8,128)(2,1)}, bf16[16,128,128]{2,1,0:T(8,128)(2,1)}, u32[]{:S(2)}, u32[]{:S(2)}) collective-permute-start(bf16[16,128,128]{2,1,0:T(8,128)(2,1)} %shard_map.89.refs_0_.refs_9_), channel_id=1, source_target_pairs={{0,128},{16,144},{32,160},{48,176},{64,192},{80,208},{96,224},{112... | collective-permute-start | bytes 1572872 | tf_op jit(solution)/shard_map/ppermute | solution.py:408
  70.5 2.2 %shard_map.90 = (bf16[10,128,128]{2,1,0:T(8,128)(2,1)}, bf16[10,128,128]{2,1,0:T(8,128)(2,1)}, bf16[10,128,128]{2,1,0:T(8,128)(2,1)}) custom-call(s32[16,128]{1,0:T(8,128)S(1)} %get-tuple-element.125.given, bf16[16,128,128]{2,1,0:T(8,128)(2,1)} %shard_map.89.refs_0_.refs_9_), custom_call_target="tpu_custom_call" | custom-call | tf_op jit(solution)/shard_map/pallas_call | solution.py:300
  72.7 1.4 %collective-permute-start.31 = (bf16[10,128,128]{2,1,0:T(8,128)(2,1)}, bf16[10,128,128]{2,1,0:T(8,128)(2,1)S(1)}, u32[]{:S(2)}, u32[]{:S(2)}) collective-permute-start(bf16[10,128,128]{2,1,0:T(8,128)(2,1)} %get-tuple-element.126), channel_id=1, source_target_pairs={{0,32},{16,48},{32,64},{48,80},{64,96},{80,112},{96,0},{112,16},{1... | collective-permute-start | bytes 983048 | tf_op jit(solution)/shard_map/ppermute | solution.py:408
  74.1 1.5 %collective-permute-start.32 = (bf16[10,128,128]{2,1,0:T(8,128)(2,1)}, bf16[10,128,128]{2,1,0:T(8,128)(2,1)S(1)}, u32[]{:S(2)}, u32[]{:S(2)}) collective-permute-start(bf16[10,128,128]{2,1,0:T(8,128)(2,1)} %get-tuple-element.127), channel_id=1, source_target_pairs={{0,96},{16,112},{32,0},{48,16},{64,32},{80,48},{96,64},{112,80},{1... | collective-permute-start | bytes 983048 | tf_op jit(solution)/shard_map/ppermute | solution.py:408
  75.7 1.8 %collective-permute-start.33 = (bf16[10,128,128]{2,1,0:T(8,128)(2,1)}, bf16[10,128,128]{2,1,0:T(8,128)(2,1)S(1)}, u32[]{:S(2)}, u32[]{:S(2)}) collective-permute-start(bf16[10,128,128]{2,1,0:T(8,128)(2,1)} %get-tuple-element.128), channel_id=1, source_target_pairs={{0,64},{16,80},{32,96},{48,112},{64,0},{80,16},{96,32},{112,48},{1... | collective-permute-start | bytes 983048 | tf_op jit(solution)/shard_map/ppermute | solution.py:408
  78.5 5.3 %collective-permute-done.31.refs_11_ = bf16[10,128,128]{2,1,0:T(8,128)(2,1)S(1)} collective-permute-done((bf16[10,128,128]{2,1,0:T(8,128)(2,1)}, bf16[10,128,128]{2,1,0:T(8,128)(2,1)S(1)}, u32[]{:S(2)}, u32[]{:S(2)}) %collective-permute-start.31) | collective-permute-done | bytes 327712 | tf_op jit(solution)/shard_map/ppermute | solution.py:408
  83.8 8.0 %collective-permute-done.33.refs_15_ = bf16[10,128,128]{2,1,0:T(8,128)(2,1)S(1)} collective-permute-done((bf16[10,128,128]{2,1,0:T(8,128)(2,1)}, bf16[10,128,128]{2,1,0:T(8,128)(2,1)S(1)}, u32[]{:S(2)}, u32[]{:S(2)}) %collective-permute-start.33) | collective-permute-done | bytes 327712 | tf_op jit(solution)/shard_map/ppermute | solution.py:408
  93.6 2.2 %shard_map.91 = (bf16[10,128,128]{2,1,0:T(8,128)(2,1)}, bf16[10,128,128]{2,1,0:T(8,128)(2,1)}, bf16[10,128,128]{2,1,0:T(8,128)(2,1)}) custom-call(s32[16,128]{1,0:T(8,128)S(1)} %get-tuple-element.125.given, bf16[16,128,128]{2,1,0:T(8,128)(2,1)} %collective-permute-done.29.refs_0_.refs_10_), custom_call_target="tpu_custom_call" | custom-call | tf_op jit(solution)/shard_map/pallas_call | solution.py:300
  96.9 1.8 %collective-permute-start.39 = (bf16[10,128,128]{2,1,0:T(8,128)(2,1)}, bf16[10,128,128]{2,1,0:T(8,128)(2,1)S(1)}, u32[]{:S(2)}, u32[]{:S(2)}) collective-permute-start(bf16[10,128,128]{2,1,0:T(8,128)(2,1)} %get-tuple-element.139), channel_id=1, source_target_pairs={{0,96},{16,112},{32,0},{48,16},{64,32},{80,48},{96,64},{112,80},{1... | collective-permute-start | bytes 983048 | tf_op jit(solution)/shard_map/ppermute | solution.py:408
  98.9 7.0 %collective-permute-start.41 = (bf16[7,128,128]{2,1,0:T(8,128)(2,1)}, bf16[7,128,128]{2,1,0:T(8,128)(2,1)S(1)}, u32[]{:S(2)}, u32[]{:S(2)}) collective-permute-start(bf16[7,128,128]{2,1,0:T(8,128)(2,1)} %get-tuple-element.141), channel_id=1, source_target_pairs={{0,1},{1,0},{2,3},{3,2},{4,5},{5,4},{6,7},{7,6},{8,9},{9,8},{10,11... | collective-permute-start | bytes 688136 | tf_op jit(solution)/shard_map/ppermute | solution.py:412
  105.8 1.5 %collective-permute-start.42 = (bf16[7,128,128]{2,1,0:T(8,128)(2,1)}, bf16[7,128,128]{2,1,0:T(8,128)(2,1)S(1)}, u32[]{:S(2)}, u32[]{:S(2)}) collective-permute-start(bf16[7,128,128]{2,1,0:T(8,128)(2,1)} %get-tuple-element.142), channel_id=1, source_target_pairs={{0,3},{1,2},{2,1},{3,0},{4,7},{5,6},{6,5},{7,4},{8,11},{9,10},{10,... | collective-permute-start | bytes 688136 | tf_op jit(solution)/shard_map/ppermute | solution.py:412
  107.4 3.5 %collective-permute-done.41.refs_7_ = bf16[7,128,128]{2,1,0:T(8,128)(2,1)S(1)} collective-permute-done((bf16[7,128,128]{2,1,0:T(8,128)(2,1)}, bf16[7,128,128]{2,1,0:T(8,128)(2,1)S(1)}, u32[]{:S(2)}, u32[]{:S(2)}) %collective-permute-start.41) | collective-permute-done | bytes 229408 | tf_op jit(solution)/shard_map/ppermute | solution.py:412
  110.9 6.0 %collective-permute-done.42.refs_8_ = bf16[7,128,128]{2,1,0:T(8,128)(2,1)S(1)} collective-permute-done((bf16[7,128,128]{2,1,0:T(8,128)(2,1)}, bf16[7,128,128]{2,1,0:T(8,128)(2,1)S(1)}, u32[]{:S(2)}, u32[]{:S(2)}) %collective-permute-start.42) | collective-permute-done | bytes 229408 | tf_op jit(solution)/shard_map/ppermute | solution.py:412
  116.9 2.2 %collective-permute-start.43 = (bf16[10,128,128]{2,1,0:T(8,128)(2,1)S(1)}, bf16[10,128,128]{2,1,0:T(8,128)(2,1)S(1)}, u32[]{:S(2)}, u32[]{:S(2)}) collective-permute-start(bf16[10,128,128]{2,1,0:T(8,128)(2,1)S(1)} %collective-permute-done.38.refs_12_), channel_id=1, source_target_pairs={{0,16},{16,0},{32,48},{48,32},{64,80},{80,64},{96,112},{112,96},{1... | collective-permute-start | bytes 983048 | tf_op jit(solution)/shard_map/ppermute | solution.py:408
  121.3 5.3 %shard_map.92 = bf16[24,128,128]{2,1,0:T(8,128)(2,1)} custom-call(s32[24,128]{1,0:T(8,128)S(1)} %copy-done, bf16[8,128,128]{2,1,0:T(8,128)(2,1)S(1)} %bitcast.15, bf16[8,128,128]{2,1,0:T(8,128)(2,1)} %copy-done.4, bf16[8,128,128]{2,1,0:T(8,128)(2,1)} %copy-done.5, bf16[8,128,128]{2,1,0:T(8,128)(2,1)} %copy-done.6, ...), custom_call_target="tpu_custom_call" | custom-call | tf_op jit(solution)/shard_map/pallas_call | solution.py:392
  (63 shorter events, 14.6 us)
Async XLA Ops:
  0.6 19.6 %collective-permute-start.15 = (bf16[8,128,128]{2,1,0:T(8,128)(2,1)}, bf16[8,128,128]{2,1,0:T(8,128)(2,1)S(1)}, u32[]{:S(2)}, u32[]{:S(2)}) collective-permute-start(bf16[8,128,128]{2,1,0:T(8,128)(2,1)} %bitcast.7), channel_id=1, source_target_pairs={{0,4},{1,5},{2,6},{3,7},{4,8},{5,9},{6,10},{7,11},{8,12},{9,13},{1... | collective-permute-start | bytes 786440 | tf_op jit(solution)/shard_map/ppermute | solution.py:412
  2.7 17.5 %collective-permute-start.16 = (bf16[8,128,128]{2,1,0:T(8,128)(2,1)}, bf16[8,128,128]{2,1,0:T(8,128)(2,1)S(1)}, u32[]{:S(2)}, u32[]{:S(2)}) collective-permute-start(bf16[8,128,128]{2,1,0:T(8,128)(2,1)} %bitcast.8), channel_id=1, source_target_pairs={{0,12},{1,13},{2,14},{3,15},{4,0},{5,1},{6,2},{7,3},{8,4},{9,5},{1... | collective-permute-start | bytes 786440 | tf_op jit(solution)/shard_map/ppermute | solution.py:412
  4.1 16.1 %collective-permute-start.17 = (bf16[8,128,128]{2,1,0:T(8,128)(2,1)}, bf16[8,128,128]{2,1,0:T(8,128)(2,1)S(1)}, u32[]{:S(2)}, u32[]{:S(2)}) collective-permute-start(bf16[8,128,128]{2,1,0:T(8,128)(2,1)} %bitcast.9), channel_id=1, source_target_pairs={{0,8},{1,9},{2,10},{3,11},{4,12},{5,13},{6,14},{7,15},{8,0},{9,1},... | collective-permute-start | bytes 786440 | tf_op jit(solution)/shard_map/ppermute | solution.py:412
  5.7 18.9 %collective-permute-start.21 = (bf16[8,128,128]{2,1,0:T(8,128)(2,1)}, bf16[8,128,128]{2,1,0:T(8,128)(2,1)S(1)}, u32[]{:S(2)}, u32[]{:S(2)}) collective-permute-start(bf16[8,128,128]{2,1,0:T(8,128)(2,1)} %bitcast.10), channel_id=1, source_target_pairs={{0,128},{16,144},{32,160},{48,176},{64,192},{80,208},{96,224},{112... | collective-permute-start | bytes 786440 | tf_op jit(solution)/shard_map/ppermute | solution.py:408
  22.6 15.5 %collective-permute-start.18 = (bf16[10,128,128]{2,1,0:T(8,128)(2,1)}, bf16[10,128,128]{2,1,0:T(8,128)(2,1)S(1)}, u32[]{:S(2)}, u32[]{:S(2)}) collective-permute-start(bf16[10,128,128]{2,1,0:T(8,128)(2,1)} %get-tuple-element.106), channel_id=1, source_target_pairs={{0,1},{1,0},{2,3},{3,2},{4,5},{5,4},{6,7},{7,6},{8,9},{9,8},{10,11... | collective-permute-start | bytes 983048 | tf_op jit(solution)/shard_map/ppermute | solution.py:412
  23.4 32.2 %collective-permute-start.19 = (bf16[17,128,128]{2,1,0:T(8,128)(2,1)}, bf16[17,128,128]{2,1,0:T(8,128)(2,1)S(1)}, u32[]{:S(2)}, u32[]{:S(2)}) collective-permute-start(bf16[17,128,128]{2,1,0:T(8,128)(2,1)} %get-tuple-element.107), channel_id=1, source_target_pairs={{0,2},{1,3},{2,0},{3,1},{4,6},{5,7},{6,4},{7,5},{8,10},{9,11},{10,... | collective-permute-start | bytes 1671176 | tf_op jit(solution)/shard_map/ppermute | solution.py:412
  25.9 20.6 %collective-permute-start.22 = (bf16[16,128,128]{2,1,0:T(8,128)(2,1)S(1)}, bf16[16,128,128]{2,1,0:T(8,128)(2,1)S(1)}, u32[]{:S(2)}, u32[]{:S(2)}) collective-permute-start(bf16[16,128,128]{2,1,0:T(8,128)(2,1)S(1)} %pad_maximum_fusion.refs_7_), channel_id=1, source_target_pairs={{0,32},{16,48},{32,64},{48,80},{64,96},{80,112},{96,0},{112,16},{1... | collective-permute-start | bytes 1572872 | tf_op jit(solution)/shard_map/ppermute | solution.py:408
  27.3 21.3 %collective-permute-start.23 = (bf16[16,128,128]{2,1,0:T(8,128)(2,1)S(1)}, bf16[16,128,128]{2,1,0:T(8,128)(2,1)S(1)}, u32[]{:S(2)}, u32[]{:S(2)}) collective-permute-start(bf16[16,128,128]{2,1,0:T(8,128)(2,1)S(1)} %pad_maximum_fusion.refs_7_), channel_id=1, source_target_pairs={{0,96},{16,112},{32,0},{48,16},{64,32},{80,48},{96,64},{112,80},{1... | collective-permute-start | bytes 1572872 | tf_op jit(solution)/shard_map/ppermute | solution.py:408
  28.8 21.9 %collective-permute-start.24 = (bf16[16,128,128]{2,1,0:T(8,128)(2,1)S(1)}, bf16[16,128,128]{2,1,0:T(8,128)(2,1)S(1)}, u32[]{:S(2)}, u32[]{:S(2)}) collective-permute-start(bf16[16,128,128]{2,1,0:T(8,128)(2,1)S(1)} %pad_maximum_fusion.refs_7_), channel_id=1, source_target_pairs={{0,64},{16,80},{32,96},{48,112},{64,0},{80,16},{96,32},{112,48},{1... | collective-permute-start | bytes 1572872 | tf_op jit(solution)/shard_map/ppermute | solution.py:408
  38.1 17.5 %collective-permute-start.20 = (bf16[10,128,128]{2,1,0:T(8,128)(2,1)}, bf16[10,128,128]{2,1,0:T(8,128)(2,1)S(1)}, u32[]{:S(2)}, u32[]{:S(2)}) collective-permute-start(bf16[10,128,128]{2,1,0:T(8,128)(2,1)} %get-tuple-element.109), channel_id=1, source_target_pairs={{0,3},{1,2},{2,1},{3,0},{4,7},{5,6},{6,5},{7,4},{8,11},{9,10},{10,... | collective-permute-start | bytes 983048 | tf_op jit(solution)/shard_map/ppermute | solution.py:412
  46.5 15.1 %collective-permute-start.25 = (bf16[16,128,128]{2,1,0:T(8,128)(2,1)S(1)}, bf16[16,128,128]{2,1,0:T(8,128)(2,1)S(1)}, u32[]{:S(2)}, u32[]{:S(2)}) collective-permute-start(bf16[16,128,128]{2,1,0:T(8,128)(2,1)S(1)} %pad_maximum_fusion.refs_7_), channel_id=1, source_target_pairs={{0,16},{16,0},{32,48},{48,32},{64,80},{80,64},{96,112},{112,96},{1... | collective-permute-start | bytes 1572872 | tf_op jit(solution)/shard_map/ppermute | solution.py:408
  55.6 7.0 %collective-permute-start.26 = (bf16[16,128,128]{2,1,0:T(8,128)(2,1)S(1)}, bf16[16,128,128]{2,1,0:T(8,128)(2,1)S(1)}, u32[]{:S(2)}, u32[]{:S(2)}) collective-permute-start(bf16[16,128,128]{2,1,0:T(8,128)(2,1)S(1)} %collective-permute-done.22.refs_8_), channel_id=1, source_target_pairs={{0,16},{16,0},{32,48},{48,32},{64,80},{80,64},{96,112},{112,96},{1... | collective-permute-start | bytes 1572872 | tf_op jit(solution)/shard_map/ppermute | solution.py:408
  61.1 2.3 %collective-permute-start.27 = (bf16[16,128,128]{2,1,0:T(8,128)(2,1)S(1)}, bf16[16,128,128]{2,1,0:T(8,128)(2,1)S(1)}, u32[]{:S(2)}, u32[]{:S(2)}) collective-permute-start(bf16[16,128,128]{2,1,0:T(8,128)(2,1)S(1)} %collective-permute-done.23.refs_9_), channel_id=1, source_target_pairs={{0,16},{16,0},{32,48},{48,32},{64,80},{80,64},{96,112},{112,96},{1... | collective-permute-start | bytes 1572872 | tf_op jit(solution)/shard_map/ppermute | solution.py:408
  61.1 3.0 %collective-permute-start.28 = (bf16[16,128,128]{2,1,0:T(8,128)(2,1)S(1)}, bf16[16,128,128]{2,1,0:T(8,128)(2,1)S(1)}, u32[]{:S(2)}, u32[]{:S(2)}) collective-permute-start(bf16[16,128,128]{2,1,0:T(8,128)(2,1)S(1)} %collective-permute-done.24.refs_10_), channel_id=1, source_target_pairs={{0,16},{16,0},{32,48},{48,32},{64,80},{80,64},{96,112},{112,96},{1... | collective-permute-start | bytes 1572872 | tf_op jit(solution)/shard_map/ppermute | solution.py:408
  66.7 25.2 %collective-permute-start.29 = (bf16[16,128,128]{2,1,0:T(8,128)(2,1)}, bf16[16,128,128]{2,1,0:T(8,128)(2,1)}, u32[]{:S(2)}, u32[]{:S(2)}) collective-permute-start(bf16[16,128,128]{2,1,0:T(8,128)(2,1)} %shard_map.89.refs_0_.refs_9_), channel_id=1, source_target_pairs={{0,128},{16,144},{32,160},{48,176},{64,192},{80,208},{96,224},{112... | collective-permute-start | bytes 1572872 | tf_op jit(solution)/shard_map/ppermute | solution.py:408
  69.9 22.0 %collective-permute-start.30 = (bf16[16,128,128]{2,1,0:T(8,128)(2,1)}, bf16[16,128,128]{2,1,0:T(8,128)(2,1)S(1)}, u32[]{:S(2)}, u32[]{:S(2)}) collective-permute-start(bf16[16,128,128]{2,1,0:T(8,128)(2,1)} %shard_map.89.refs_0_.refs_9_), channel_id=1, source_target_pairs={{0,16},{16,0},{32,48},{48,32},{64,80},{80,64},{96,112},{112,96},{1... | collective-permute-start | bytes 1572872 | tf_op jit(solution)/shard_map/ppermute | solution.py:408
  72.7 11.0 %collective-permute-start.31 = (bf16[10,128,128]{2,1,0:T(8,128)(2,1)}, bf16[10,128,128]{2,1,0:T(8,128)(2,1)S(1)}, u32[]{:S(2)}, u32[]{:S(2)}) collective-permute-start(bf16[10,128,128]{2,1,0:T(8,128)(2,1)} %get-tuple-element.126), channel_id=1, source_target_pairs={{0,32},{16,48},{32,64},{48,80},{64,96},{80,112},{96,0},{112,16},{1... | collective-permute-start | bytes 983048 | tf_op jit(solution)/shard_map/ppermute | solution.py:408
  74.1 9.7 %collective-permute-start.32 = (bf16[10,128,128]{2,1,0:T(8,128)(2,1)}, bf16[10,128,128]{2,1,0:T(8,128)(2,1)S(1)}, u32[]{:S(2)}, u32[]{:S(2)}) collective-permute-start(bf16[10,128,128]{2,1,0:T(8,128)(2,1)} %get-tuple-element.127), channel_id=1, source_target_pairs={{0,96},{16,112},{32,0},{48,16},{64,32},{80,48},{96,64},{112,80},{1... | collective-permute-start | bytes 983048 | tf_op jit(solution)/shard_map/ppermute | solution.py:408
  75.7 16.2 %collective-permute-start.33 = (bf16[10,128,128]{2,1,0:T(8,128)(2,1)}, bf16[10,128,128]{2,1,0:T(8,128)(2,1)S(1)}, u32[]{:S(2)}, u32[]{:S(2)}) collective-permute-start(bf16[10,128,128]{2,1,0:T(8,128)(2,1)} %get-tuple-element.128), channel_id=1, source_target_pairs={{0,64},{16,80},{32,96},{48,112},{64,0},{80,16},{96,32},{112,48},{1... | collective-permute-start | bytes 983048 | tf_op jit(solution)/shard_map/ppermute | solution.py:408
  92.1 29.3 %copy-start.3 = (bf16[1,1,8,128,128]{4,3,2,1,0:T(8,128)(2,1)S(1)}, bf16[1,1,8,128,128]{4,3,2,1,0:T(8,128)(2,1)}, u32[]{:S(2)}) copy-start(bf16[1,1,8,128,128]{4,3,2,1,0:T(8,128)(2,1)} %param.11) | copy-start | bytes 786436
  92.1 4.0 %collective-permute-start.34 = (bf16[16,128,128]{2,1,0:T(8,128)(2,1)}, bf16[16,128,128]{2,1,0:T(8,128)(2,1)S(1)}, u32[]{:S(2)}, u32[]{:S(2)}) collective-permute-start(bf16[16,128,128]{2,1,0:T(8,128)(2,1)} %collective-permute-done.29.refs_0_.refs_10_), channel_id=1, source_target_pairs={{0,16},{16,0},{32,48},{48,32},{64,80},{80,64},{96,112},{112,96},{1... | collective-permute-start | bytes 1572872 | tf_op jit(solution)/shard_map/ppermute | solution.py:408
  93.0 2.9 %collective-permute-start.35 = (bf16[10,128,128]{2,1,0:T(8,128)(2,1)S(1)}, bf16[10,128,128]{2,1,0:T(8,128)(2,1)}, u32[]{:S(2)}, u32[]{:S(2)}) collective-permute-start(bf16[10,128,128]{2,1,0:T(8,128)(2,1)S(1)} %collective-permute-done.31.refs_11_), channel_id=1, source_target_pairs={{0,16},{16,0},{32,48},{48,32},{64,80},{80,64},{96,112},{112,96},{1... | collective-permute-start | bytes 983048 | tf_op jit(solution)/shard_map/ppermute | solution.py:408
  93.1 2.8 %collective-permute-start.36 = (bf16[10,128,128]{2,1,0:T(8,128)(2,1)S(1)}, bf16[10,128,128]{2,1,0:T(8,128)(2,1)}, u32[]{:S(2)}, u32[]{:S(2)}) collective-permute-start(bf16[10,128,128]{2,1,0:T(8,128)(2,1)S(1)} %collective-permute-done.32.refs_13_), channel_id=1, source_target_pairs={{0,16},{16,0},{32,48},{48,32},{64,80},{80,64},{96,112},{112,96},{1... | collective-permute-start | bytes 983048 | tf_op jit(solution)/shard_map/ppermute | solution.py:408
  93.5 2.6 %collective-permute-start.37 = (bf16[10,128,128]{2,1,0:T(8,128)(2,1)S(1)}, bf16[10,128,128]{2,1,0:T(8,128)(2,1)}, u32[]{:S(2)}, u32[]{:S(2)}) collective-permute-start(bf16[10,128,128]{2,1,0:T(8,128)(2,1)S(1)} %collective-permute-done.33.refs_15_), channel_id=1, source_target_pairs={{0,16},{16,0},{32,48},{48,32},{64,80},{80,64},{96,112},{112,96},{1... | collective-permute-start | bytes 983048 | tf_op jit(solution)/shard_map/ppermute | solution.py:408
  96.1 20.8 %collective-permute-start.38 = (bf16[10,128,128]{2,1,0:T(8,128)(2,1)}, bf16[10,128,128]{2,1,0:T(8,128)(2,1)S(1)}, u32[]{:S(2)}, u32[]{:S(2)}) collective-permute-start(bf16[10,128,128]{2,1,0:T(8,128)(2,1)} %get-tuple-element.138), channel_id=1, source_target_pairs={{0,32},{16,48},{32,64},{48,80},{64,96},{80,112},{96,0},{112,16},{1... | collective-permute-start | bytes 983048 | tf_op jit(solution)/shard_map/ppermute | solution.py:408
  96.9 20.0 %collective-permute-start.39 = (bf16[10,128,128]{2,1,0:T(8,128)(2,1)}, bf16[10,128,128]{2,1,0:T(8,128)(2,1)S(1)}, u32[]{:S(2)}, u32[]{:S(2)}) collective-permute-start(bf16[10,128,128]{2,1,0:T(8,128)(2,1)} %get-tuple-element.139), channel_id=1, source_target_pairs={{0,96},{16,112},{32,0},{48,16},{64,32},{80,48},{96,64},{112,80},{1... | collective-permute-start | bytes 983048 | tf_op jit(solution)/shard_map/ppermute | solution.py:408
  98.7 18.2 %collective-permute-start.40 = (bf16[10,128,128]{2,1,0:T(8,128)(2,1)}, bf16[10,128,128]{2,1,0:T(8,128)(2,1)S(1)}, u32[]{:S(2)}, u32[]{:S(2)}) collective-permute-start(bf16[10,128,128]{2,1,0:T(8,128)(2,1)} %get-tuple-element.140), channel_id=1, source_target_pairs={{0,64},{16,80},{32,96},{48,112},{64,0},{80,16},{96,32},{112,48},{1... | collective-permute-start | bytes 983048 | tf_op jit(solution)/shard_map/ppermute | solution.py:408
  98.9 12.0 %collective-permute-start.41 = (bf16[7,128,128]{2,1,0:T(8,128)(2,1)}, bf16[7,128,128]{2,1,0:T(8,128)(2,1)S(1)}, u32[]{:S(2)}, u32[]{:S(2)}) collective-permute-start(bf16[7,128,128]{2,1,0:T(8,128)(2,1)} %get-tuple-element.141), channel_id=1, source_target_pairs={{0,1},{1,0},{2,3},{3,2},{4,5},{5,4},{6,7},{7,6},{8,9},{9,8},{10,11... | collective-permute-start | bytes 688136 | tf_op jit(solution)/shard_map/ppermute | solution.py:412
  105.8 11.1 %collective-permute-start.42 = (bf16[7,128,128]{2,1,0:T(8,128)(2,1)}, bf16[7,128,128]{2,1,0:T(8,128)(2,1)S(1)}, u32[]{:S(2)}, u32[]{:S(2)}) collective-permute-start(bf16[7,128,128]{2,1,0:T(8,128)(2,1)} %get-tuple-element.142), channel_id=1, source_target_pairs={{0,3},{1,2},{2,1},{3,0},{4,7},{5,6},{6,5},{7,4},{8,11},{9,10},{10,... | collective-permute-start | bytes 688136 | tf_op jit(solution)/shard_map/ppermute | solution.py:412
  116.9 3.5 %collective-permute-start.43 = (bf16[10,128,128]{2,1,0:T(8,128)(2,1)S(1)}, bf16[10,128,128]{2,1,0:T(8,128)(2,1)S(1)}, u32[]{:S(2)}, u32[]{:S(2)}) collective-permute-start(bf16[10,128,128]{2,1,0:T(8,128)(2,1)S(1)} %collective-permute-done.38.refs_12_), channel_id=1, source_target_pairs={{0,16},{16,0},{32,48},{48,32},{64,80},{80,64},{96,112},{112,96},{1... | collective-permute-start | bytes 983048 | tf_op jit(solution)/shard_map/ppermute | solution.py:408
  119.1 1.7 %collective-permute-start.44 = (bf16[10,128,128]{2,1,0:T(8,128)(2,1)S(1)}, bf16[10,128,128]{2,1,0:T(8,128)(2,1)S(1)}, u32[]{:S(2)}, u32[]{:S(2)}) collective-permute-start(bf16[10,128,128]{2,1,0:T(8,128)(2,1)S(1)} %collective-permute-done.39.refs_14_), channel_id=1, source_target_pairs={{0,16},{16,0},{32,48},{48,32},{64,80},{80,64},{96,112},{112,96},{1... | collective-permute-start | bytes 983048 | tf_op jit(solution)/shard_map/ppermute | solution.py:408
  119.2 2.1 %collective-permute-start.45 = (bf16[10,128,128]{2,1,0:T(8,128)(2,1)S(1)}, bf16[10,128,128]{2,1,0:T(8,128)(2,1)S(1)}, u32[]{:S(2)}, u32[]{:S(2)}) collective-permute-start(bf16[10,128,128]{2,1,0:T(8,128)(2,1)S(1)} %collective-permute-done.40.refs_16_), channel_id=1, source_target_pairs={{0,16},{16,0},{32,48},{48,32},{64,80},{80,64},{96,112},{112,96},{1... | collective-permute-start | bytes 983048 | tf_op jit(solution)/shard_map/ppermute | solution.py:408
  (7 other events, 66.1 us)
